TPU v7x, 32 devices: a whole 2x2x4 slice. The times are simulated.
32 devices in a mesh: wide: 8 (over z, x), narrow: 4 (over y, core).
Axes of the slice: x: 2, y: 2, z: 4, core: 2. Of those that a mesh axis runs over, the one named last changes fastest.
Arguments:
- tokens: bfloat16 [64, 320, 1152], P('wide', 'narrow'), may hold values from -6 to 6
- skip_store: bfloat16 [64, 320, 1152], P('wide', None, 'narrow'), may hold values from -6 to 6
- cotangent: bfloat16 [64, 320, 1152], P('wide', 'narrow'), may hold values from -6 to 6
- lengths: int32 [64], P('wide'), may hold values from 192 to 320, as said below
- w_skip: float32 [2304, 1152], P(('wide', 'narrow')), may hold values from -20 to 20
- mom_skip: float32 [2304, 1152], P(('wide', 'narrow')), may hold values from -572.4334 to 572.4334
- sq_skip: float32 [2304, 1152], P(('wide', 'narrow')), may hold values from 0 to 81920
- w_qkv: float32 [1152, 3456], P(('wide', 'narrow')), may hold values from -20 to 20
- mom_qkv: float32 [1152, 3456], P(('wide', 'narrow')), may hold values from -572.4334 to 572.4334
- sq_qkv: float32 [1152, 3456], P(('wide', 'narrow')), may hold values from 0 to 81920
- w_proj: float32 [1152, 1152], P(('wide', 'narrow')), may hold values from -20 to 20
- mom_proj: float32 [1152, 1152], P(('wide', 'narrow')), may hold values from -572.4334 to 572.4334
- sq_proj: float32 [1152, 1152], P(('wide', 'narrow')), may hold values from 0 to 81920
- w_fc1: float32 [1152, 4608], P(('wide', 'narrow')), may hold values from -20 to 20
- mom_fc1: float32 [1152, 4608], P(('wide', 'narrow')), may hold values from -572.4334 to 572.4334
- sq_fc1: float32 [1152, 4608], P(('wide', 'narrow')), may hold values from 0 to 81920
- w_fc2: float32 [4608, 1152], P(('wide', 'narrow')), may hold values from -20 to 20
- mom_fc2: float32 [4608, 1152], P(('wide', 'narrow')), may hold values from -572.4334 to 572.4334
- sq_fc2: float32 [4608, 1152], P(('wide', 'narrow')), may hold values from 0 to 81920
- norm_table: float32 [1152, 4], P(('wide', 'narrow')), may hold values from -2 to 2
- norm_mom: float32 [1152, 4], P(('wide', 'narrow')), may hold values from -715.54175 to 715.54175
- norm_sq: float32 [1152, 4], P(('wide', 'narrow')), may hold values from 0 to 245760
Outputs:
- block_out: bfloat16 [64, 320, 1152], P('wide', 'narrow')
- grad_tokens: bfloat16 [64, 320, 1152], P('wide', 'narrow')
- grad_skip: bfloat16 [64, 320, 1152], P('wide', None, 'narrow')
- new_w_skip: float32 [2304, 1152], P(('wide', 'narrow'))
- new_mom_skip: float32 [2304, 1152], P(('wide', 'narrow'))
- new_sq_skip: float32 [2304, 1152], P(('wide', 'narrow'))
- copy_skip: bfloat16 [2304, 1152], P(('wide', 'narrow'))
- new_w_qkv: float32 [1152, 3456], P(('wide', 'narrow'))
- new_mom_qkv: float32 [1152, 3456], P(('wide', 'narrow'))
- new_sq_qkv: float32 [1152, 3456], P(('wide', 'narrow'))
- copy_qkv: bfloat16 [1152, 3456], P(('wide', 'narrow'))
- new_w_proj: float32 [1152, 1152], P(('wide', 'narrow'))
- new_mom_proj: float32 [1152, 1152], P(('wide', 'narrow'))
- new_sq_proj: float32 [1152, 1152], P(('wide', 'narrow'))
- copy_proj: bfloat16 [1152, 1152], P(('wide', 'narrow'))
- new_w_fc1: float32 [1152, 4608], P(('wide', 'narrow'))
- new_mom_fc1: float32 [1152, 4608], P(('wide', 'narrow'))
- new_sq_fc1: float32 [1152, 4608], P(('wide', 'narrow'))
- copy_fc1: bfloat16 [1152, 4608], P(('wide', 'narrow'))
- new_w_fc2: float32 [4608, 1152], P(('wide', 'narrow'))
- new_mom_fc2: float32 [4608, 1152], P(('wide', 'narrow'))
- new_sq_fc2: float32 [4608, 1152], P(('wide', 'narrow'))
- copy_fc2: bfloat16 [4608, 1152], P(('wide', 'narrow'))
- new_norm_table: float32 [1152, 4], P(('wide', 'narrow'))
- new_norm_mom: float32 [1152, 4], P(('wide', 'narrow'))
- new_norm_sq: float32 [1152, 4], P(('wide', 'narrow'))
- lamb_stats: float32 [3, 5], replicated
Inputs may be any that keep to these rules, and one draw needn't show every extreme that they name: `lengths`: among the 8 items of each index of wide, one has length 320.
All inputs are finite; a program needn't handle non-finite values.
Results may differ from a plain program's by a relative error of at most 0.015.
The roundings to bfloat16 on the way count: a program that leaves them out, or rounds other values in their place, can miss the bound.
Values may be sent and summed in bfloat16 or wider, within the bound.
No kernel may reach another device: no remote copies, remote signals or barrier semaphores. Data moves between devices by JAX's collectives and lax.ppermute only.
A program may use at most 384 MiB of HBM per device.

v0:
```python
import math

import jax
import jax.numpy as jnp
from jax import lax
from jax.sharding import PartitionSpec as P

HEAD_DIM = 72
STEP = 10


EPS_NORM = 1e-05
BETA_ONE = 0.5
BETA_TWO = 0.5
EPS_ADAM = 1e-06
DECAY = 0.01
RATE = 0.5
RATE_TABLE = 0.1
NEGATIVE = -1e30


def project(left, right):
    return jnp.dot(left, right, preferred_element_type=jnp.float32)


def across(left, right):
    return lax.dot_general(
        left, right, (((0,), (0,)), ((), ())), preferred_element_type=jnp.float32
    )


def against(left, right):
    return lax.dot_general(
        left, right, (((1,), (1,)), ((), ())), preferred_element_type=jnp.float32
    )


def norm_stats(values):
    center = values - jnp.mean(values, -1, keepdims=True)
    inv_std = lax.rsqrt(jnp.mean(center * center, -1, keepdims=True) + EPS_NORM)
    return (center * inv_std, inv_std)


def norm_back(grad_out, normed, inv_std, gain_col):
    scaled = grad_out * gain_col
    return inv_std * (
        scaled
        - jnp.mean(scaled, -1, keepdims=True)
        - normed * jnp.mean(scaled * normed, -1, keepdims=True)
    )


def masked_logits(queries, key_rows, key_valid):
    logits = jnp.einsum(
        "inhd,imhd->ihnm", queries, key_rows, preferred_element_type=jnp.float32
    ) * (1.0 / math.sqrt(HEAD_DIM))
    return jnp.where(key_valid[:, None, None, :], logits, NEGATIVE)


def forward(token_rows, skip_rows, weights, lengths, collect):
    w_skip, w_qkv, w_proj, w_fc1, w_fc2, norm_low = weights
    table = norm_low.astype(jnp.float32)
    item_count, row_count, model_width = token_rows.shape
    row_total = item_count * row_count
    joined = jnp.concatenate([token_rows, skip_rows], -1).reshape(row_total, 2 * model_width)
    first = project(joined, w_skip)
    normed_one, inv_one = norm_stats(first)
    act_one = (normed_one * table[:, 0] + table[:, 1]).astype(jnp.bfloat16)
    projected = project(act_one, w_qkv).astype(jnp.bfloat16)
    queries = projected[:, :model_width].reshape(item_count, row_count, -1, HEAD_DIM)
    key_full, value_full = collect(
        (
            projected[:, model_width : 2 * model_width].reshape(item_count, row_count, model_width),
            projected[:, 2 * model_width :].reshape(item_count, row_count, model_width),
        )
    )
    key_count = key_full.shape[1]
    key_rows = key_full.reshape(item_count, key_count, -1, HEAD_DIM)
    value_rows = value_full.reshape(item_count, key_count, -1, HEAD_DIM)
    key_valid = jnp.arange(key_count, dtype=jnp.int32)[None, :] < lengths[:, None]
    logits = masked_logits(queries, key_rows, key_valid)
    row_max = jnp.max(logits, -1, keepdims=True)
    log_total = row_max + jnp.log(jnp.sum(jnp.exp(logits - row_max), -1, keepdims=True))
    attn_probs = jnp.exp(logits - log_total).astype(jnp.bfloat16)
    heads_out = (
        jnp.einsum("ihnm,imhd->inhd", attn_probs, value_rows, preferred_element_type=jnp.float32)
        .astype(jnp.bfloat16)
        .reshape(row_total, model_width)
    )
    second = first + project(heads_out, w_proj)
    normed_two, inv_two = norm_stats(second)
    act_two = (normed_two * table[:, 2] + table[:, 3]).astype(jnp.bfloat16)
    pre_act = project(act_two, w_fc1)
    hidden = jax.nn.gelu(pre_act).astype(jnp.bfloat16)
    result = second + project(hidden, w_fc2)
    return (
        joined,
        normed_one,
        inv_one,
        act_one,
        queries,
        key_rows,
        value_rows,
        key_valid,
        log_total,
        heads_out,
        normed_two,
        inv_two,
        act_two,
        pre_act,
        hidden,
        result,
    )


def backward(kept, cotangent, weights, reduce_keys):
    (
        joined,
        normed_one,
        inv_one,
        act_one,
        queries,
        key_rows,
        value_rows,
        key_valid,
        log_total,
        heads_out,
        normed_two,
        inv_two,
        act_two,
        pre_act,
        hidden,
        result,
    ) = kept
    w_skip, w_qkv, w_proj, w_fc1, w_fc2, norm_low = weights
    table = norm_low.astype(jnp.float32)
    item_count, row_count, model_width = cotangent.shape
    row_total = item_count * row_count
    key_count = key_rows.shape[1]
    score_scale = 1.0 / math.sqrt(HEAD_DIM)
    grad_out = cotangent.reshape(row_total, model_width)
    grad_fc2 = across(hidden, grad_out)
    _, gelu_pull = jax.vjp(jax.nn.gelu, pre_act)
    d_pre = gelu_pull(against(grad_out, w_fc2))[0].astype(jnp.bfloat16)
    grad_fc1 = across(act_two, d_pre)
    d_act_two = against(d_pre, w_fc1)
    d_second = grad_out.astype(jnp.float32) + norm_back(d_act_two, normed_two, inv_two, table[:, 2])
    d_second_low = d_second.astype(jnp.bfloat16)
    grad_proj = across(heads_out, d_second_low)
    d_heads = against(d_second_low, w_proj).astype(jnp.bfloat16).reshape(queries.shape)
    logits = masked_logits(queries, key_rows, key_valid)
    prob_full = jnp.exp(logits - log_total)
    d_probs = jnp.einsum("inhd,imhd->ihnm", d_heads, value_rows, preferred_element_type=jnp.float32)
    d_logits = (prob_full * (d_probs - jnp.sum(prob_full * d_probs, -1, keepdims=True))).astype(
        jnp.bfloat16
    )
    d_queries = (
        jnp.einsum("ihnm,imhd->inhd", d_logits, key_rows, preferred_element_type=jnp.float32)
        * score_scale
    )
    part_keys = (
        jnp.einsum("ihnm,inhd->imhd", d_logits, queries, preferred_element_type=jnp.float32)
        * score_scale
    )
    part_values = jnp.einsum(
        "ihnm,inhd->imhd",
        prob_full.astype(jnp.bfloat16),
        d_heads,
        preferred_element_type=jnp.float32,
    )
    d_keys, d_values = reduce_keys(
        (
            part_keys.reshape(item_count, key_count, model_width),
            part_values.reshape(item_count, key_count, model_width),
        )
    )
    d_projected = jnp.concatenate(
        [
            d_queries.reshape(row_total, model_width),
            d_keys.reshape(row_total, model_width),
            d_values.reshape(row_total, model_width),
        ],
        -1,
    ).astype(jnp.bfloat16)
    grad_qkv = across(act_one, d_projected)
    d_act_one = against(d_projected, w_qkv)
    d_first = d_second + norm_back(d_act_one, normed_one, inv_one, table[:, 0])
    d_first_low = d_first.astype(jnp.bfloat16)
    grad_skip_lin = across(joined, d_first_low)
    d_joined = against(d_first_low, w_skip)
    grad_rows = (
        d_joined[:, :model_width].astype(jnp.bfloat16).reshape(item_count, row_count, model_width)
    )
    grad_skip_rows = (
        d_joined[:, model_width:].astype(jnp.bfloat16).reshape(item_count, row_count, model_width)
    )
    table_grads = jnp.stack(
        [
            jnp.sum(d_act_one * normed_one, 0),
            jnp.sum(d_act_one, 0),
            jnp.sum(d_act_two * normed_two, 0),
            jnp.sum(d_act_two, 0),
        ],
        1,
    )
    return (
        grad_rows,
        grad_skip_rows,
        (grad_skip_lin, grad_qkv, grad_proj, grad_fc1, grad_fc2, table_grads),
    )


def adam_step(grad, moment, square):
    new_mom = BETA_ONE * moment + (1.0 - BETA_ONE) * grad
    new_sq = BETA_TWO * square + (1.0 - BETA_TWO) * grad * grad
    step_dir = (
        new_mom / (1.0 - BETA_ONE**STEP) / (jnp.sqrt(new_sq / (1.0 - BETA_TWO**STEP)) + EPS_ADAM)
    )
    return (new_mom, new_sq, step_dir)


def local(
    tokens,
    skip_store,
    cotangent,
    lengths,
    w_skip,
    mom_skip,
    sq_skip,
    w_qkv,
    mom_qkv,
    sq_qkv,
    w_proj,
    mom_proj,
    sq_proj,
    w_fc1,
    mom_fc1,
    sq_fc1,
    w_fc2,
    mom_fc2,
    sq_fc2,
    norm_table,
    norm_mom,
    norm_sq,
):
    masters = (w_skip, w_qkv, w_proj, w_fc1, w_fc2)
    momenta = (mom_skip, mom_qkv, mom_proj, mom_fc1, mom_fc2)
    seconds = (sq_skip, sq_qkv, sq_proj, sq_fc1, sq_fc2)
    lowered = tuple((matrix.astype(jnp.bfloat16) for matrix in masters)) + (
        norm_table.astype(jnp.bfloat16),
    )
    local_sq = jnp.stack([jnp.sum(matrix * matrix) for matrix in masters])
    weights = (
        lax.all_gather(lowered[0], ("wide", "narrow"), axis=0, tiled=True),
        lax.all_gather(lowered[1], ("wide", "narrow"), axis=0, tiled=True),
        lax.all_gather(lowered[2], ("wide", "narrow"), axis=0, tiled=True),
        lax.all_gather(lowered[3], ("wide", "narrow"), axis=0, tiled=True),
        lax.all_gather(lowered[4], ("wide", "narrow"), axis=0, tiled=True),
        lax.all_gather(lowered[5], ("wide", "narrow"), axis=0, tiled=True),
    )
    skip_rows = lax.all_to_all(skip_store, "narrow", split_axis=1, concat_axis=2, tiled=True)

    def first_keys(pair):
        return (
            lax.all_gather(pair[0], "narrow", axis=1, tiled=True),
            lax.all_gather(pair[1], "narrow", axis=1, tiled=True),
        )

    def again_keys(pair):
        return (
            lax.all_gather(pair[0], "narrow", axis=1, tiled=True),
            lax.all_gather(pair[1], "narrow", axis=1, tiled=True),
        )

    def reduce_keys(pair):
        return (
            lax.psum_scatter(
                pair[0].astype(jnp.bfloat16), "narrow", scatter_dimension=1, tiled=True
            ).astype(jnp.float32),
            lax.psum_scatter(
                pair[1].astype(jnp.bfloat16), "narrow", scatter_dimension=1, tiled=True
            ).astype(jnp.float32),
        )

    kept = forward(tokens, skip_rows, weights, lengths, first_keys)
    block_low = kept[-1].reshape(tokens.shape).astype(jnp.bfloat16)
    _, again_low, again_tokens, again_skip = lax.optimization_barrier(
        (kept[-1], lowered, tokens, skip_rows)
    )
    weights = (
        lax.all_gather(again_low[0], ("wide", "narrow"), axis=0, tiled=True),
        lax.all_gather(again_low[1], ("wide", "narrow"), axis=0, tiled=True),
        lax.all_gather(again_low[2], ("wide", "narrow"), axis=0, tiled=True),
        lax.all_gather(again_low[3], ("wide", "narrow"), axis=0, tiled=True),
        lax.all_gather(again_low[4], ("wide", "narrow"), axis=0, tiled=True),
        lax.all_gather(again_low[5], ("wide", "narrow"), axis=0, tiled=True),
    )
    kept = forward(again_tokens, again_skip, weights, lengths, again_keys)
    grad_rows, grad_skip_rows, local_grads = backward(kept, cotangent, weights, reduce_keys)
    grad_skip = lax.all_to_all(grad_skip_rows, "narrow", split_axis=2, concat_axis=1, tiled=True)
    reduced = (
        lax.psum_scatter(local_grads[0], ("wide", "narrow"), scatter_dimension=0, tiled=True),
        lax.psum_scatter(local_grads[1], ("wide", "narrow"), scatter_dimension=0, tiled=True),
        lax.psum_scatter(local_grads[2], ("wide", "narrow"), scatter_dimension=0, tiled=True),
        lax.psum_scatter(local_grads[3], ("wide", "narrow"), scatter_dimension=0, tiled=True),
        lax.psum_scatter(local_grads[4], ("wide", "narrow"), scatter_dimension=0, tiled=True),
        lax.psum_scatter(local_grads[5], ("wide", "narrow"), scatter_dimension=0, tiled=True),
    )
    renewed = []
    update_list = []
    for index in range(5):
        new_mom, new_sq, step_dir = adam_step(reduced[index], momenta[index], seconds[index])
        update_list.append(step_dir + DECAY * masters[index])
        renewed.append((new_mom, new_sq))
    update_sq = jnp.stack([jnp.sum(update * update) for update in update_list])
    weight_sq, update_total = lax.psum((local_sq, update_sq), ("wide", "narrow"))
    weight_norm = jnp.sqrt(weight_sq)
    update_norm = jnp.sqrt(update_total)
    trust = weight_norm / (update_norm + EPS_ADAM)
    new_weights = [masters[index] - RATE * trust[index] * update_list[index] for index in range(5)]
    table_mom, table_sq, table_step = adam_step(reduced[5], norm_mom, norm_sq)
    new_table = norm_table - RATE_TABLE * table_step
    lamb_stats = jnp.stack([weight_norm, update_norm, trust], 0)
    return (
        block_low,
        grad_rows,
        grad_skip,
        new_weights[0],
        renewed[0][0],
        renewed[0][1],
        new_weights[0].astype(jnp.bfloat16),
        new_weights[1],
        renewed[1][0],
        renewed[1][1],
        new_weights[1].astype(jnp.bfloat16),
        new_weights[2],
        renewed[2][0],
        renewed[2][1],
        new_weights[2].astype(jnp.bfloat16),
        new_weights[3],
        renewed[3][0],
        renewed[3][1],
        new_weights[3].astype(jnp.bfloat16),
        new_weights[4],
        renewed[4][0],
        renewed[4][1],
        new_weights[4].astype(jnp.bfloat16),
        new_table,
        table_mom,
        table_sq,
        lamb_stats,
    )


def solution(mesh):
    placed = (
        P("wide", "narrow", None),
        P("wide", None, "narrow"),
        P("wide", "narrow", None),
        P("wide"),
        P(("wide", "narrow"), None),
        P(("wide", "narrow"), None),
        P(("wide", "narrow"), None),
        P(("wide", "narrow"), None),
        P(("wide", "narrow"), None),
        P(("wide", "narrow"), None),
        P(("wide", "narrow"), None),
        P(("wide", "narrow"), None),
        P(("wide", "narrow"), None),
        P(("wide", "narrow"), None),
        P(("wide", "narrow"), None),
        P(("wide", "narrow"), None),
        P(("wide", "narrow"), None),
        P(("wide", "narrow"), None),
        P(("wide", "narrow"), None),
        P(("wide", "narrow"), None),
        P(("wide", "narrow"), None),
        P(("wide", "narrow"), None),
    )
    return jax.shard_map(
        local,
        mesh=mesh,
        in_specs=placed,
        out_specs=(
            P("wide", "narrow", None),
            P("wide", "narrow", None),
            P("wide", None, "narrow"),
            P(("wide", "narrow"), None),
            P(("wide", "narrow"), None),
            P(("wide", "narrow"), None),
            P(("wide", "narrow"), None),
            P(("wide", "narrow"), None),
            P(("wide", "narrow"), None),
            P(("wide", "narrow"), None),
            P(("wide", "narrow"), None),
            P(("wide", "narrow"), None),
            P(("wide", "narrow"), None),
            P(("wide", "narrow"), None),
            P(("wide", "narrow"), None),
            P(("wide", "narrow"), None),
            P(("wide", "narrow"), None),
            P(("wide", "narrow"), None),
            P(("wide", "narrow"), None),
            P(("wide", "narrow"), None),
            P(("wide", "narrow"), None),
            P(("wide", "narrow"), None),
            P(("wide", "narrow"), None),
            P(("wide", "narrow"), None),
            P(("wide", "narrow"), None),
            P(("wide", "narrow"), None),
            P(),
        ),
        check_vma=False,
    )
```

profile of v0, /device:TPU:0, one launch (start us, length us, event | category | flops | bytes accessed | tf_op | source)
XLA Modules:
  0.0 2267.4 jit_solution(9061896096575650764)
XLA Ops:
  21.7 61.6 %all-gather = bf16[32,36,4]{1,2,0:T(4,128)(2,1)S(1)} all-gather(bf16[1,36,4]{1,2,0:T(4,128)(2,1)S(1)} %convert_bitcast_fusion.4), channel_id=1, replica_groups=mesh['wide'=8,'narrow'=4] {'wide','narrow'}, dimensions={0}, use_global_device_ids=true | all-gather | bytes 9504 | tf_op jit(solution)/shard_map/all_gather | solution.py:259
  89.9 7.2 fusion.107
  99.2 64.1 %all-gather.39.cloned.1.call-done = bf16[32,36,3456]{2,1,0:T(8,128)(2,1)} async-done(((bf16[1,36,3456]{2,1,0:T(8,128)(2,1)}), bf16[32,36,3456]{2,1,0:T(8,128)(2,1)}) %all-gather.39.cloned.1.call-update) | async-done | bytes 7962640 | tf_op jit(solution)/shard_map/all_gather | solution.py:255
  163.3 12.4 reshape.268
  175.7 10.4 convolution_convert_fusion.2
  195.8 28.4 %all-gather.41.cloned.1.call-done = bf16[32,36,1152]{2,1,0:T(8,128)(2,1)} async-done(((bf16[1,36,1152]{2,1,0:T(8,128)(2,1)}), bf16[32,36,1152]{2,1,0:T(8,128)(2,1)}) %all-gather.41.cloned.1.call-update) | async-done | bytes 2654224 | tf_op jit(solution)/shard_map/all_gather | solution.py:256
  229.3 5.9 reshape.283
  235.2 83.5 %all-gather.43.cloned.1.call-done = bf16[32,36,4608]{2,1,0:T(8,128)(2,1)} async-done(((bf16[1,36,4608]{2,1,0:T(8,128)(2,1)}), bf16[32,36,4608]{2,1,0:T(8,128)(2,1)}) %all-gather.43.cloned.1.call-update) | async-done | bytes 10616848 | tf_op jit(solution)/shard_map/all_gather | solution.py:257
  318.7 14.3 reshape.272
  333.0 30.2 %all-gather.27.cloned.1.call-done = bf16[8,320,1152]{2,1,0:T(8,128)(2,1)} async-done(((bf16[8,80,1152]{2,1,0:T(8,128)(2,1)}), bf16[8,320,1152]{2,1,0:T(8,128)(2,1)}) %all-gather.27.cloned.1.call-update) | async-done | bytes 5898256 | tf_op jit(solution)/shard_map/all_gather | solution.py:265
  363.2 9.3 copy.149
  372.5 36.9 %all-gather.25.cloned.1.call-done = bf16[8,320,1152]{2,1,0:T(8,128)(2,1)} async-done(((bf16[8,80,1152]{2,1,0:T(8,128)(2,1)}), bf16[8,320,1152]{2,1,0:T(8,128)(2,1)}) %all-gather.25.cloned.1.call-update) | async-done | bytes 5898256 | tf_op jit(solution)/shard_map/all_gather | solution.py:266
  409.4 9.4 copy.147
  429.9 9.6 convert_bitcast_fusion.1
  444.0 5.7 fusion.108
  451.7 48.6 %all-gather.29.cloned.1.call-done = bf16[4608,1152]{1,0:T(8,128)(2,1)} async-done(((bf16[144,1152]{1,0:T(8,128)(2,1)}), bf16[4608,1152]{1,0:T(8,128)(2,1)}) %all-gather.29.cloned.1.call-update) | async-done | bytes 10616848 | tf_op jit(solution)/shard_map/all_gather | solution.py:258
  500.3 25.7 %fusion.36 = bf16[640,1152]{1,0:T(8,128)(2,1)} fusion(f32[640,1152]{1,0:T(8,128)} %copy-done.23, bf16[4608,1152]{1,0:T(8,128)(2,1)} %all-gather.29.cloned.1.call-done, bf16[1152,4608]{1,0:T(8,128)(2,1)} %reshape.272, f32[1152]{0:T(1024)S(1)} %get-tuple-element.174, f32[1152]{0:T(1024)S(1)} %get-tuple-element.173, f32[640]{0:T(1024)S(1)} %add_rsqrt_fusion.2, ...), kind=kOutput, calls=%fused_computation.55 | convolution fusion | flops 13621248000 | bytes 25671680 | tf_op jit(solution)/shard_map/dot_general | solution.py:23
  528.1 39.0 %all-gather.4 = bf16[32,36,4]{1,2,0:T(4,128)(2,1)S(1)} all-gather(bf16[1,36,4]{1,2,0:T(4,128)(2,1)S(1)} %bitcast.166), channel_id=1, replica_groups=mesh['wide'=8,'narrow'=4] {'wide','narrow'}, dimensions={0}, use_global_device_ids=true | all-gather | bytes 9504 | tf_op jit(solution)/shard_map/all_gather | solution.py:296
  569.2 21.0 all-gather.31.cloned.1.call-done
  590.2 7.5 fusion.109
  598.2 73.8 %all-gather.45.cloned.1.call-done = bf16[32,36,3456]{2,1,0:T(8,128)(2,1)} async-done(((bf16[1,36,3456]{2,1,0:T(8,128)(2,1)}), bf16[32,36,3456]{2,1,0:T(8,128)(2,1)}) %all-gather.45.cloned.1.call-update) | async-done | bytes 7962640 | tf_op jit(solution)/shard_map/all_gather | solution.py:292
  672.0 12.4 reshape.276
  684.5 9.9 convolution_convert_fusion.1
  698.0 34.7 %all-gather.47.cloned.1.call-done = bf16[32,36,1152]{2,1,0:T(8,128)(2,1)} async-done(((bf16[1,36,1152]{2,1,0:T(8,128)(2,1)}), bf16[32,36,1152]{2,1,0:T(8,128)(2,1)}) %all-gather.47.cloned.1.call-update) | async-done | bytes 2654224 | tf_op jit(solution)/shard_map/all_gather | solution.py:293
  738.2 5.9 reshape.286
  747.5 79.9 %all-gather.49.cloned.1.call-done = bf16[32,36,4608]{2,1,0:T(8,128)(2,1)} async-done(((bf16[1,36,4608]{2,1,0:T(8,128)(2,1)}), bf16[32,36,4608]{2,1,0:T(8,128)(2,1)}) %all-gather.49.cloned.1.call-update) | async-done | bytes 10616848 | tf_op jit(solution)/shard_map/all_gather | solution.py:294
  827.4 14.4 reshape.280
  841.8 30.1 %all-gather.35.cloned.1.call-done = bf16[8,320,1152]{2,1,0:T(8,128)(2,1)} async-done(((bf16[8,80,1152]{2,1,0:T(8,128)(2,1)}), bf16[8,320,1152]{2,1,0:T(8,128)(2,1)}) %all-gather.35.cloned.1.call-update) | async-done | bytes 5898256 | tf_op jit(solution)/shard_map/all_gather | solution.py:271
  871.9 9.3 copy.156
  881.3 36.4 %all-gather.33.cloned.1.call-done = bf16[8,320,1152]{2,1,0:T(8,128)(2,1)} async-done(((bf16[8,80,1152]{2,1,0:T(8,128)(2,1)}), bf16[8,320,1152]{2,1,0:T(8,128)(2,1)}) %all-gather.33.cloned.1.call-update) | async-done | bytes 5898256 | tf_op jit(solution)/shard_map/all_gather | solution.py:272
  917.7 9.3 copy.154
  927.0 9.1 fusion.4
  941.5 10.0 convert_bitcast_fusion
  961.8 14.1 fusion.90
  975.9 32.5 %all-gather.37.cloned.1.call-done = bf16[4608,1152]{1,0:T(8,128)(2,1)} async-done(((bf16[144,1152]{1,0:T(8,128)(2,1)}), bf16[4608,1152]{1,0:T(8,128)(2,1)}) %all-gather.37.cloned.1.call-update) | async-done | bytes 10616848 | tf_op jit(solution)/shard_map/all_gather | solution.py:295
  1008.4 18.2 fusion.11
  1026.6 16.4 multiply_reduce_fusion.1
  1060.0 14.5 multiply_reduce_fusion
  1074.5 11.5 multiply_convert_fusion
  1091.3 9.3 copy.164
  1100.7 10.8 convolution_convert_fusion
  1111.5 9.4 copy.166
  1121.0 8.3 fusion.45
  1137.0 18.0 reduce-scatter.14.cloned.1.call-done
  1158.7 54.7 %reduce-scatter.16.cloned.1.call-done = bf16[8,80,1152]{2,1,0:T(8,128)(2,1)} async-done(((bf16[8,320,1152]{2,1,0:T(8,128)(2,1)}), bf16[8,80,1152]{2,1,0:T(8,128)(2,1)}) %reduce-scatter.16.cloned.1.call-update) | async-done | bytes 1474576 | tf_op jit(solution)/shard_map/reduce_scatter | solution.py:280
  1217.0 13.1 multiply_reduce_fusion.2
  1234.0 7.2 fusion.111
  1241.2 17.7 fusion.29
  1258.9 7.4 fusion.62
  1266.4 15.3 fusion.89
  1281.7 14.2 fusion.46
  1295.9 622.5 %fusion.91 = (f32[48,3456]{1,0:T(8,128)}, f32[48,1152]{1,0:T(8,128)S(1)}, f32[40,4608]{1,0:T(8,128)}) fusion(f32[1152,3456]{1,0:T(8,128)} %fusion.46, f32[1152,1152]{1,0:T(8,128)} %fusion.62, f32[1152,4608]{1,0:T(8,128)} %fusion.89), kind=kCustom, calls=%all-reduce-scatter.3 | all-reduce-scatter fusion | flops 12976130 | bytes 44089344
  1919.8 17.9 collective-permute-start.10
  1939.0 9.4 collective-permute-start.12
  1948.4 7.1 collective-permute-start.13
  1969.0 6.8 convolution_convert_fusion.3
  1975.8 11.9 collective-permute-start.2
  1994.3 14.3 collective-permute-start.5
  2008.6 27.1 %collective-permute-start.6 = (f32[48,3456]{1,0:T(8,128)}, f32[48,3456]{1,0:T(8,128)}, u32[]{:S(2)}, u32[]{:S(2)}) collective-permute-start(f32[48,3456]{1,0:T(8,128)} %get-tuple-element.183), channel_id=1, source_target_pairs={{0,7},{1,8},{2,9},{3,10},{4,11},{5,12},{6,13},{7,14},{8,15},{9,16}... | collective-permute-start | bytes 1990664
  2059.6 14.9 concatenate.21
  2077.2 31.2 %collective-permute-start.19 = (f32[4,4608]{1,0:T(4,128)}, f32[4,4608]{1,0:T(4,128)S(1)}, u32[]{:S(2)}, u32[]{:S(2)}) collective-permute-start(f32[4,4608]{1,0:T(4,128)} %slice.106), channel_id=1, source_target_pairs={{0,4},{1,5},{2,6},{3,7},{4,8},{5,9},{6,10},{7,11},{8,12},{9,13},{1... | collective-permute-start | bytes 221192
  2108.4 36.9 %concatenate.20 = f32[420,3456]{1,0:T(8,128)} concatenate(f32[36,3456]{1,0:T(8,128)} %copy-done.42, f32[48,3456]{1,0:T(8,128)} %collective-permute-done.6, f32[48,3456]{1,0:T(8,128)} %collective-permute-done.5, f32[48,3456]{1,0:T(8,128)} %collective-permute-done.4, f32[48,3456]{1,0:T(8,128)} %collective-permute-done.3, f32[48,3456]{1,0:T(8,128)} %collective-permute-done.2, ...), dimensions={0} | concatenate | bytes 11612160
  2149.0 18.1 concatenate.22
  2192.9 53.2 %all-reduce.8 = (f32[5]{0:T(128)S(1)}, f32[5]{0:T(128)S(1)}, f32[1152,4]{0,1:T(4,128)}) all-reduce(f32[5]{0:T(128)} %stack.74, f32[5]{0:T(128)S(1)} %stack.68, f32[1152,4]{0,1:T(4,128)} %pad_maximum_fusion.4), channel_id=1, replica_groups=mesh['wide'=8,'narrow'=4] {'wide','narrow'}, use_global_device_ids=true, to_apply=%region_35.36 | all-reduce | flops 4618 | bytes 36944 | tf_op jit(solution)/shard_map/psum | solution.py:316
  (299 shorter events, 218.7 us)
Async XLA Ops:
  7.2 82.7 %all-gather.23.cloned.1.call-start = ((), (), s32[]{:S(2)}) async-start(), calls=%async_computation.6 | async-start | bytes 5474304 | tf_op jit(solution)/shard_map/all_gather | solution.py:254
  9.1 154.2 %all-gather.39.cloned.1.call-start = ((), (), s32[]{:S(2)}) async-start(), calls=%async_computation.17 | async-start | bytes 9123840 | tf_op jit(solution)/shard_map/all_gather | solution.py:255
  10.9 213.2 %all-gather.41.cloned.1.call-start = ((), (), s32[]{:S(2)}) async-start(), calls=%async_computation.18 | async-start | bytes 3041280 | tf_op jit(solution)/shard_map/all_gather | solution.py:256
  12.6 306.1 %all-gather.43.cloned.1.call-start = ((), (), s32[]{:S(2)}) async-start(), calls=%async_computation.19 | async-start | bytes 12165120 | tf_op jit(solution)/shard_map/all_gather | solution.py:257
  17.4 66.0 %all-to-all-start = ((bf16[8,320,288]{2,0,1:T(8,128)(2,1)}), bf16[8,320,288]{2,0,1:T(8,128)(2,1)S(1)}, u32[]{:S(2)}, u32[]{:S(2)}) async-start(bf16[8,320,288]{2,0,1:T(8,128)(2,1)} %copy.143), calls=%async_computation | async-start | bytes 3932160 | tf_op jit(solution)/shard_map/all_to_all | solution.py:261
  21.7 68.3 %copy-start.28 = (bf16[8,80,1152]{2,1,0:T(8,128)(2,1)S(1)}, bf16[8,80,1152]{2,1,0:T(8,128)(2,1)}, u32[]{:S(2)}) copy-start(bf16[8,80,1152]{2,1,0:T(8,128)(2,1)} %param.22) | copy-start | bytes 4423684
  21.7 341.6 %all-gather.27.cloned.1.call-start = ((), (), s32[]{:S(2)}) async-start(), calls=%async_computation.8 | async-start | bytes 7372800 | tf_op jit(solution)/shard_map/all_gather | solution.py:265
  188.4 221.0 %all-gather.25.cloned.1.call-start = ((), (), s32[]{:S(2)}) async-start(), calls=%async_computation.7 | async-start | bytes 7372800 | tf_op jit(solution)/shard_map/all_gather | solution.py:266
  189.0 311.3 %all-gather.29.cloned.1.call-start = ((), (), s32[]{:S(2)}) async-start(), calls=%async_computation.9 | async-start | bytes 10948608 | tf_op jit(solution)/shard_map/all_gather | solution.py:258
  190.9 399.4 %all-gather.31.cloned.1.call-start = ((), (), s32[]{:S(2)}) async-start(), calls=%async_computation.10 | async-start | bytes 5474304 | tf_op jit(solution)/shard_map/all_gather | solution.py:291
  500.3 67.1 %copy-start.17 = (bf16[8,80,1152]{2,1,0:T(8,128)(2,1)S(1)}, bf16[8,80,1152]{2,1,0:T(8,128)(2,1)}, u32[]{:S(2)}) copy-start(bf16[8,80,1152]{2,1,0:T(8,128)(2,1)} %all_to_all.29) | copy-start | bytes 4423684
  500.3 67.1 %copy-start.29 = (bf16[8,80,1152]{2,1,0:T(8,128)(2,1)S(1)}, bf16[8,80,1152]{2,1,0:T(8,128)(2,1)}, u32[]{:S(2)}) copy-start(bf16[8,80,1152]{2,1,0:T(8,128)(2,1)} %param.22) | copy-start | bytes 4423684
  526.0 145.9 %all-gather.45.cloned.1.call-start = ((), (), s32[]{:S(2)}) async-start(), calls=%async_computation.20 | async-start | bytes 9123840 | tf_op jit(solution)/shard_map/all_gather | solution.py:292
  526.8 205.9 %all-gather.47.cloned.1.call-start = ((), (), s32[]{:S(2)}) async-start(), calls=%async_computation.21 | async-start | bytes 3041280 | tf_op jit(solution)/shard_map/all_gather | solution.py:293
  527.4 300.1 %all-gather.49.cloned.1.call-start = ((), (), s32[]{:S(2)}) async-start(), calls=%async_computation.22 | async-start | bytes 12165120 | tf_op jit(solution)/shard_map/all_gather | solution.py:294
  528.1 343.8 %all-gather.35.cloned.1.call-start = ((), (), s32[]{:S(2)}) async-start(), calls=%async_computation.12 | async-start | bytes 7372800 | tf_op jit(solution)/shard_map/all_gather | solution.py:271
  567.3 117.1 %copy-start.53 = (f32[1152]{0:T(1024)}, f32[1152]{0:T(1024)S(1)}, u32[]{:S(2)}) copy-start(f32[1152]{0:T(1024)S(1)} %get-tuple-element.172) | copy-start | bytes 13828
  567.4 117.1 %copy-start.59 = (f32[1152]{0:T(1024)}, f32[1152]{0:T(1024)S(1)}, u32[]{:S(2)}) copy-start(f32[1152]{0:T(1024)S(1)} %get-tuple-element.171) | copy-start | bytes 13828
  567.4 394.4 %copy-start.43 = (f32[1152]{0:T(1024)}, f32[1152]{0:T(1024)S(1)}, u32[]{:S(2)}) copy-start(f32[1152]{0:T(1024)S(1)} %get-tuple-element.170) | copy-start | bytes 13828
  597.7 86.7 %copy-start.6 = (f32[640,1152]{1,0:T(8,128)}, f32[640,1152]{1,0:T(8,128)S(1)}, u32[]{:S(2)}) copy-start(f32[640,1152]{1,0:T(8,128)S(1)} %get-tuple-element.232) | copy-start | bytes 8847364
  597.7 86.7 %copy-start.51 = (f32[640]{0:T(1024)}, f32[640]{0:T(1024)S(1)}, u32[]{:S(2)}) copy-start(f32[640]{0:T(1024)S(1)} %broadcast_multiply_fusion.5) | copy-start | bytes 7684
  598.2 86.3 %copy-start.57 = (f32[640]{0:T(1024)}, f32[640]{0:T(1024)S(1)}, u32[]{:S(2)}) copy-start(f32[640]{0:T(1024)S(1)} %add_rsqrt_fusion.1) | copy-start | bytes 7684
  696.7 221.0 %all-gather.33.cloned.1.call-start = ((), (), s32[]{:S(2)}) async-start(), calls=%async_computation.11 | async-start | bytes 7372800 | tf_op jit(solution)/shard_map/all_gather | solution.py:272
  697.4 311.0 %all-gather.37.cloned.1.call-start = ((), (), s32[]{:S(2)}) async-start(), calls=%async_computation.13 | async-start | bytes 10948608 | tf_op jit(solution)/shard_map/all_gather | solution.py:295
  698.0 457.1 %reduce-scatter.14.cloned.1.call-start = ((), (), s32[]{:S(2)}) async-start(), calls=%async_computation.14 | async-start | bytes 7372800 | tf_op jit(solution)/shard_map/reduce_scatter | solution.py:277
  961.4 81.7 %copy-start.4 = (f32[640,1152]{1,0:T(8,128)}, f32[640,1152]{1,0:T(8,128)S(1)}, u32[]{:S(2)}) copy-start(f32[640,1152]{1,0:T(8,128)S(1)} %get-tuple-element.236) | copy-start | bytes 8847364
  1100.7 112.7 %reduce-scatter.16.cloned.1.call-start = ((), (), s32[]{:S(2)}) async-start(), calls=%async_computation.15 | async-start | bytes 7372800 | tf_op jit(solution)/shard_map/reduce_scatter | solution.py:280
  1121.0 1055.7 %reduce-scatter.20.cloned.1.call-start = ((), (), s32[]{:S(2)}) async-start(), calls=%async_computation.23 | async-start | bytes 10948608
  1132.2 84.8 %copy-start.7 = (f32[640,1152]{1,0:T(8,128)S(1)}, f32[640,1152]{1,0:T(8,128)}, u32[]{:S(2)}) copy-start(f32[640,1152]{1,0:T(8,128)} %copy-done.6) | copy-start | bytes 8847364
  1132.2 84.8 %copy-start.52 = (f32[640]{0:T(1024)S(1)}, f32[640]{0:T(1024)}, u32[]{:S(2)}) copy-start(f32[640]{0:T(1024)} %copy-done.51) | copy-start | bytes 7684
  1132.2 84.8 %copy-start.54 = (f32[1152]{0:T(1024)S(1)}, f32[1152]{0:T(1024)}, u32[]{:S(2)}) copy-start(f32[1152]{0:T(1024)} %copy-done.53) | copy-start | bytes 13828
  1132.2 84.8 %copy-start.58 = (f32[640]{0:T(1024)S(1)}, f32[640]{0:T(1024)}, u32[]{:S(2)}) copy-start(f32[640]{0:T(1024)} %copy-done.57) | copy-start | bytes 7684
  1241.2 938.5 %reduce-scatter.18.cloned.1.call-start = ((), (), s32[]{:S(2)}) async-start(), calls=%async_computation.16 | async-start | bytes 21897216 | tf_op jit(solution)/shard_map/reduce_scatter | solution.py:306
  1295.9 673.0 %copy-start.31 = (bf16[640,1152]{1,0:T(8,128)(2,1)S(1)}, bf16[640,1152]{1,0:T(8,128)(2,1)}, u32[]{:S(2)}) copy-start(bf16[640,1152]{1,0:T(8,128)(2,1)} %copy-done.30) | copy-start | bytes 4423684
  1918.5 37.0 %collective-permute-start.15 = (f32[36,1152]{1,0:T(8,128)S(1)}, f32[36,1152]{1,0:T(8,128)S(1)}, u32[]{:S(2)}, u32[]{:S(2)}) collective-permute-start(f32[36,1152]{1,0:T(8,128)S(1)} %slice.105), channel_id=1, source_target_pairs={{0,8},{1,9},{2,10},{3,11},{4,12},{5,13},{6,14},{7,15},{8,16},{9,17... | collective-permute-start | bytes 497672
  1919.8 38.1 %collective-permute-start.10 = (f32[48,1152]{1,0:T(8,128)S(1)}, f32[48,1152]{1,0:T(8,128)S(1)}, u32[]{:S(2)}, u32[]{:S(2)}) collective-permute-start(f32[48,1152]{1,0:T(8,128)S(1)} %get-tuple-element.184), channel_id=1, source_target_pairs={{0,3},{1,4},{2,5},{3,6},{4,7},{5,8},{6,9},{7,10},{8,11},{9,12},{10... | collective-permute-start | bytes 663560
  1937.7 21.7 collective-permute-start.11
  1939.0 23.3 %collective-permute-start.12 = (f32[48,1152]{1,0:T(8,128)S(1)}, f32[48,1152]{1,0:T(8,128)}, u32[]{:S(2)}, u32[]{:S(2)}) collective-permute-start(f32[48,1152]{1,0:T(8,128)S(1)} %get-tuple-element.184), channel_id=1, source_target_pairs={{0,5},{1,6},{2,7},{3,8},{4,9},{5,10},{6,11},{7,12},{8,13},{9,14},{... | collective-permute-start | bytes 663560
  1948.4 17.0 collective-permute-start.13
  1955.5 12.1 collective-permute-start.14
  1958.0 17.8 collective-permute-start.8
  1959.4 28.4 %collective-permute-start.9 = (f32[48,1152]{1,0:T(8,128)S(1)}, f32[48,1152]{1,0:T(8,128)S(1)}, u32[]{:S(2)}, u32[]{:S(2)}) collective-permute-start(f32[48,1152]{1,0:T(8,128)S(1)} %get-tuple-element.184), channel_id=1, source_target_pairs={{0,2},{1,3},{2,4},{3,5},{4,6},{5,7},{6,8},{7,9},{8,10},{9,11},{10,... | collective-permute-start | bytes 663560
  1962.3 32.0 %collective-permute-start = (f32[48,3456]{1,0:T(8,128)}, f32[48,3456]{1,0:T(8,128)S(1)}, u32[]{:S(2)}, u32[]{:S(2)}) collective-permute-start(f32[48,3456]{1,0:T(8,128)} %get-tuple-element.183), channel_id=1, source_target_pairs={{0,1},{1,2},{2,3},{3,4},{4,5},{5,6},{6,7},{7,8},{8,9},{9,10},{10,1... | collective-permute-start | bytes 1990664
  1965.4 43.2 %collective-permute-start.1 = (f32[48,3456]{1,0:T(8,128)}, f32[48,3456]{1,0:T(8,128)S(1)}, u32[]{:S(2)}, u32[]{:S(2)}) collective-permute-start(f32[48,3456]{1,0:T(8,128)} %get-tuple-element.183), channel_id=1, source_target_pairs={{0,2},{1,3},{2,4},{3,5},{4,6},{5,7},{6,8},{7,9},{8,10},{9,11},{10,... | collective-permute-start | bytes 1990664
  1967.6 24.5 %collective-permute-start.7 = (f32[36,3456]{1,0:T(8,128)S(1)}, f32[36,3456]{1,0:T(8,128)S(1)}, u32[]{:S(2)}, u32[]{:S(2)}) collective-permute-start(f32[36,3456]{1,0:T(8,128)S(1)} %slice.104), channel_id=1, source_target_pairs={{0,8},{1,9},{2,10},{3,11},{4,12},{5,13},{6,14},{7,15},{8,16},{9,17... | collective-permute-start | bytes 1493000
  1975.8 61.2 %copy-start.48 = (f32[48,1152]{1,0:T(8,128)}, f32[48,1152]{1,0:T(8,128)S(1)}, u32[]{:S(2)}) copy-start(f32[48,1152]{1,0:T(8,128)S(1)} %collective-permute-done.8) | copy-start | bytes 663556
  1975.8 70.9 %collective-permute-start.2 = (f32[48,3456]{1,0:T(8,128)}, f32[48,3456]{1,0:T(8,128)}, u32[]{:S(2)}, u32[]{:S(2)}) collective-permute-start(f32[48,3456]{1,0:T(8,128)} %get-tuple-element.183), channel_id=1, source_target_pairs={{0,3},{1,4},{2,5},{3,6},{4,7},{5,8},{6,9},{7,10},{8,11},{9,12},{10... | collective-permute-start | bytes 1990664
  1987.7 49.3 %copy-start.49 = (f32[48,1152]{1,0:T(8,128)}, f32[48,1152]{1,0:T(8,128)S(1)}, u32[]{:S(2)}) copy-start(f32[48,1152]{1,0:T(8,128)S(1)} %collective-permute-done.9) | copy-start | bytes 663556
  1987.7 62.2 %collective-permute-start.3 = (f32[48,3456]{1,0:T(8,128)}, f32[48,3456]{1,0:T(8,128)}, u32[]{:S(2)}, u32[]{:S(2)}) collective-permute-start(f32[48,3456]{1,0:T(8,128)} %get-tuple-element.183), channel_id=1, source_target_pairs={{0,4},{1,5},{2,6},{3,7},{4,8},{5,9},{6,10},{7,11},{8,12},{9,13},{1... | collective-permute-start | bytes 1990664
  1992.1 44.8 %copy-start.42 = (f32[36,3456]{1,0:T(8,128)}, f32[36,3456]{1,0:T(8,128)S(1)}, u32[]{:S(2)}) copy-start(f32[36,3456]{1,0:T(8,128)S(1)} %collective-permute-done.7) | copy-start | bytes 1492996
  1992.1 61.6 %collective-permute-start.4 = (f32[48,3456]{1,0:T(8,128)}, f32[48,3456]{1,0:T(8,128)}, u32[]{:S(2)}, u32[]{:S(2)}) collective-permute-start(f32[48,3456]{1,0:T(8,128)} %get-tuple-element.183), channel_id=1, source_target_pairs={{0,5},{1,6},{2,7},{3,8},{4,9},{5,10},{6,11},{7,12},{8,13},{9,14},{... | collective-permute-start | bytes 1990664
  1994.3 45.5 %copy-start.39 = (f32[48,3456]{1,0:T(8,128)}, f32[48,3456]{1,0:T(8,128)S(1)}, u32[]{:S(2)}) copy-start(f32[48,3456]{1,0:T(8,128)S(1)} %collective-permute-done) | copy-start | bytes 1990660
  1994.3 82.9 %collective-permute-start.5 = (f32[48,3456]{1,0:T(8,128)}, f32[48,3456]{1,0:T(8,128)}, u32[]{:S(2)}, u32[]{:S(2)}) collective-permute-start(f32[48,3456]{1,0:T(8,128)} %get-tuple-element.183), channel_id=1, source_target_pairs={{0,6},{1,7},{2,8},{3,9},{4,10},{5,11},{6,12},{7,13},{8,14},{9,15},... | collective-permute-start | bytes 1990664
  2008.6 99.8 %collective-permute-start.6 = (f32[48,3456]{1,0:T(8,128)}, f32[48,3456]{1,0:T(8,128)}, u32[]{:S(2)}, u32[]{:S(2)}) collective-permute-start(f32[48,3456]{1,0:T(8,128)} %get-tuple-element.183), channel_id=1, source_target_pairs={{0,7},{1,8},{2,9},{3,10},{4,11},{5,12},{6,13},{7,14},{8,15},{9,16}... | collective-permute-start | bytes 1990664
  2039.8 34.8 %copy-start.20 = (f32[36,1152]{1,0:T(8,128)S(1)}, f32[36,1152]{1,0:T(8,128)}, u32[]{:S(2)}) copy-start(f32[36,1152]{1,0:T(8,128)} %param.32) | copy-start | bytes 497668
  2039.8 131.2 %all-to-all-start.1 = ((bf16[8,80,1152]{1,0,2:T(8,128)(2,1)}), bf16[8,80,1152]{1,0,2:T(8,128)(2,1)S(1)}, u32[]{:S(2)}, u32[]{:S(2)}) async-start(bf16[8,80,1152]{1,0,2:T(8,128)(2,1)} %copy.169), calls=%async_computation.3 | async-start | bytes 4718592 | tf_op jit(solution)/shard_map/all_to_all | solution.py:300
  2045.0 63.4 %copy-start.40 = (f32[48,3456]{1,0:T(8,128)S(1)}, f32[48,3456]{1,0:T(8,128)}, u32[]{:S(2)}) copy-start(f32[48,3456]{1,0:T(8,128)} %copy-done.39) | copy-start | bytes 1990660
  2046.7 102.3 %collective-permute-start.16 = (f32[40,4608]{1,0:T(8,128)}, f32[40,4608]{1,0:T(8,128)}, u32[]{:S(2)}, u32[]{:S(2)}) collective-permute-start(f32[40,4608]{1,0:T(8,128)} %get-tuple-element.185), channel_id=1, source_target_pairs={{0,1},{1,2},{2,3},{3,4},{4,5},{5,6},{6,7},{7,8},{8,9},{9,10},{10,1... | collective-permute-start | bytes 2211848
  2050.0 99.0 %collective-permute-start.17 = (f32[40,4608]{1,0:T(8,128)}, f32[40,4608]{1,0:T(8,128)}, u32[]{:S(2)}, u32[]{:S(2)}) collective-permute-start(f32[40,4608]{1,0:T(8,128)} %get-tuple-element.185), channel_id=1, source_target_pairs={{0,2},{1,3},{2,4},{3,5},{4,6},{5,7},{6,8},{7,9},{8,10},{9,11},{10,... | collective-permute-start | bytes 2211848
  2053.8 95.2 %collective-permute-start.18 = (f32[40,4608]{1,0:T(8,128)}, f32[40,4608]{1,0:T(8,128)}, u32[]{:S(2)}, u32[]{:S(2)}) collective-permute-start(f32[40,4608]{1,0:T(8,128)} %get-tuple-element.185), channel_id=1, source_target_pairs={{0,3},{1,4},{2,5},{3,6},{4,7},{5,8},{6,9},{7,10},{8,11},{9,12},{10... | collective-permute-start | bytes 2211848
  2077.2 71.8 %collective-permute-start.19 = (f32[4,4608]{1,0:T(4,128)}, f32[4,4608]{1,0:T(4,128)S(1)}, u32[]{:S(2)}, u32[]{:S(2)}) collective-permute-start(f32[4,4608]{1,0:T(4,128)} %slice.106), channel_id=1, source_target_pairs={{0,4},{1,5},{2,6},{3,7},{4,8},{5,9},{6,10},{7,11},{8,12},{9,13},{1... | collective-permute-start | bytes 221192
  2192.9 64.0 %copy-start.13 = (f32[36,3456]{1,0:T(8,128)S(1)}, f32[36,3456]{1,0:T(8,128)}, u32[]{:S(2)}) copy-start(f32[36,3456]{1,0:T(8,128)} %param.29) | copy-start | bytes 1492996
  2192.9 64.0 %copy-start.25 = (f32[36,3456]{1,0:T(8,128)S(1)}, f32[36,3456]{1,0:T(8,128)}, u32[]{:S(2)}) copy-start(f32[36,3456]{1,0:T(8,128)} %get-tuple-element.205) | copy-start | bytes 1492996
  2192.9 64.0 %copy-start.26 = (f32[36,3456]{1,0:T(8,128)S(1)}, f32[36,3456]{1,0:T(8,128)}, u32[]{:S(2)}) copy-start(f32[36,3456]{1,0:T(8,128)} %get-tuple-element.206) | copy-start | bytes 1492996
  (42 other events, 328.9 us)
Sparse Core Ops, SparseCore 0:
  11.4 70.0 all-gather.22
  85.0 78.2 all-gather.38
  166.7 57.4 all-gather.40
  227.5 91.1 all-gather.42
  320.7 42.4 all-gather.26
  365.2 44.1 all-gather.24
  412.9 87.3 all-gather.28
  526.2 64.0 all-gather.30
  593.7 78.2 all-gather.44
  675.2 57.4 all-gather.46
  736.2 91.1 all-gather.48
  829.4 42.4 all-gather.34
  873.5 44.1 all-gather.32
  921.0 87.3 all-gather.36
  1100.8 54.2 reduce-scatter.13
  1157.6 55.7 reduce-scatter.15
  1241.3 218.1 reduce-scatter.19
  1465.8 318.2 reduce-scatter.17
where the time goes:
time: 2280 us; the launch traced here: 2270 us
  blocking collectives  776 us (34%)
  waiting for transfers between devices  677 us (30%)
  local copies, waits for them, and re-layouts  284 us (12%)
  matrix products  278 us (12%)
  starting transfers between devices  163 us (7%)
  other arithmetic  70.6 us (3%)
    unnamed x1, blocking collectives  623 us
    unnamed x21, starting transfers between devices  153 us
    unnamed x146, local copies, waits for them, and re-layouts  150 us
    dot_general x8, matrix products, project(): return jnp.dot(left, right, preferred_element_type=jnp.float32)  86.1 us
    all_gather x1, waiting for transfers between devices, local(): lax.all_gather(lowered[3], ('wide', 'narrow'), axis=0, tiled=True)  83.5 us
    all_gather x1, waiting for transfers between devices, local(): lax.all_gather(again_low[3], ('wide', 'narrow'), axis=0, tiled=True)  79.9 us
    all_gather x1, waiting for transfers between devices, local(): lax.all_gather(again_low[1], ('wide', 'narrow'), axis=0, tiled=True)  73.8 us
    all_gather x1, waiting for transfers between devices, local(): lax.all_gather(lowered[1], ('wide', 'narrow'), axis=0, tiled=True)  64.1 us
  transfers between devices with their start and end apart: 40, of which 15 were waited for; matrix products, arithmetic and copies ran while one was open for 47% of the time, Pallas kernels for 0%

commit v1 on v0

v1 whole, which is shorter than its diff:
```python
import functools
import math

import jax
import jax.numpy as jnp
from jax import lax
from jax.experimental import pallas as pl
from jax.experimental.pallas import tpu as pltpu
from jax.sharding import PartitionSpec as P

LOW = jnp.bfloat16
CHIP_X = 2
CHIP_Y = 2
CORES = 2


class Place:
    def __init__(self, wide, narrow):
        self.wide, self.narrow = wide, narrow
        self.depth = wide // CHIP_X
        at_wide, at_narrow = lax.axis_index("wide"), lax.axis_index("narrow")
        self.z, self.x = at_wide // CHIP_X, at_wide % CHIP_X
        self.y, self.c = at_narrow // CORES, at_narrow % CORES
        self.spot = jnp.stack([self.z, self.x, self.y, self.c]).astype(jnp.int32)

    def swap_x(self, value):
        return lax.ppermute(value, "wide", [(i, i ^ 1) for i in range(self.wide)])

    def swap_y(self, value):
        return lax.ppermute(value, "narrow", [(i, i ^ 2) for i in range(self.narrow)])

    def swap_c(self, value):
        return lax.ppermute(value, "narrow", [(i, i ^ 1) for i in range(self.narrow)])

    def up_z(self, value):
        return lax.ppermute(value, "wide", [(i, i + CHIP_X) for i in range(self.wide - CHIP_X)])

    def down_z(self, value):
        return lax.ppermute(value, "wide", [(i + CHIP_X, i) for i in range(self.wide - CHIP_X)])


def run_moves(name, place, inputs, out_shapes, plan):
    count = len(inputs)
    out_count = len(out_shapes)

    def body(spot_ref, *refs):
        ins, outs, sems = refs[:count], refs[count : count + out_count], refs[count + out_count]
        spot = [spot_ref[k] for k in range(4)]
        moves = plan(spot, ins, outs)
        for start in (True, False):
            for at, (when, source, target) in enumerate(moves):
                copy = pltpu.make_async_copy(source, target, sems.at[at])
                act = copy.start if start else copy.wait
                if when is None:
                    act()
                else:
                    pl.when(when)(act)

    return pl.pallas_call(
        body,
        out_shape=out_shapes,
        in_specs=[pl.BlockSpec(memory_space=pltpu.SMEM)] + [pl.BlockSpec(memory_space=pl.ANY)] * count,
        out_specs=[pl.BlockSpec(memory_space=pl.ANY)] * out_count,
        scratch_shapes=[pltpu.SemaphoreType.DMA((64,))],
        name=name,
    )(place.spot, *inputs)


def line_gather(place, piece):
    below, above = [piece], [piece]
    for _ in range(place.depth - 1):
        below.append(place.up_z(below[-1]))
        above.append(place.down_z(above[-1]))
    return piece, below[1:], above[1:]


def pack_line(place, piece, below, above, parts):
    depth = place.depth
    out = [jax.ShapeDtypeStruct((depth,) + piece.shape[1:], piece.dtype)] * parts

    def plan(spot, ins, outs):
        z = spot[0]
        moves = []
        for part in range(parts):
            moves.append((None, ins[0].at[part], outs[part].at[z]))
            for k in range(1, depth):
                moves.append((z >= k, ins[k].at[part], outs[part].at[jnp.maximum(z - k, 0)]))
                moves.append((z < depth - k, ins[depth - 1 + k].at[part], outs[part].at[jnp.minimum(z + k, depth - 1)]))
        return moves

    return run_moves("pack_line", place, [piece] + below + above, out, plan)


def plane_gather(place, first, second):
    first_pair = jnp.stack([first, place.swap_x(first)])
    second_pair = jnp.stack([second, place.swap_y(second)])
    return first_pair, place.swap_y(first_pair), second_pair, place.swap_x(second_pair)


def line_scatter(place, blocks):
    depth, z = place.depth, place.z

    def pick(at):
        return lax.dynamic_index_in_dim(blocks, jnp.clip(at, 0, depth - 1), 0, keepdims=False)

    up = down = None
    for k in range(depth - 1, 0, -1):
        up_part, down_part = pick(z + k), pick(z - k)
        if up is not None:
            up_part = (up_part.astype(jnp.float32) + up.astype(jnp.float32)).astype(LOW)
            down_part = (down_part.astype(jnp.float32) + down.astype(jnp.float32)).astype(LOW)
        up, down = place.up_z(up_part), place.down_z(down_part)
    return pick(z).astype(jnp.float32) + up.astype(jnp.float32) + down.astype(jnp.float32)


def added(mine, other):
    return (mine.astype(jnp.float32) + other.astype(jnp.float32)).astype(LOW)


def choose(value, axis, at):
    return lax.dynamic_index_in_dim(value, at, axis, keepdims=False)


def plane_scatter(place, first, second):
    x, y = place.x, place.y
    first_got = place.swap_x(choose(first, 1, 1 - x))
    second_got = place.swap_y(choose(second, 2, 1 - y))
    first_sum = added(choose(first, 1, x), first_got)
    second_sum = added(choose(second, 2, y), second_got)
    first_got = place.swap_y(choose(first_sum, 1, 1 - y))
    second_got = place.swap_x(choose(second_sum, 1, 1 - x))
    return added(choose(first_sum, 1, y), first_got), added(choose(second_sum, 1, x), second_got)


HEAD_DIM = 72
STEP = 10
EPS_NORM = 1e-05
BETA_ONE = 0.5
BETA_TWO = 0.5
EPS_ADAM = 1e-06
DECAY = 0.01
RATE = 0.5
RATE_TABLE = 0.1
NEGATIVE = -1e30
BOTH = ("wide", "narrow")
SKIP_CUT = 640


def project(left, right):
    return jnp.dot(left, right, preferred_element_type=jnp.float32)


def across(left, right):
    return lax.dot_general(
        left, right, (((0,), (0,)), ((), ())), preferred_element_type=jnp.float32
    )


def against(left, right):
    return lax.dot_general(
        left, right, (((1,), (1,)), ((), ())), preferred_element_type=jnp.float32
    )


def norm_stats(values):
    center = values - jnp.mean(values, -1, keepdims=True)
    inv_std = lax.rsqrt(jnp.mean(center * center, -1, keepdims=True) + EPS_NORM)
    return (center * inv_std, inv_std)


def norm_back(grad_out, normed, inv_std, gain_col):
    scaled = grad_out * gain_col
    return inv_std * (
        scaled
        - jnp.mean(scaled, -1, keepdims=True)
        - normed * jnp.mean(scaled * normed, -1, keepdims=True)
    )


def adam_step(grad, moment, square):
    new_mom = BETA_ONE * moment + (1.0 - BETA_ONE) * grad
    new_sq = BETA_TWO * square + (1.0 - BETA_TWO) * grad * grad
    step_dir = (
        new_mom / (1.0 - BETA_ONE**STEP) / (jnp.sqrt(new_sq / (1.0 - BETA_TWO**STEP)) + EPS_ADAM)
    )
    return (new_mom, new_sq, step_dir)


def halves_by_core(place, both):
    half = both.shape[1] // 2
    mine = lax.dynamic_slice_in_dim(both, place.c * half, half, 1)
    got = place.swap_c(lax.dynamic_slice_in_dim(both, (1 - place.c) * half, half, 1))
    first = place.c == 0
    return jnp.concatenate([jnp.where(first, mine, got), jnp.where(first, got, mine)], 0)


def gather_columns(place, block):
    unit = block.shape[1] // 2
    piece = jnp.stack([block[:, :unit], block[:, unit:]])
    first, second = pack_line(place, *line_gather(place, piece), 2)
    kept = plane_gather(place, first, second)
    return kept + tuple(place.swap_c(value) for value in kept)


def plane_moves(spot, kept, out_one, out_two, when_one=None, when_two=None):
    x, y = spot[1], spot[2]
    moves = []
    for turn in range(2):
        at = x if turn == 0 else 1 - x
        moves.append((when_one, kept[0].at[turn], out_one(at, y)))
        moves.append((when_one, kept[1].at[turn], out_one(at, 1 - y)))
        at = y if turn == 0 else 1 - y
        moves.append((when_two, kept[2].at[turn], out_two(x, at)))
        moves.append((when_two, kept[3].at[turn], out_two(1 - x, at)))
    return moves


def assemble_fc1(place, kept, rows, unit):
    depth = place.depth
    out = [jax.ShapeDtypeStruct((depth, CHIP_X, CHIP_Y, rows, 4 * unit), LOW)]

    def plan(spot, ins, outs):
        moves = []
        for core in range(2):
            at = spot[3] if core == 0 else 1 - spot[3]
            start = pl.multiple_of(at * (2 * unit), 128)

            def one(x, y, start=start):
                return outs[0].at[:, x, y, :, pl.ds(start, unit)]

            def two(x, y, start=start):
                return outs[0].at[:, x, y, :, pl.ds(start + unit, unit)]

            moves += plane_moves(spot, ins[4 * core : 4 * core + 4], one, two)
        return moves

    (full,) = run_moves("assemble_fc1", place, kept, out, plan)
    return full.reshape(depth * CHIP_X * CHIP_Y * rows, 4 * unit)


def assemble_qkvp(place, kept, rows, unit):
    depth = place.depth
    lead = (depth, CHIP_X, CHIP_Y, rows)
    out = [jax.ShapeDtypeStruct(lead + (3 * unit,), LOW), jax.ShapeDtypeStruct(lead + (unit,), LOW)]

    def plan(spot, ins, outs):
        moves = []
        for core in range(2):
            at = spot[3] if core == 0 else 1 - spot[3]
            start = pl.multiple_of(at * (2 * unit), 128)
            x, y = spot[1], spot[2]

            def one(x, y, start=start):
                return outs[0].at[:, x, y, :, pl.ds(start, unit)]

            def key(x, y):
                return outs[0].at[:, x, y, :, pl.ds(unit, unit)]

            def last(x, y):
                return outs[1].at[:, x, y]

            kept = ins[4 * core : 4 * core + 4]
            for turn, move in enumerate(plane_moves(spot, kept, one, key)):
                if turn % 4 < 2:
                    moves.append(move)
                else:
                    moves.append((at == 0, move[1], move[2]))
            for turn, move in enumerate(plane_moves(spot, kept, one, last)):
                if turn % 4 >= 2:
                    moves.append((at == 1, move[1], move[2]))
        return moves

    qkv, proj = run_moves("assemble_qkvp", place, kept, out, plan)
    total = depth * CHIP_X * CHIP_Y * rows
    return qkv.reshape(total, 3 * unit), proj.reshape(total, unit)


def gather_skip(place, low):
    piece = low[None]
    (line,) = pack_line(place, *line_gather(place, piece), 1)
    kept = plane_gather(place, line[:, :, :SKIP_CUT], line[:, :, SKIP_CUT:])
    kept = kept + tuple(place.swap_c(value) for value in kept)
    rows, cols = low.shape
    depth = place.depth
    out = [jax.ShapeDtypeStruct((depth, CHIP_X, CHIP_Y, CORES, rows, cols), LOW)]

    def plan(spot, ins, outs):
        moves = []
        for core in range(2):
            at = spot[3] if core == 0 else 1 - spot[3]

            def one(x, y, at=at):
                return outs[0].at[:, x, y, at, :, pl.ds(0, SKIP_CUT)]

            def two(x, y, at=at):
                return outs[0].at[:, x, y, at, :, pl.ds(SKIP_CUT, cols - SKIP_CUT)]

            moves += plane_moves(spot, ins[4 * core : 4 * core + 4], one, two)
        return moves

    (full,) = run_moves("assemble_skip", place, kept, out, plan)
    return full.reshape(depth * CHIP_X * CHIP_Y * CORES * rows, cols)


def gather_fc2(place, low):
    rows, cols = low.shape
    half = rows // 2
    kept = plane_gather(place, low[:half], low[half:])
    piece = jnp.concatenate(kept, 0)[None]
    (line,) = pack_line(place, *line_gather(place, piece), 1)
    other = place.swap_c(line)
    depth = place.depth
    out = [jax.ShapeDtypeStruct((depth, CHIP_X, CHIP_Y, CORES, 2, half, cols), LOW)]

    def plan(spot, ins, outs):
        x, y = spot[1], spot[2]
        moves = []
        for core in range(2):
            at = spot[3] if core == 0 else 1 - spot[3]
            for turn in range(2):
                to = x if turn == 0 else 1 - x
                moves.append((None, ins[core].at[:, turn], outs[0].at[:, to, y, at, 0]))
                moves.append((None, ins[core].at[:, 2 + turn], outs[0].at[:, to, 1 - y, at, 0]))
                to = y if turn == 0 else 1 - y
                moves.append((None, ins[core].at[:, 4 + turn], outs[0].at[:, x, to, at, 1]))
                moves.append((None, ins[core].at[:, 6 + turn], outs[0].at[:, 1 - x, to, at, 1]))
        return moves

    (full,) = run_moves("assemble_fc2", place, [line, other], out, plan)
    return full.reshape(depth * CHIP_X * CHIP_Y * CORES * rows, cols)


def gather_weights(place, lows):
    w_skip, w_qkv, w_proj, w_fc1, w_fc2 = lows
    if place.short:
        return tuple(lax.all_gather(low, BOTH, axis=0, tiled=True) for low in lows)
    rows, unit = 2 * w_proj.shape[0], w_proj.shape[1]
    skip = gather_skip(place, w_skip)
    pair = jnp.concatenate([w_qkv, w_proj], 1)
    qkv, proj = assemble_qkvp(place, gather_columns(place, halves_by_core(place, pair)), rows, unit)
    fc1 = assemble_fc1(place, gather_columns(place, halves_by_core(place, w_fc1)), rows, unit)
    fc2 = gather_fc2(place, w_fc2)
    return skip, qkv, proj, fc1, fc2


def blocks_of(place, grad):
    return grad.reshape(place.depth, CHIP_X, CHIP_Y, -1, grad.shape[-1])


def halves_to_rows(place, parts):
    rows = parts.shape[1] // 2
    keep = lax.dynamic_slice_in_dim(parts, place.c * rows, rows, 1)
    got = place.swap_c(lax.dynamic_slice_in_dim(parts, (1 - place.c) * rows, rows, 1))
    first = place.c == 0
    low, high = jnp.where(first, keep, got), jnp.where(first, got, keep)
    return jnp.concatenate([low[0], low[1], high[0], high[1]], 1)


def scatter_columns(place, sends, keeps):
    gots = [place.swap_c(across(*pair).astype(LOW)) for pair in sends]
    sums = [added(across(*pair), got) for pair, got in zip(keeps, gots)]
    lines = plane_scatter(place, *[blocks_of(place, value) for value in sums])
    return halves_to_rows(place, line_scatter(place, jnp.stack(lines, 1)))


def scatter_skip(place, joined, grad):
    sums = []
    for part in (grad[:, :SKIP_CUT], grad[:, SKIP_CUT:]):
        full = across(joined, part).astype(LOW)
        full = full.reshape(place.depth, CHIP_X, CHIP_Y, CORES, -1, part.shape[1])
        got = place.swap_c(choose(full, 3, 1 - place.c))
        sums.append(added(choose(full, 3, place.c), got))
    line = jnp.concatenate(plane_scatter(place, *sums), 2)
    return line_scatter(place, line)


def scatter_fc2(place, hidden, grad):
    full = across(hidden, grad).astype(LOW)
    rows = full.shape[0] // (place.depth * CHIP_X * CHIP_Y * CORES * 2)
    full = full.reshape(place.depth, CHIP_X, CHIP_Y, CORES, 2, rows, -1)
    got = place.swap_c(choose(full, 3, 1 - place.c))
    sums = added(choose(full, 3, place.c), got)
    plane = line_scatter(place, sums).astype(LOW)[None]
    first, second = plane_scatter(place, plane[:, :, :, 0], plane[:, :, :, 1])
    return jnp.concatenate([first[0], second[0]], 0).astype(jnp.float32)


def sum_small(value):
    return lax.psum(value, BOTH)


def local(
    short,
    wide,
    narrow,
    tokens,
    skip_store,
    cotangent,
    lengths,
    w_skip,
    mom_skip,
    sq_skip,
    w_qkv,
    mom_qkv,
    sq_qkv,
    w_proj,
    mom_proj,
    sq_proj,
    w_fc1,
    mom_fc1,
    sq_fc1,
    w_fc2,
    mom_fc2,
    sq_fc2,
    norm_table,
    norm_mom,
    norm_sq,
):
    place = Place(wide, narrow)
    place.short = short
    devices = wide * narrow
    masters = (w_skip, w_qkv, w_proj, w_fc1, w_fc2)
    momenta = (mom_skip, mom_qkv, mom_proj, mom_fc1, mom_fc2)
    seconds = (sq_skip, sq_qkv, sq_proj, sq_fc1, sq_fc2)
    model = tokens.shape[-1]

    token_rows = lax.all_to_all(tokens, "narrow", split_axis=0, concat_axis=1, tiled=True)
    skip_rows = lax.all_to_all(skip_store, "narrow", split_axis=0, concat_axis=2, tiled=True)
    cot_rows = lax.all_to_all(cotangent, "narrow", split_axis=0, concat_axis=1, tiled=True)
    items, slots = token_rows.shape[:2]
    rows = items * slots
    lengths = lax.dynamic_slice_in_dim(lengths, lax.axis_index("narrow") * items, items)

    table_low = norm_table.astype(LOW)
    spread = jnp.broadcast_to(table_low.reshape(1, -1), (devices, table_low.size))
    table = lax.all_to_all(spread, BOTH, 0, 0, tiled=True).reshape(model, 4).astype(jnp.float32)
    table = table.T

    lows = tuple(matrix.astype(LOW) for matrix in masters)
    full_skip, full_qkv, full_proj, full_fc1, full_fc2 = gather_weights(place, lows)

    joined = jnp.concatenate([token_rows, skip_rows], -1).reshape(rows, 2 * model)
    first = project(joined, full_skip)
    normed_one, inv_one = norm_stats(first)
    act_one = (normed_one * table[0] + table[1]).astype(LOW)
    projected = project(act_one, full_qkv).astype(LOW)
    heads = model // HEAD_DIM
    split = projected.reshape(items, slots, 3, heads, HEAD_DIM)
    queries, keys, values = split[:, :, 0], split[:, :, 1], split[:, :, 2]
    key_valid = jnp.arange(slots, dtype=jnp.int32)[None, :] < lengths[:, None]
    scale = 1.0 / math.sqrt(HEAD_DIM)
    logits = jnp.einsum("inhd,imhd->ihnm", queries, keys, preferred_element_type=jnp.float32) * scale
    logits = jnp.where(key_valid[:, None, None, :], logits, NEGATIVE)
    row_max = jnp.max(logits, -1, keepdims=True)
    log_total = row_max + jnp.log(jnp.sum(jnp.exp(logits - row_max), -1, keepdims=True))
    probs = jnp.exp(logits - log_total)
    probs_low = probs.astype(LOW)
    heads_out = (
        jnp.einsum("ihnm,imhd->inhd", probs_low, values, preferred_element_type=jnp.float32)
        .astype(LOW)
        .reshape(rows, model)
    )
    second = first + project(heads_out, full_proj)
    normed_two, inv_two = norm_stats(second)
    act_two = (normed_two * table[2] + table[3]).astype(LOW)
    pre_act = project(act_two, full_fc1)
    hidden = jax.nn.gelu(pre_act).astype(LOW)
    block_rows = (second + project(hidden, full_fc2)).astype(LOW).reshape(items, slots, model)
    block_out = lax.all_to_all(block_rows, "narrow", split_axis=1, concat_axis=0, tiled=True)

    grad_out = cot_rows.reshape(rows, model)
    if place.short:
        grad_fc2 = lax.psum_scatter(across(hidden, grad_out), BOTH, scatter_dimension=0, tiled=True)
    else:
        grad_fc2 = scatter_fc2(place, hidden, grad_out)
    _, gelu_pull = jax.vjp(jax.nn.gelu, pre_act)
    d_pre = gelu_pull(against(grad_out, full_fc2))[0].astype(LOW)
    if place.short:
        grad_fc1 = lax.psum_scatter(across(act_two, d_pre), BOTH, scatter_dimension=0, tiled=True)
    else:

        def cut(value, half, unit):
            return lax.dynamic_slice_in_dim(value, half * 2 * model + unit * model, model, 1)

        sends = [(act_two, cut(d_pre, 1 - place.c, unit)) for unit in range(2)]
        keeps = [(act_two, cut(d_pre, place.c, unit)) for unit in range(2)]
        grad_fc1 = scatter_columns(place, sends, keeps)
    d_act_two = against(d_pre, full_fc1)
    d_second = grad_out.astype(jnp.float32) + norm_back(d_act_two, normed_two, inv_two, table[2])
    d_second_low = d_second.astype(LOW)
    d_heads = against(d_second_low, full_proj).astype(LOW).reshape(items, slots, heads, HEAD_DIM)
    d_probs = jnp.einsum("inhd,imhd->ihnm", d_heads, values, preferred_element_type=jnp.float32)
    d_logits = (probs * (d_probs - jnp.sum(probs * d_probs, -1, keepdims=True))).astype(LOW)
    d_queries = jnp.einsum("ihnm,imhd->inhd", d_logits, keys, preferred_element_type=jnp.float32)
    d_keys = jnp.einsum("ihnm,inhd->imhd", d_logits, queries, preferred_element_type=jnp.float32)
    d_values = jnp.einsum("ihnm,inhd->imhd", probs_low, d_heads, preferred_element_type=jnp.float32)
    d_projected = jnp.concatenate(
        [
            (d_queries * scale).astype(LOW).reshape(rows, model),
            (d_keys * scale).astype(LOW).reshape(rows, model),
            d_values.astype(LOW).reshape(rows, model),
        ],
        -1,
    )
    if place.short:
        grad_qkv = lax.psum_scatter(across(act_one, d_projected), BOTH, scatter_dimension=0, tiled=True)
        grad_proj = lax.psum_scatter(across(heads_out, d_second_low), BOTH, scatter_dimension=0, tiled=True)
    else:

        def pair(half):
            left = jnp.where(half == 0, act_one, heads_out)
            key = d_projected[:, model : 2 * model]
            return [
                (act_one, lax.dynamic_slice_in_dim(d_projected, half * 2 * model, model, 1)),
                (left, jnp.where(half == 0, key, d_second_low)),
            ]

        both = scatter_columns(place, pair(1 - place.c), pair(place.c))
        grad_qkv, grad_proj = both[:, : 3 * model], both[:, 3 * model :]
    d_act_one = against(d_projected, full_qkv)
    d_first = d_second + norm_back(d_act_one, normed_one, inv_one, table[0])
    d_first_low = d_first.astype(LOW)
    if place.short:
        grad_skip_lin = lax.psum_scatter(across(joined, d_first_low), BOTH, scatter_dimension=0, tiled=True)
    else:
        grad_skip_lin = scatter_skip(place, joined, d_first_low)
    d_joined = against(d_first_low, full_skip).astype(LOW).reshape(items, slots, 2 * model)
    grad_tokens = lax.all_to_all(d_joined[:, :, :model], "narrow", split_axis=1, concat_axis=0, tiled=True)
    grad_skip = lax.all_to_all(d_joined[:, :, model:], "narrow", split_axis=2, concat_axis=0, tiled=True)

    table_grads = jnp.stack(
        [
            jnp.sum(d_act_one * normed_one, 0),
            jnp.sum(d_act_one, 0),
            jnp.sum(d_act_two * normed_two, 0),
            jnp.sum(d_act_two, 0),
        ],
        1,
    )
    table_parts = lax.all_to_all(table_grads.reshape(devices, -1), BOTH, 0, 0, tiled=True)
    table_grad = jnp.sum(table_parts, 0).reshape(norm_table.shape)

    reduced = (grad_skip_lin, grad_qkv, grad_proj, grad_fc1, grad_fc2)
    renewed = []
    update_list = []
    for index in range(5):
        new_mom, new_sq, step_dir = adam_step(reduced[index], momenta[index], seconds[index])
        update_list.append(step_dir + DECAY * masters[index])
        renewed.append((new_mom, new_sq))
    squares = [jnp.sum(matrix * matrix) for matrix in masters]
    squares += [jnp.sum(update * update) for update in update_list]
    squares = jnp.broadcast_to(jnp.stack(squares)[None, :], (devices, 10))
    totals = jnp.sum(lax.all_to_all(squares, BOTH, 0, 0, tiled=True), 0)
    weight_norm = jnp.sqrt(totals[:5])
    update_norm = jnp.sqrt(totals[5:])
    trust = weight_norm / (update_norm + EPS_ADAM)
    new_weights = [masters[index] - RATE * trust[index] * update_list[index] for index in range(5)]
    table_mom, table_sq, table_step = adam_step(table_grad, norm_mom, norm_sq)
    new_table = norm_table - RATE_TABLE * table_step
    lamb_stats = jnp.stack([weight_norm, update_norm, trust], 0)
    outs = [block_out, grad_tokens, grad_skip]
    for index in range(5):
        outs += [new_weights[index], *renewed[index], new_weights[index].astype(LOW)]
    return (*outs, new_table, table_mom, table_sq, lamb_stats)


def solution(mesh):
    wide, narrow = mesh.shape["wide"], mesh.shape["narrow"]
    short = not (wide == 8 and narrow == 4)
    rows = P("wide", "narrow", None)
    store = P("wide", None, "narrow")
    shard = P(BOTH, None)
    return jax.shard_map(
        functools.partial(local, short, wide, narrow),
        mesh=mesh,
        in_specs=(rows, store, rows, P("wide")) + (shard,) * 18,
        out_specs=(rows, rows, store) + (shard,) * 23 + (P(),),
        check_vma=False,
    )
```

time: 2280 us -> 2480 us (1.088)
  Pallas kernels: 0 us -> 1410 us
  blocking collectives: 776 us -> 0 us
  waiting for transfers between devices: 677 us -> 347 us
  local copies, waits for them, and re-layouts: 284 us -> 166 us
  matrix products: 278 us -> 213 us
  starting transfers between devices: 163 us -> 226 us
  other arithmetic: 70.6 us -> 101 us
    pallas_call x0 -> x8, Pallas kernels: none -> 1410 us  [run_moves(): pl.pallas_call(body, out_shape=out_shapes, in_specs=[pl.BlockSpec(memory_...]
    unnamed x1 -> x0, blocking collectives: 623 us -> none
    all_gather x14 -> x0, waiting for transfers between devices: 600 us -> none  [the longest x1 83.5 us: local(): lax.all_gather(lowered[3], ('wide', 'narrow'), axis=0, tiled=True)]
    ppermute x0 -> x104, waiting for transfers between devices: none -> 315 us  [the longest x24 119 us: up_z(): lax.ppermute(value, 'wide', [(i, i + CHIP_X) for i in range(self.wide - C...]
    ppermute x0 -> x104, starting transfers between devices: none -> 187 us  [the longest x24 112 us: up_z(): lax.ppermute(value, 'wide', [(i, i + CHIP_X) for i in range(self.wide - C...]
    unnamed x21 -> x0, starting transfers between devices: 153 us -> none
    unnamed x146 -> x212, local copies, waits for them, and re-layouts: 150 us -> 35.1 us
    all_gather x2 -> x0, blocking collectives: 101 us -> none  [the longest x1 61.6 us: local(): lax.all_gather(lowered[5], ('wide', 'narrow'), axis=0, tiled=True)]
  transfers between devices with their start and end apart: 40 -> 113, of which waited for: 15 -> 38; matrix products, arithmetic and copies ran while one was open for 47% -> 10% of each run, Pallas kernels for 0% -> 24%
where the time goes in v1:
time: 2480 us; the launch traced here: 2470 us
  Pallas kernels  1410 us (57%)
  waiting for transfers between devices  347 us (14%)
  starting transfers between devices  226 us (9%)
  matrix products  213 us (9%)
  local copies, waits for them, and re-layouts  166 us (7%)
  other arithmetic  101 us (4%)
    pallas_call x8, Pallas kernels, run_moves(): pl.pallas_call(body, out_shape=out_shapes, in_specs=[pl.BlockSpec(memory_...  1410 us
    ppermute x24, waiting for transfers between devices, up_z(): lax.ppermute(value, 'wide', [(i, i + CHIP_X) for i in range(self.wide - C...  119 us
    ppermute x24, starting transfers between devices, up_z(): lax.ppermute(value, 'wide', [(i, i + CHIP_X) for i in range(self.wide - C...  112 us
    ppermute x24, waiting for transfers between devices, down_z(): lax.ppermute(value, 'wide', [(i + CHIP_X, i) for i in range(self.wide - C...  76.7 us
    ppermute x16, waiting for transfers between devices, swap_x(): return lax.ppermute(value, 'wide', [(i, i ^ 1) for i in range(self.wide)])  62.7 us
    dot_general x5, matrix products, against(): lax.dot_general(left, right, (((1,), (1,)), ((), ())), preferred_element_...  53.7 us
    dot_general x11, matrix products, across(): lax.dot_general(left, right, (((0,), (0,)), ((), ())), preferred_element_...  53.7 us
  transfers between devices with their start and end apart: 113, of which 38 were waited for; matrix products, arithmetic and copies ran while one was open for 10% of the time, Pallas kernels for 24%

profile of v1, /device:TPU:0, one launch (start us, length us, event | category | flops | bytes accessed | tf_op | source)
XLA Modules:
  0.0 2466.2 jit_solution(8736207770328322844)
XLA Ops:
  2.3 7.3 all-to-all-start.2
  24.8 5.3 collective-permute-start.15
  37.2 8.4 all-to-all-done.1
  56.1 5.3 collective-permute-start.30
  62.7 5.3 collective-permute-start.16
  70.5 22.4 pack_line.4
  96.0 5.3 collective-permute-start.31
  125.1 42.5 %pack_line.5 = (bf16[4,72,1152]{2,1,0:T(8,128)(2,1)}, bf16[4,72,1152]{2,1,0:T(8,128)(2,1)}) custom-call(s32[4]{0:T(128)} %pad_add_fusion.spot_ref, bf16[2,72,1152]{2,1,0:T(8,128)(2,1)} %copy-done.56, bf16[2,72,1152]{2,1,0:T(8,128)(2,1)} %collective-permute-done.15.refs_1_, bf16[2,72,1152]{2,1,0:T(8,128)(2,1)} %collective-permute-done.16.refs_2_, ...), custom_call_target="tpu_custom_call" | custom-call | tf_op jit(solution)/shard_map/pack_line/pallas_call | solution.py:59
  173.2 42.5 %pack_line.6 = (bf16[4,72,1152]{2,1,0:T(8,128)(2,1)}, bf16[4,72,1152]{2,1,0:T(8,128)(2,1)}) custom-call(s32[4]{0:T(128)} %pad_add_fusion.spot_ref, bf16[2,72,1152]{2,1,0:T(8,128)(2,1)} %copy-done.55, bf16[2,72,1152]{2,1,0:T(8,128)(2,1)} %collective-permute-done.30.refs_1_, bf16[2,72,1152]{2,1,0:T(8,128)(2,1)} %collective-permute-done.31.refs_2_, ...), custom_call_target="tpu_custom_call" | custom-call | tf_op jit(solution)/shard_map/pack_line/pallas_call | solution.py:59
  247.7 163.1 %assemble_skip.1 = bf16[4,2,2,2,72,1152]{5,4,3,2,1,0:T(8,128)(2,1)} custom-call(s32[4]{0:T(128)} %pad_add_fusion.spot_ref, bf16[2,4,72,640]{3,2,1,0:T(8,128)(2,1)} %copy-done.28, bf16[2,4,72,640]{3,2,1,0:T(8,128)(2,1)} %collective-permute-done.7.refs_1_, bf16[2,4,72,512]{3,2,1,0:T(8,128)(2,1)} %pad_maximum_fusion.10.refs_2_, ...), custom_call_target="tpu_custom_call" | custom-call | tf_op jit(solution)/shard_map/assemble_skip/pallas_call | solution.py:59
  410.8 7.5 fusion.195
  422.1 27.5 %collective-permute-done.39.refs_3_ = bf16[2,4,72,1152]{3,2,1,0:T(8,128)(2,1)} collective-permute-done((bf16[2,4,72,1152]{3,2,1,0:T(8,128)(2,1)}, bf16[2,4,72,1152]{3,2,1,0:T(8,128)(2,1)}, u32[]{:S(2)}, u32[]{:S(2)}) %collective-permute-start.39) | collective-permute-done | bytes 1327136 | tf_op jit(solution)/shard_map/ppermute | solution.py:27
  450.2 324.0 %assemble_qkvp.1 = (bf16[4,2,2,72,3456]{4,3,2,1,0:T(8,128)(2,1)}, bf16[4,2,2,72,1152]{4,3,2,1,0:T(8,128)(2,1)}) custom-call(s32[4]{0:T(128)} %pad_add_fusion.spot_ref, bf16[2,4,72,1152]{3,2,1,0:T(8,128)(2,1)} %pad_maximum_fusion.1.refs_0_, bf16[2,4,72,1152]{3,2,1,0:T(8,128)(2,1)} %collective-permute-done.22.refs_1_, ...), custom_call_target="tpu_custom_call" | custom-call | tf_op jit(solution)/shard_map/assemble_qkvp/pallas_call | solution.py:59
  774.1 11.1 convolution_convert_fusion.5
  785.2 16.6 reshape.422
  801.8 5.6 fusion.191
  821.0 12.1 fusion
  833.1 9.4 exponential_reduce_fusion
  842.5 10.0 convert_bitcast_fusion.1
  855.7 4.8 reshape.363
  867.0 324.0 %assemble_fc1.1 = bf16[4,2,2,72,4608]{4,3,2,1,0:T(8,128)(2,1)} custom-call(s32[4]{0:T(128)} %pad_add_fusion.spot_ref, bf16[2,4,72,1152]{3,2,1,0:T(8,128)(2,1)} %pad_maximum_fusion.3.refs_0_, bf16[2,4,72,1152]{3,2,1,0:T(8,128)(2,1)} %collective-permute-done.37.refs_1_, bf16[2,4,72,1152]{3,2,1,0:T(8,128)(2,1)} %pad_maximum_fusion.4.refs_2_, ...), custom_call_target="tpu_custom_call" | custom-call | tf_op jit(solution)/shard_map/assemble_fc1/pallas_call | solution.py:59
  1191.0 10.6 fusion.197
  1201.7 12.5 convolution_convert_fusion
  1214.1 8.8 constant_dynamic-slice_fusion.1
  1222.9 5.2 copy.513
  1228.1 9.1 collective-permute-done.93
  1237.2 5.3 fusion.11
  1245.2 5.7 collective-permute-start.94
  1252.2 26.6 %collective-permute-done.94 = bf16[2,2,2,72,1152]{4,3,0,2,1:T(8,128)(2,1)} collective-permute-done((bf16[2,2,2,72,1152]{4,3,0,2,1:T(8,128)(2,1)}, bf16[2,2,2,72,1152]{4,3,0,2,1:T(8,128)(2,1)}, u32[]{:S(2)}, u32[]{:S(2)}) %collective-permute-start.94) | collective-permute-done | bytes 1327136 | tf_op jit(solution)/shard_map/ppermute | solution.py:36
  1281.8 5.5 collective-permute-start.95
  1287.3 27.1 %collective-permute-done.95 = bf16[2,2,2,72,1152]{4,3,0,2,1:T(8,128)(2,1)} collective-permute-done((bf16[2,2,2,72,1152]{4,3,0,2,1:T(8,128)(2,1)}, bf16[2,2,2,72,1152]{4,3,0,2,1:T(8,128)(2,1)}, u32[]{:S(2)}, u32[]{:S(2)}) %collective-permute-start.95) | collective-permute-done | bytes 1327136 | tf_op jit(solution)/shard_map/ppermute | solution.py:36
  1319.5 5.1 collective-permute-start.96
  1324.6 26.0 %collective-permute-done.98 = bf16[2,2,2,72,1152]{4,3,0,2,1:T(8,128)(2,1)} collective-permute-done((bf16[2,2,2,72,1152]{4,3,0,2,1:T(8,128)(2,1)}, bf16[2,2,2,72,1152]{4,3,0,2,1:T(8,128)(2,1)}, u32[]{:S(2)}, u32[]{:S(2)}) %collective-permute-start.98) | collective-permute-done | bytes 1327136 | tf_op jit(solution)/shard_map/ppermute | solution.py:39
  1355.0 29.7 %collective-permute-done.99 = bf16[2,2,2,72,1152]{4,3,0,2,1:T(8,128)(2,1)} collective-permute-done((bf16[2,2,2,72,1152]{4,3,0,2,1:T(8,128)(2,1)}, bf16[2,2,2,72,1152]{4,3,0,2,1:T(8,128)(2,1)}, u32[]{:S(2)}, u32[]{:S(2)}) %collective-permute-start.99) | collective-permute-done | bytes 1327136 | tf_op jit(solution)/shard_map/ppermute | solution.py:39
  1389.5 5.7 collective-permute-done.102
  1407.5 5.1 collective-permute-done.44
  1414.8 5.0 collective-permute-done.45
  1426.0 23.5 collective-permute-done.48.refs_1_
  1455.5 23.3 collective-permute-done.49.refs_2_
  1484.6 17.8 collective-permute-done.50.refs_3_
  1506.7 163.1 %pack_line.7.refs_0_ = bf16[4,8,72,1152]{3,2,1,0:T(8,128)(2,1)} custom-call(s32[4]{0:T(128)} %pad_add_fusion.spot_ref, bf16[1,8,72,1152]{3,2,1,0:T(8,128)(2,1)} %bitcast.473, bf16[1,8,72,1152]{3,2,1,0:T(8,128)(2,1)} %copy-done.50, bf16[1,8,72,1152]{3,2,1,0:T(8,128)(2,1)} %copy-done.52, bf16[1,8,72,1152]{3,2,1,0:T(8,128)(2,1)} %copy-done.54, ...), custom_call_target="tpu_custom_call" | custom-call | tf_op jit(solution)/shard_map/pack_line/pallas_call | solution.py:59
  1672.2 6.8 collective-permute-done.54.refs_1_
  1679.0 324.0 %assemble_fc2.1 = bf16[4,2,2,2,2,72,1152]{6,5,4,3,2,1,0:T(8,128)(2,1)} custom-call(s32[4]{0:T(128)} %pad_add_fusion.spot_ref, bf16[4,8,72,1152]{3,2,1,0:T(8,128)(2,1)} %pack_line.7.refs_0_, bf16[4,8,72,1152]{3,2,1,0:T(8,128)(2,1)} %collective-permute-done.54.refs_1_), custom_call_target="tpu_custom_call" | custom-call | tf_op jit(solution)/shard_map/assemble_fc2/pallas_call | solution.py:59
  2003.0 15.5 fusion.13
  2018.5 17.4 fusion.7
  2035.9 15.4 multiply_reduce_fusion.1
  2058.0 5.9 reshape.423
  2066.9 18.0 multiply_reduce_fusion
  2084.9 12.0 multiply_convert_fusion
  2102.4 10.5 convert_bitcast_fusion
  2131.8 11.7 multiply_reduce_fusion.2
  2144.8 5.8 convolution_convert_fusion.7
  2168.4 5.6 convolution_convert_fusion.4
  2199.2 6.2 collective-permute-done.59
  2208.0 5.1 collective-permute-done.56
  2223.6 6.5 copy.474
  2244.9 4.8 add_convert_fusion.3
  2277.5 4.8 collective-permute-start.63
  2290.3 20.4 collective-permute-done.81
  2318.7 12.3 collective-permute-done.69
  2337.4 6.8 collective-permute-done.82
  2396.8 15.8 all-to-all-done.5
  2426.1 6.5 stack.234
  2432.7 6.8 all-to-all-done.6
  (585 shorter events, 434.2 us)
Async XLA Ops:
  19.9 25.8 %all-to-all-start.1 = ((bf16[8,320,288]{1,2,0:T(8,128)(2,1)}), bf16[8,320,288]{1,2,0:T(8,128)(2,1)S(1)}, u32[]{:S(2)}, u32[]{:S(2)}) async-start(bf16[8,320,288]{1,2,0:T(8,128)(2,1)} %param.23), calls=%async_computation.1 | async-start | bytes 3538944 | tf_op jit(solution)/shard_map/all_to_all | solution.py:428
  24.8 37.9 %collective-permute-start.15 = (bf16[2,72,1152]{2,1,0:T(8,128)(2,1)S(1)}, bf16[2,72,1152]{2,1,0:T(8,128)(2,1)}, u32[]{:S(2)}, u32[]{:S(2)}) collective-permute-start(bf16[2,72,1152]{2,1,0:T(8,128)(2,1)S(1)} %pad_maximum_fusion.12.refs_0_), channel_id=1, source_target_pairs={{0,8},{4,12},{8,16},{12,20},{16,24},{20,28},{1,9},{5,13},{9,17},{1... | collective-permute-start | bytes 995336 | tf_op jit(solution)/shard_map/ppermute | solution.py:36
  30.1 37.9 %collective-permute-start.18 = (bf16[2,72,1152]{2,1,0:T(8,128)(2,1)S(1)}, bf16[2,72,1152]{2,1,0:T(8,128)(2,1)}, u32[]{:S(2)}, u32[]{:S(2)}) collective-permute-start(bf16[2,72,1152]{2,1,0:T(8,128)(2,1)S(1)} %pad_maximum_fusion.12.refs_0_), channel_id=1, source_target_pairs={{8,0},{12,4},{16,8},{20,12},{24,16},{28,20},{9,1},{13,5},{17,9},{2... | collective-permute-start | bytes 995336 | tf_op jit(solution)/shard_map/ppermute | solution.py:39
  45.7 66.8 %all-to-all-start = ((bf16[8,80,1152]{2,1,0:T(8,128)(2,1)}), bf16[8,80,1152]{2,1,0:T(8,128)(2,1)}, u32[]{:S(2)}, u32[]{:S(2)}) async-start(bf16[8,80,1152]{2,1,0:T(8,128)(2,1)} %param.22), calls=%async_computation | async-start | bytes 2949120 | tf_op jit(solution)/shard_map/all_to_all | solution.py:427
  56.1 40.0 %collective-permute-start.30 = (bf16[2,72,1152]{2,1,0:T(8,128)(2,1)S(1)}, bf16[2,72,1152]{2,1,0:T(8,128)(2,1)}, u32[]{:S(2)}, u32[]{:S(2)}) collective-permute-start(bf16[2,72,1152]{2,1,0:T(8,128)(2,1)S(1)} %pad_maximum_fusion.13.refs_0_), channel_id=1, source_target_pairs={{0,8},{4,12},{8,16},{12,20},{16,24},{20,28},{1,9},{5,13},{9,17},{1... | collective-permute-start | bytes 995336 | tf_op jit(solution)/shard_map/ppermute | solution.py:36
  61.4 40.0 %collective-permute-start.33 = (bf16[2,72,1152]{2,1,0:T(8,128)(2,1)S(1)}, bf16[2,72,1152]{2,1,0:T(8,128)(2,1)}, u32[]{:S(2)}, u32[]{:S(2)}) collective-permute-start(bf16[2,72,1152]{2,1,0:T(8,128)(2,1)S(1)} %pad_maximum_fusion.13.refs_0_), channel_id=1, source_target_pairs={{8,0},{12,4},{16,8},{20,12},{24,16},{28,20},{9,1},{13,5},{17,9},{2... | collective-permute-start | bytes 995336 | tf_op jit(solution)/shard_map/ppermute | solution.py:39
  62.7 40.0 %collective-permute-start.16 = (bf16[2,72,1152]{2,1,0:T(8,128)(2,1)}, bf16[2,72,1152]{2,1,0:T(8,128)(2,1)}, u32[]{:S(2)}, u32[]{:S(2)}) collective-permute-start(bf16[2,72,1152]{2,1,0:T(8,128)(2,1)} %collective-permute-done.15.refs_1_), channel_id=1, source_target_pairs={{0,8},{4,12},{8,16},{12,20},{16,24},{20,28},{1,9},{5,13},{9,17},{1... | collective-permute-start | bytes 995336 | tf_op jit(solution)/shard_map/ppermute | solution.py:36
  68.0 39.2 %collective-permute-start.19 = (bf16[2,72,1152]{2,1,0:T(8,128)(2,1)}, bf16[2,72,1152]{2,1,0:T(8,128)(2,1)}, u32[]{:S(2)}, u32[]{:S(2)}) collective-permute-start(bf16[2,72,1152]{2,1,0:T(8,128)(2,1)} %collective-permute-done.18.refs_4_), channel_id=1, source_target_pairs={{8,0},{12,4},{16,8},{20,12},{24,16},{28,20},{9,1},{13,5},{17,9},{2... | collective-permute-start | bytes 995336 | tf_op jit(solution)/shard_map/ppermute | solution.py:39
  96.0 22.6 collective-permute-start.31
  111.0 58.2 %collective-permute-start.6 = (bf16[4,72,640]{2,1,0:T(8,128)(2,1)}, bf16[4,72,640]{2,1,0:T(8,128)(2,1)}, u32[]{:S(2)}, u32[]{:S(2)}) collective-permute-start(bf16[4,72,640]{2,1,0:T(8,128)(2,1)} %get-tuple-element.297), channel_id=1, source_target_pairs={{0,4},{4,0},{8,12},{12,8},{16,20},{20,16},{24,28},{28,24},{1,5},{5... | collective-permute-start | bytes 1105928 | tf_op jit(solution)/shard_map/ppermute | solution.py:27
  112.5 118.3 %all-to-all-start.4 = ((bf16[8,80,1152]{2,1,0:T(8,128)(2,1)}), bf16[8,80,1152]{2,1,0:T(8,128)(2,1)}, u32[]{:S(2)}, u32[]{:S(2)}) async-start(bf16[8,80,1152]{2,1,0:T(8,128)(2,1)} %param.24), calls=%async_computation.4 | async-start | bytes 2949120 | tf_op jit(solution)/shard_map/all_to_all | solution.py:429
  118.7 54.0 %collective-permute-start.9 = (bf16[2,4,72,512]{3,2,1,0:T(8,128)(2,1)}, bf16[2,4,72,512]{3,2,1,0:T(8,128)(2,1)}, u32[]{:S(2)}, u32[]{:S(2)}) collective-permute-start(bf16[2,4,72,512]{3,2,1,0:T(8,128)(2,1)} %pad_maximum_fusion.10.refs_2_), channel_id=1, source_target_pairs={{0,4},{4,0},{8,12},{12,8},{16,20},{20,16},{24,28},{28,24},{1,5},{5... | collective-permute-start | bytes 1769480 | tf_op jit(solution)/shard_map/ppermute | solution.py:27
  119.2 51.2 %collective-permute-start.32 = (bf16[2,72,1152]{2,1,0:T(8,128)(2,1)}, bf16[2,72,1152]{2,1,0:T(8,128)(2,1)S(1)}, u32[]{:S(2)}, u32[]{:S(2)}) collective-permute-start(bf16[2,72,1152]{2,1,0:T(8,128)(2,1)} %collective-permute-done.31.refs_2_), channel_id=1, source_target_pairs={{0,8},{4,12},{8,16},{12,20},{16,24},{20,28},{1,9},{5,13},{9,17},{1... | collective-permute-start | bytes 995336 | tf_op jit(solution)/shard_map/ppermute | solution.py:36
  123.8 48.6 %collective-permute-start.35 = (bf16[2,72,1152]{2,1,0:T(8,128)(2,1)}, bf16[2,72,1152]{2,1,0:T(8,128)(2,1)}, u32[]{:S(2)}, u32[]{:S(2)}) collective-permute-start(bf16[2,72,1152]{2,1,0:T(8,128)(2,1)} %collective-permute-done.34.refs_5_), channel_id=1, source_target_pairs={{8,0},{12,4},{16,8},{20,12},{24,16},{28,20},{9,1},{13,5},{17,9},{2... | collective-permute-start | bytes 995336 | tf_op jit(solution)/shard_map/ppermute | solution.py:39
  167.7 48.7 %collective-permute-start.21 = (bf16[4,72,1152]{2,1,0:T(8,128)(2,1)}, bf16[4,72,1152]{2,1,0:T(8,128)(2,1)}, u32[]{:S(2)}, u32[]{:S(2)}) collective-permute-start(bf16[4,72,1152]{2,1,0:T(8,128)(2,1)} %get-tuple-element.33), channel_id=1, source_target_pairs={{0,4},{4,0},{8,12},{12,8},{16,20},{20,16},{24,28},{28,24},{1,5},{5... | collective-permute-start | bytes 1990664 | tf_op jit(solution)/shard_map/ppermute | solution.py:27
  169.2 46.5 %collective-permute-start.12 = (bf16[2,4,72,512]{3,2,1,0:T(8,128)(2,1)}, bf16[2,4,72,512]{3,2,1,0:T(8,128)(2,1)}, u32[]{:S(2)}, u32[]{:S(2)}) collective-permute-start(bf16[2,4,72,512]{3,2,1,0:T(8,128)(2,1)} %pad_maximum_fusion.10.refs_2_), channel_id=1, source_target_pairs={{0,1},{1,0},{2,3},{3,2},{4,5},{5,4},{6,7},{7,6},{8,9},{9,8},{10,11... | collective-permute-start | bytes 1769480 | tf_op jit(solution)/shard_map/ppermute | solution.py:33
  170.4 65.4 %collective-permute-start.7 = (bf16[2,4,72,640]{3,2,1,0:T(8,128)(2,1)S(1)}, bf16[2,4,72,640]{3,2,1,0:T(8,128)(2,1)}, u32[]{:S(2)}, u32[]{:S(2)}) collective-permute-start(bf16[2,4,72,640]{3,2,1,0:T(8,128)(2,1)S(1)} %pad_maximum_fusion.8.refs_0_), channel_id=1, source_target_pairs={{0,2},{1,3},{2,0},{3,1},{4,6},{5,7},{6,4},{7,5},{8,10},{9,11},{10,... | collective-permute-start | bytes 2211848 | tf_op jit(solution)/shard_map/ppermute | solution.py:30
  172.5 63.3 %collective-permute-start.23 = (bf16[4,72,1152]{2,1,0:T(8,128)(2,1)}, bf16[4,72,1152]{2,1,0:T(8,128)(2,1)}, u32[]{:S(2)}, u32[]{:S(2)}) collective-permute-start(bf16[4,72,1152]{2,1,0:T(8,128)(2,1)} %get-tuple-element.34), channel_id=1, source_target_pairs={{0,2},{1,3},{2,0},{3,1},{4,6},{5,7},{6,4},{7,5},{8,10},{9,11},{10,... | collective-permute-start | bytes 1990664 | tf_op jit(solution)/shard_map/ppermute | solution.py:30
  172.6 66.1 %collective-permute-start.10 = (bf16[2,4,72,640]{3,2,1,0:T(8,128)(2,1)S(1)}, bf16[2,4,72,640]{3,2,1,0:T(8,128)(2,1)}, u32[]{:S(2)}, u32[]{:S(2)}) collective-permute-start(bf16[2,4,72,640]{3,2,1,0:T(8,128)(2,1)S(1)} %pad_maximum_fusion.8.refs_0_), channel_id=1, source_target_pairs={{0,1},{1,0},{2,3},{3,2},{4,5},{5,4},{6,7},{7,6},{8,9},{9,8},{10,11... | collective-permute-start | bytes 2211848 | tf_op jit(solution)/shard_map/ppermute | solution.py:33
  215.8 23.2 collective-permute-start.36
  238.7 179.6 %collective-permute-start.22 = (bf16[2,4,72,1152]{3,2,1,0:T(8,128)(2,1)}, bf16[2,4,72,1152]{3,2,1,0:T(8,128)(2,1)}, u32[]{:S(2)}, u32[]{:S(2)}) collective-permute-start(bf16[2,4,72,1152]{3,2,1,0:T(8,128)(2,1)} %pad_maximum_fusion.1.refs_0_), channel_id=1, source_target_pairs={{0,2},{1,3},{2,0},{3,1},{4,6},{5,7},{6,4},{7,5},{8,10},{9,11},{10,... | collective-permute-start | bytes 3981320 | tf_op jit(solution)/shard_map/ppermute | solution.py:30
  239.0 180.0 %collective-permute-start.25 = (bf16[2,4,72,1152]{3,2,1,0:T(8,128)(2,1)}, bf16[2,4,72,1152]{3,2,1,0:T(8,128)(2,1)}, u32[]{:S(2)}, u32[]{:S(2)}) collective-permute-start(bf16[2,4,72,1152]{3,2,1,0:T(8,128)(2,1)} %pad_maximum_fusion.1.refs_0_), channel_id=1, source_target_pairs={{0,1},{1,0},{2,3},{3,2},{4,5},{5,4},{6,7},{7,6},{8,9},{9,8},{10,11... | collective-permute-start | bytes 3981320 | tf_op jit(solution)/shard_map/ppermute | solution.py:33
  239.0 180.0 %collective-permute-start.24 = (bf16[2,4,72,1152]{3,2,1,0:T(8,128)(2,1)}, bf16[2,4,72,1152]{3,2,1,0:T(8,128)(2,1)}, u32[]{:S(2)}, u32[]{:S(2)}) collective-permute-start(bf16[2,4,72,1152]{3,2,1,0:T(8,128)(2,1)} %pad_maximum_fusion.2.refs_2_), channel_id=1, source_target_pairs={{0,4},{4,0},{8,12},{12,8},{16,20},{20,16},{24,28},{28,24},{1,5},{5... | collective-permute-start | bytes 3981320 | tf_op jit(solution)/shard_map/ppermute | solution.py:27
  245.1 176.5 %collective-permute-start.27 = (bf16[2,4,72,1152]{3,2,1,0:T(8,128)(2,1)}, bf16[2,4,72,1152]{3,2,1,0:T(8,128)(2,1)}, u32[]{:S(2)}, u32[]{:S(2)}) collective-permute-start(bf16[2,4,72,1152]{3,2,1,0:T(8,128)(2,1)} %pad_maximum_fusion.2.refs_2_), channel_id=1, source_target_pairs={{0,1},{1,0},{2,3},{3,2},{4,5},{5,4},{6,7},{7,6},{8,9},{9,8},{10,11... | collective-permute-start | bytes 3981320 | tf_op jit(solution)/shard_map/ppermute | solution.py:33
  245.9 175.8 %collective-permute-start.37 = (bf16[2,4,72,1152]{3,2,1,0:T(8,128)(2,1)}, bf16[2,4,72,1152]{3,2,1,0:T(8,128)(2,1)}, u32[]{:S(2)}, u32[]{:S(2)}) collective-permute-start(bf16[2,4,72,1152]{3,2,1,0:T(8,128)(2,1)} %pad_maximum_fusion.3.refs_0_), channel_id=1, source_target_pairs={{0,2},{1,3},{2,0},{3,1},{4,6},{5,7},{6,4},{7,5},{8,10},{9,11},{10,... | collective-permute-start | bytes 3981320 | tf_op jit(solution)/shard_map/ppermute | solution.py:30
  418.4 31.3 %collective-permute-start.39 = (bf16[2,4,72,1152]{3,2,1,0:T(8,128)(2,1)}, bf16[2,4,72,1152]{3,2,1,0:T(8,128)(2,1)}, u32[]{:S(2)}, u32[]{:S(2)}) collective-permute-start(bf16[2,4,72,1152]{3,2,1,0:T(8,128)(2,1)} %pad_maximum_fusion.4.refs_2_), channel_id=1, source_target_pairs={{0,4},{4,0},{8,12},{12,8},{16,20},{20,16},{24,28},{28,24},{1,5},{5... | collective-permute-start | bytes 3981320 | tf_op jit(solution)/shard_map/ppermute | solution.py:27
  419.0 30.7 %collective-permute-start.26 = (bf16[2,4,72,1152]{3,2,1,0:T(8,128)(2,1)}, bf16[2,4,72,1152]{3,2,1,0:T(8,128)(2,1)}, u32[]{:S(2)}, u32[]{:S(2)}) collective-permute-start(bf16[2,4,72,1152]{3,2,1,0:T(8,128)(2,1)} %collective-permute-done.22.refs_1_), channel_id=1, source_target_pairs={{0,1},{1,0},{2,3},{3,2},{4,5},{5,4},{6,7},{7,6},{8,9},{9,8},{10,11... | collective-permute-start | bytes 3981320 | tf_op jit(solution)/shard_map/ppermute | solution.py:33
  419.0 31.2 %collective-permute-start.28 = (bf16[2,4,72,1152]{3,2,1,0:T(8,128)(2,1)}, bf16[2,4,72,1152]{3,2,1,0:T(8,128)(2,1)}, u32[]{:S(2)}, u32[]{:S(2)}) collective-permute-start(bf16[2,4,72,1152]{3,2,1,0:T(8,128)(2,1)} %collective-permute-done.24.refs_3_), channel_id=1, source_target_pairs={{0,1},{1,0},{2,3},{3,2},{4,5},{5,4},{6,7},{7,6},{8,9},{9,8},{10,11... | collective-permute-start | bytes 3981320 | tf_op jit(solution)/shard_map/ppermute | solution.py:33
  421.6 445.4 %collective-permute-start.40 = (bf16[2,4,72,1152]{3,2,1,0:T(8,128)(2,1)}, bf16[2,4,72,1152]{3,2,1,0:T(8,128)(2,1)}, u32[]{:S(2)}, u32[]{:S(2)}) collective-permute-start(bf16[2,4,72,1152]{3,2,1,0:T(8,128)(2,1)} %pad_maximum_fusion.3.refs_0_), channel_id=1, source_target_pairs={{0,1},{1,0},{2,3},{3,2},{4,5},{5,4},{6,7},{7,6},{8,9},{9,8},{10,11... | collective-permute-start | bytes 3981320 | tf_op jit(solution)/shard_map/ppermute | solution.py:33
  421.7 445.3 %collective-permute-start.42 = (bf16[2,4,72,1152]{3,2,1,0:T(8,128)(2,1)}, bf16[2,4,72,1152]{3,2,1,0:T(8,128)(2,1)}, u32[]{:S(2)}, u32[]{:S(2)}) collective-permute-start(bf16[2,4,72,1152]{3,2,1,0:T(8,128)(2,1)} %pad_maximum_fusion.4.refs_2_), channel_id=1, source_target_pairs={{0,1},{1,0},{2,3},{3,2},{4,5},{5,4},{6,7},{7,6},{8,9},{9,8},{10,11... | collective-permute-start | bytes 3981320 | tf_op jit(solution)/shard_map/ppermute | solution.py:33
  449.6 417.4 %collective-permute-start.41 = (bf16[2,4,72,1152]{3,2,1,0:T(8,128)(2,1)}, bf16[2,4,72,1152]{3,2,1,0:T(8,128)(2,1)}, u32[]{:S(2)}, u32[]{:S(2)}) collective-permute-start(bf16[2,4,72,1152]{3,2,1,0:T(8,128)(2,1)} %collective-permute-done.37.refs_1_), channel_id=1, source_target_pairs={{0,1},{1,0},{2,3},{3,2},{4,5},{5,4},{6,7},{7,6},{8,9},{9,8},{10,11... | collective-permute-start | bytes 3981320 | tf_op jit(solution)/shard_map/ppermute | solution.py:33
  449.7 417.4 %collective-permute-start.43 = (bf16[2,4,72,1152]{3,2,1,0:T(8,128)(2,1)}, bf16[2,4,72,1152]{3,2,1,0:T(8,128)(2,1)}, u32[]{:S(2)}, u32[]{:S(2)}) collective-permute-start(bf16[2,4,72,1152]{3,2,1,0:T(8,128)(2,1)} %collective-permute-done.39.refs_3_), channel_id=1, source_target_pairs={{0,1},{1,0},{2,3},{3,2},{4,5},{5,4},{6,7},{7,6},{8,9},{9,8},{10,11... | collective-permute-start | bytes 3981320 | tf_op jit(solution)/shard_map/ppermute | solution.py:33
  1245.2 33.5 %collective-permute-start.94 = (bf16[2,2,2,72,1152]{4,3,0,2,1:T(8,128)(2,1)}, bf16[2,2,2,72,1152]{4,3,0,2,1:T(8,128)(2,1)}, u32[]{:S(2)}, u32[]{:S(2)}) collective-permute-start(bf16[2,2,2,72,1152]{4,3,0,2,1:T(8,128)(2,1)} %get-tuple-element.253), channel_id=1, source_target_pairs={{0,8},{4,12},{8,16},{12,20},{16,24},{20,28},{1,9},{5,13},{9,17},{1... | collective-permute-start | bytes 3981320 | tf_op jit(solution)/shard_map/ppermute | solution.py:36
  1250.9 36.5 %collective-permute-start.97 = (bf16[2,2,2,72,1152]{4,3,0,2,1:T(8,128)(2,1)S(1)}, bf16[2,2,2,72,1152]{4,3,0,2,1:T(8,128)(2,1)S(1)}, u32[]{:S(2)}, u32[]{:S(2)}) collective-permute-start(bf16[2,2,2,72,1152]{4,3,0,2,1:T(8,128)(2,1)S(1)} %get-tuple-element.254), channel_id=1, source_target_pairs={{8,0},{12,4},{16,8},{20,12},{24,16},{28,20},{9,1},{13,5},{17,9},{2... | collective-permute-start | bytes 3981320 | tf_op jit(solution)/shard_map/ppermute | solution.py:39
  1281.8 32.5 %collective-permute-start.95 = (bf16[2,2,2,72,1152]{4,3,0,2,1:T(8,128)(2,1)}, bf16[2,2,2,72,1152]{4,3,0,2,1:T(8,128)(2,1)}, u32[]{:S(2)}, u32[]{:S(2)}) collective-permute-start(bf16[2,2,2,72,1152]{4,3,0,2,1:T(8,128)(2,1)} %fusion.17), channel_id=1, source_target_pairs={{0,8},{4,12},{8,16},{12,20},{16,24},{20,28},{1,9},{5,13},{9,17},{1... | collective-permute-start | bytes 3981320 | tf_op jit(solution)/shard_map/ppermute | solution.py:36
  1318.2 32.4 %collective-permute-start.98 = (bf16[2,2,2,72,1152]{4,3,0,2,1:T(8,128)(2,1)}, bf16[2,2,2,72,1152]{4,3,0,2,1:T(8,128)(2,1)}, u32[]{:S(2)}, u32[]{:S(2)}) collective-permute-start(bf16[2,2,2,72,1152]{4,3,0,2,1:T(8,128)(2,1)} %get-tuple-element.252), channel_id=1, source_target_pairs={{8,0},{12,4},{16,8},{20,12},{24,16},{28,20},{9,1},{13,5},{17,9},{2... | collective-permute-start | bytes 3981320 | tf_op jit(solution)/shard_map/ppermute | solution.py:39
  1319.5 35.5 %collective-permute-start.96 = (bf16[2,2,2,72,1152]{4,3,0,2,1:T(8,128)(2,1)S(1)}, bf16[2,2,2,72,1152]{4,3,0,2,1:T(8,128)(2,1)S(1)}, u32[]{:S(2)}, u32[]{:S(2)}) collective-permute-start(bf16[2,2,2,72,1152]{4,3,0,2,1:T(8,128)(2,1)S(1)} %get-tuple-element.251), channel_id=1, source_target_pairs={{0,8},{4,12},{8,16},{12,20},{16,24},{20,28},{1,9},{5,13},{9,17},{1... | collective-permute-start | bytes 3981320 | tf_op jit(solution)/shard_map/ppermute | solution.py:36
  1353.7 31.0 %collective-permute-start.99 = (bf16[2,2,2,72,1152]{4,3,0,2,1:T(8,128)(2,1)}, bf16[2,2,2,72,1152]{4,3,0,2,1:T(8,128)(2,1)}, u32[]{:S(2)}, u32[]{:S(2)}) collective-permute-start(bf16[2,2,2,72,1152]{4,3,0,2,1:T(8,128)(2,1)} %fusion.16), channel_id=1, source_target_pairs={{8,0},{12,4},{16,8},{20,12},{24,16},{28,20},{9,1},{13,5},{17,9},{2... | collective-permute-start | bytes 3981320 | tf_op jit(solution)/shard_map/ppermute | solution.py:39
  1420.6 29.0 %collective-permute-start.48 = (bf16[1,8,72,1152]{3,2,1,0:T(8,128)(2,1)S(1)}, bf16[1,8,72,1152]{3,2,1,0:T(8,128)(2,1)S(1)}, u32[]{:S(2)}, u32[]{:S(2)}) collective-permute-start(bf16[1,8,72,1152]{3,2,1,0:T(8,128)(2,1)S(1)} %bitcast.471), channel_id=1, source_target_pairs={{0,8},{4,12},{8,16},{12,20},{16,24},{20,28},{1,9},{5,13},{9,17},{1... | collective-permute-start | bytes 3981320 | tf_op jit(solution)/shard_map/ppermute | solution.py:36
  1424.7 29.5 %collective-permute-start.51 = (bf16[1,8,72,1152]{3,2,1,0:T(8,128)(2,1)S(1)}, bf16[1,8,72,1152]{3,2,1,0:T(8,128)(2,1)S(1)}, u32[]{:S(2)}, u32[]{:S(2)}) collective-permute-start(bf16[1,8,72,1152]{3,2,1,0:T(8,128)(2,1)S(1)} %bitcast.472), channel_id=1, source_target_pairs={{8,0},{12,4},{16,8},{20,12},{24,16},{28,20},{9,1},{13,5},{17,9},{2... | collective-permute-start | bytes 3981320 | tf_op jit(solution)/shard_map/ppermute | solution.py:39
  1449.5 29.3 %collective-permute-start.49 = (bf16[1,8,72,1152]{3,2,1,0:T(8,128)(2,1)S(1)}, bf16[1,8,72,1152]{3,2,1,0:T(8,128)(2,1)S(1)}, u32[]{:S(2)}, u32[]{:S(2)}) collective-permute-start(bf16[1,8,72,1152]{3,2,1,0:T(8,128)(2,1)S(1)} %collective-permute-done.48.refs_1_), channel_id=1, source_target_pairs={{0,8},{4,12},{8,16},{12,20},{16,24},{20,28},{1,9},{5,13},{9,17},{1... | collective-permute-start | bytes 3981320 | tf_op jit(solution)/shard_map/ppermute | solution.py:36
  1454.2 29.1 %collective-permute-start.52 = (bf16[1,8,72,1152]{3,2,1,0:T(8,128)(2,1)S(1)}, bf16[1,8,72,1152]{3,2,1,0:T(8,128)(2,1)S(1)}, u32[]{:S(2)}, u32[]{:S(2)}) collective-permute-start(bf16[1,8,72,1152]{3,2,1,0:T(8,128)(2,1)S(1)} %collective-permute-done.51.refs_4_), channel_id=1, source_target_pairs={{8,0},{12,4},{16,8},{20,12},{24,16},{28,20},{9,1},{13,5},{17,9},{2... | collective-permute-start | bytes 3981320 | tf_op jit(solution)/shard_map/ppermute | solution.py:39
  1478.8 23.6 collective-permute-start.50
  1483.3 23.4 collective-permute-start.53
  2165.0 26.7 %collective-permute-start.55 = (bf16[4,2,2,72,640]{4,3,0,2,1:T(8,128)(2,1)}, bf16[4,2,2,72,640]{4,3,0,2,1:T(8,128)(2,1)}, u32[]{:S(2)}, u32[]{:S(2)}) collective-permute-start(bf16[4,2,2,72,640]{4,3,0,2,1:T(8,128)(2,1)} %bitcast.441), channel_id=1, source_target_pairs={{0,1},{1,0},{2,3},{3,2},{4,5},{5,4},{6,7},{7,6},{8,9},{9,8},{10,11... | collective-permute-start | bytes 4423688 | tf_op jit(solution)/shard_map/ppermute | solution.py:33
  2174.0 69.4 %collective-permute-start.67 = (bf16[1152,1152]{1,0:T(8,128)(2,1)}, bf16[1152,1152]{1,0:T(8,128)(2,1)}, u32[]{:S(2)}, u32[]{:S(2)}) collective-permute-start(bf16[1152,1152]{1,0:T(8,128)(2,1)} %convolution_convert_fusion.4), channel_id=1, source_target_pairs={{0,1},{1,0},{2,3},{3,2},{4,5},{5,4},{6,7},{7,6},{8,9},{9,8},{10,11... | collective-permute-start | bytes 7962632 | tf_op jit(solution)/shard_map/ppermute | solution.py:33
  2178.5 71.6 %collective-permute-start.70 = (bf16[1152,1152]{1,0:T(8,128)(2,1)}, bf16[1152,1152]{1,0:T(8,128)(2,1)}, u32[]{:S(2)}, u32[]{:S(2)}) collective-permute-start(bf16[1152,1152]{1,0:T(8,128)(2,1)} %convolution_convert_fusion.3), channel_id=1, source_target_pairs={{0,1},{1,0},{2,3},{3,2},{4,5},{5,4},{6,7},{7,6},{8,9},{9,8},{10,11... | collective-permute-start | bytes 7962632 | tf_op jit(solution)/shard_map/ppermute | solution.py:33
  2181.3 48.8 %all-to-all-start.8 = ((f32[32,1,144]{2,1,0:T(1,128)}), f32[32,1,144]{2,1,0:T(1,128)}, u32[]{:S(2)}, u32[]{:S(2)}) async-start(f32[32,1,144]{2,1,0:T(1,128)} %all_to_all.111), calls=%async_computation.8 | async-start | bytes 65536 | tf_op jit(solution)/shard_map/all_to_all | solution.py:540
  2206.3 30.5 %collective-permute-start.60 = (bf16[4,72,512]{2,1,0:T(8,128)(2,1)}, bf16[4,72,512]{2,1,0:T(8,128)(2,1)}, u32[]{:S(2)}, u32[]{:S(2)}) collective-permute-start(bf16[4,72,512]{2,1,0:T(8,128)(2,1)} %dynamic-slice_bitcast_fusion.11), channel_id=1, source_target_pairs={{0,4},{4,0},{8,12},{12,8},{16,20},{20,16},{24,28},{28,24},{1,5},{5... | collective-permute-start | bytes 884744 | tf_op jit(solution)/shard_map/ppermute | solution.py:27
  2214.2 24.2 collective-permute-start.57
  2230.1 26.2 %collective-permute-start.80 = (bf16[1152,1152]{1,0:T(8,128)(2,1)}, bf16[1152,1152]{1,0:T(8,128)(2,1)}, u32[]{:S(2)}, u32[]{:S(2)}) collective-permute-start(bf16[1152,1152]{1,0:T(8,128)(2,1)} %convolution_convert_fusion.2), channel_id=1, source_target_pairs={{0,1},{1,0},{2,3},{3,2},{4,5},{5,4},{6,7},{7,6},{8,9},{9,8},{10,11... | collective-permute-start | bytes 7962632 | tf_op jit(solution)/shard_map/ppermute | solution.py:33
  2230.1 159.9 %all-to-all-start.3 = ((bf16[2,320,1152]{2,0,1:T(2,128)(2,1)}), bf16[2,320,1152]{2,0,1:T(2,128)(2,1)}, u32[]{:S(2)}, u32[]{:S(2)}) async-start(bf16[2,320,1152]{2,0,1:T(2,128)(2,1)} %copy.419), calls=%async_computation.3 | async-start | bytes 2949120 | tf_op jit(solution)/shard_map/all_to_all | solution.py:469
  2236.8 32.1 %collective-permute-start.83 = (bf16[1152,1152]{1,0:T(8,128)(2,1)}, bf16[1152,1152]{1,0:T(8,128)(2,1)S(1)}, u32[]{:S(2)}, u32[]{:S(2)}) collective-permute-start(bf16[1152,1152]{1,0:T(8,128)(2,1)} %convolution_convert_fusion.1), channel_id=1, source_target_pairs={{0,1},{1,0},{2,3},{3,2},{4,5},{5,4},{6,7},{7,6},{8,9},{9,8},{10,11... | collective-permute-start | bytes 7962632 | tf_op jit(solution)/shard_map/ppermute | solution.py:33
  2239.6 23.1 collective-permute-start.61
  2250.1 36.6 %collective-permute-start.68 = (bf16[4,2,72,1152]{3,2,0,1:T(8,128)(2,1)S(1)}, bf16[4,2,72,1152]{3,2,0,1:T(8,128)(2,1)S(1)}, u32[]{:S(2)}, u32[]{:S(2)}) collective-permute-start(bf16[4,2,72,1152]{3,2,0,1:T(8,128)(2,1)S(1)} %bitcast.480), channel_id=1, source_target_pairs={{0,4},{4,0},{8,12},{12,8},{16,20},{20,16},{24,28},{28,24},{1,5},{5... | collective-permute-start | bytes 3981320 | tf_op jit(solution)/shard_map/ppermute | solution.py:27
  2256.3 32.1 %collective-permute-start.71 = (bf16[4,2,72,1152]{3,2,0,1:T(8,128)(2,1)S(1)}, bf16[4,2,72,1152]{3,2,0,1:T(8,128)(2,1)S(1)}, u32[]{:S(2)}, u32[]{:S(2)}) collective-permute-start(bf16[4,2,72,1152]{3,2,0,1:T(8,128)(2,1)S(1)} %bitcast.481), channel_id=1, source_target_pairs={{0,2},{1,3},{2,0},{3,1},{4,6},{5,7},{6,4},{7,5},{8,10},{9,11},{10,... | collective-permute-start | bytes 3981320 | tf_op jit(solution)/shard_map/ppermute | solution.py:30
  2262.7 48.0 %collective-permute-start.81 = (bf16[4,2,72,1152]{3,2,0,1:T(8,128)(2,1)S(1)}, bf16[4,2,72,1152]{3,2,0,1:T(8,128)(2,1)S(1)}, u32[]{:S(2)}, u32[]{:S(2)}) collective-permute-start(bf16[4,2,72,1152]{3,2,0,1:T(8,128)(2,1)S(1)} %bitcast.482), channel_id=1, source_target_pairs={{0,4},{4,0},{8,12},{12,8},{16,20},{20,16},{24,28},{28,24},{1,5},{5... | collective-permute-start | bytes 3981320 | tf_op jit(solution)/shard_map/ppermute | solution.py:27
  2283.4 33.4 %collective-permute-start.84 = (bf16[4,2,72,1152]{3,2,0,1:T(8,128)(2,1)S(1)}, bf16[4,2,72,1152]{3,2,0,1:T(8,128)(2,1)S(1)}, u32[]{:S(2)}, u32[]{:S(2)}) collective-permute-start(bf16[4,2,72,1152]{3,2,0,1:T(8,128)(2,1)S(1)} %bitcast.483), channel_id=1, source_target_pairs={{0,2},{1,3},{2,0},{3,1},{4,6},{5,7},{6,4},{7,5},{8,10},{9,11},{10,... | collective-permute-start | bytes 3981320 | tf_op jit(solution)/shard_map/ppermute | solution.py:30
  2287.1 44.0 %collective-permute-start.69 = (bf16[4,72,1152]{2,1,0:T(8,128)(2,1)S(1)}, bf16[4,72,1152]{2,1,0:T(8,128)(2,1)S(1)}, u32[]{:S(2)}, u32[]{:S(2)}) collective-permute-start(bf16[4,72,1152]{2,1,0:T(8,128)(2,1)S(1)} %dynamic-slice_bitcast_fusion.6), channel_id=1, source_target_pairs={{0,2},{1,3},{2,0},{3,1},{4,6},{5,7},{6,4},{7,5},{8,10},{9,11},{10,... | collective-permute-start | bytes 1990664 | tf_op jit(solution)/shard_map/ppermute | solution.py:30
  2288.8 42.5 %collective-permute-start.72 = (bf16[4,72,1152]{2,1,0:T(8,128)(2,1)S(1)}, bf16[4,72,1152]{2,1,0:T(8,128)(2,1)S(1)}, u32[]{:S(2)}, u32[]{:S(2)}) collective-permute-start(bf16[4,72,1152]{2,1,0:T(8,128)(2,1)S(1)} %dynamic-slice_bitcast_fusion.5), channel_id=1, source_target_pairs={{0,4},{4,0},{8,12},{12,8},{16,20},{20,16},{24,28},{28,24},{1,5},{5... | collective-permute-start | bytes 1990664 | tf_op jit(solution)/shard_map/ppermute | solution.py:27
  2311.0 33.2 %collective-permute-start.82 = (bf16[4,72,1152]{2,1,0:T(8,128)(2,1)S(1)}, bf16[4,72,1152]{2,1,0:T(8,128)(2,1)S(1)}, u32[]{:S(2)}, u32[]{:S(2)}) collective-permute-start(bf16[4,72,1152]{2,1,0:T(8,128)(2,1)S(1)} %dynamic-slice_bitcast_fusion.4), channel_id=1, source_target_pairs={{0,2},{1,3},{2,0},{3,1},{4,6},{5,7},{6,4},{7,5},{8,10},{9,11},{10,... | collective-permute-start | bytes 1990664 | tf_op jit(solution)/shard_map/ppermute | solution.py:30
  2317.2 27.2 %collective-permute-start.85 = (bf16[4,72,1152]{2,1,0:T(8,128)(2,1)S(1)}, bf16[4,72,1152]{2,1,0:T(8,128)(2,1)S(1)}, u32[]{:S(2)}, u32[]{:S(2)}) collective-permute-start(bf16[4,72,1152]{2,1,0:T(8,128)(2,1)S(1)} %dynamic-slice_bitcast_fusion.3), channel_id=1, source_target_pairs={{0,4},{4,0},{8,12},{12,8},{16,20},{20,16},{24,28},{28,24},{1,5},{5... | collective-permute-start | bytes 1990664 | tf_op jit(solution)/shard_map/ppermute | solution.py:27
  2390.0 22.6 all-to-all-start.5
  2413.8 25.7 %all-to-all-start.6 = ((bf16[2,320,1152]{1,0,2:T(2,128)(2,1)}), bf16[2,320,1152]{1,0,2:T(2,128)(2,1)S(1)}, u32[]{:S(2)}, u32[]{:S(2)}) async-start(bf16[2,320,1152]{1,0,2:T(2,128)(2,1)} %copy.474), calls=%async_computation.6 | async-start | bytes 3538944 | tf_op jit(solution)/shard_map/all_to_all | solution.py:529
  (149 other events, 4160.1 us)

commit v2 on v1

--- a/solution.py
+++ b/solution.py
@@ -22,6 +22,13 @@
         self.z, self.x = at_wide // CHIP_X, at_wide % CHIP_X
         self.y, self.c = at_narrow // CORES, at_narrow % CORES
         self.spot = jnp.stack([self.z, self.x, self.y, self.c]).astype(jnp.int32)
+        self.last = {}
+
+    def turn(self, kind, values, hops):
+        before = self.last.get(kind, ())
+        values = lax.optimization_barrier((*values, *before))[: len(values)]
+        self.last[kind] = tuple(hop(value) for hop, value in zip(hops, values))
+        return self.last[kind]
 
     def swap_x(self, value):
         return lax.ppermute(value, "wide", [(i, i ^ 1) for i in range(self.wide)])
@@ -60,8 +67,9 @@
         body,
         out_shape=out_shapes,
         in_specs=[pl.BlockSpec(memory_space=pltpu.SMEM)] + [pl.BlockSpec(memory_space=pl.ANY)] * count,
-        out_specs=[pl.BlockSpec(memory_space=pl.ANY)] * out_count,
+        out_specs=[pl.BlockSpec(memory_space=pltpu.VMEM)] * out_count,
         scratch_shapes=[pltpu.SemaphoreType.DMA((64,))],
+        compiler_params=pltpu.CompilerParams(vmem_limit_bytes=40 * 1024 * 1024),
         name=name,
     )(place.spot, *inputs)
 
@@ -69,8 +77,9 @@
 def line_gather(place, piece):
     below, above = [piece], [piece]
     for _ in range(place.depth - 1):
-        below.append(place.up_z(below[-1]))
-        above.append(place.down_z(above[-1]))
+        low, high = place.turn("z", (below[-1], above[-1]), (place.up_z, place.down_z))
+        below.append(low)
+        above.append(high)
     return piece, below[1:], above[1:]
 
 
@@ -92,9 +101,11 @@
 
 
 def plane_gather(place, first, second):
-    first_pair = jnp.stack([first, place.swap_x(first)])
-    second_pair = jnp.stack([second, place.swap_y(second)])
-    return first_pair, place.swap_y(first_pair), second_pair, place.swap_x(second_pair)
+    first_got, second_got = place.turn("plane", (first, second), (place.swap_x, place.swap_y))
+    first_pair = jnp.stack([first, first_got])
+    second_pair = jnp.stack([second, second_got])
+    first_far, second_far = place.turn("plane", (first_pair, second_pair), (place.swap_y, place.swap_x))
+    return first_pair, first_far, second_pair, second_far
 
 
 def line_scatter(place, blocks):
@@ -109,7 +120,7 @@
         if up is not None:
             up_part = (up_part.astype(jnp.float32) + up.astype(jnp.float32)).astype(LOW)
             down_part = (down_part.astype(jnp.float32) + down.astype(jnp.float32)).astype(LOW)
-        up, down = place.up_z(up_part), place.down_z(down_part)
+        up, down = place.turn("z", (up_part, down_part), (place.up_z, place.down_z))
     return pick(z).astype(jnp.float32) + up.astype(jnp.float32) + down.astype(jnp.float32)
 
 
@@ -123,12 +134,12 @@
 
 def plane_scatter(place, first, second):
     x, y = place.x, place.y
-    first_got = place.swap_x(choose(first, 1, 1 - x))
-    second_got = place.swap_y(choose(second, 2, 1 - y))
+    parts = (choose(first, 1, 1 - x), choose(second, 2, 1 - y))
+    first_got, second_got = place.turn("plane", parts, (place.swap_x, place.swap_y))
     first_sum = added(choose(first, 1, x), first_got)
     second_sum = added(choose(second, 2, y), second_got)
-    first_got = place.swap_y(choose(first_sum, 1, 1 - y))
-    second_got = place.swap_x(choose(second_sum, 1, 1 - x))
+    parts = (choose(first_sum, 1, 1 - y), choose(second_sum, 1, 1 - x))
+    first_got, second_got = place.turn("plane", parts, (place.swap_y, place.swap_x))
     return added(choose(first_sum, 1, y), first_got), added(choose(second_sum, 1, x), second_got)
 
 
@@ -186,12 +197,132 @@
     return (new_mom, new_sq, step_dir)
 
 
+ATTN_VMEM = 48 * 1024 * 1024
+
+
+def head_window(head):
+    start = head * HEAD_DIM
+    base = start // 128 * 128
+    width = 128 if start - base + HEAD_DIM <= 128 else 256
+    return base, width, start - base
+
+
+def lane_mask(rows, width, offset):
+    lane = lax.broadcasted_iota(jnp.int32, (rows, width), 1)
+    return (lane >= offset) & (lane < offset + HEAD_DIM)
+
+
+def score_rows(queries, keys, length, slots):
+    logits = against(keys, queries) * (1.0 / math.sqrt(HEAD_DIM))
+    key_at = lax.broadcasted_iota(jnp.int32, (slots, slots), 0)
+    return jnp.where(key_at < length, logits, NEGATIVE)
+
+
+def rows_of(ref, window):
+    return ref[:, 0, :, window].reshape(-1, window.size)
+
+
+def put_rows(ref, window, mask, value):
+    merged = jnp.where(mask, value, rows_of(ref, window))
+    ref[:, 0, :, window] = merged.reshape(ref.shape[0], ref.shape[2], window.size)
+
+
+def attend_kernel(model, lengths_ref, qkv_ref, out_ref, lse_ref):
+    slots = qkv_ref.shape[0] * qkv_ref.shape[2]
+    length = lengths_ref[pl.program_id(0)]
+    for head in range(model // HEAD_DIM):
+        base, width, offset = head_window(head)
+        mask = lane_mask(slots, width, offset)
+        window = pl.ds(base, width)
+        queries = jnp.where(mask, rows_of(qkv_ref, window), jnp.zeros((), LOW))
+        logits = score_rows(queries, rows_of(qkv_ref, pl.ds(model + base, width)), length, slots)
+        top = jnp.max(logits, 0, keepdims=True)
+        lse = top + jnp.log(jnp.sum(jnp.exp(logits - top), 0, keepdims=True))
+        probs = jnp.exp(logits - lse).astype(LOW)
+        lse_ref[0, pl.ds(head, 1), :] = lse
+        heads_out = across(probs, rows_of(qkv_ref, pl.ds(2 * model + base, width))).astype(LOW)
+        put_rows(out_ref, window, mask, heads_out)
+
+
+def attend_back_kernel(model, lengths_ref, qkv_ref, d_heads_ref, lse_ref, out_ref):
+    slots = qkv_ref.shape[0] * qkv_ref.shape[2]
+    length = lengths_ref[pl.program_id(0)]
+    scale = 1.0 / math.sqrt(HEAD_DIM)
+    for head in range(model // HEAD_DIM):
+        base, width, offset = head_window(head)
+        mask = lane_mask(slots, width, offset)
+        window = pl.ds(base, width)
+        key_window = pl.ds(model + base, width)
+        value_window = pl.ds(2 * model + base, width)
+        zero = jnp.zeros((), LOW)
+        queries = jnp.where(mask, rows_of(qkv_ref, window), zero)
+        d_heads = jnp.where(mask, rows_of(d_heads_ref, window), zero)
+        keys = rows_of(qkv_ref, key_window)
+        logits = score_rows(queries, keys, length, slots)
+        probs = jnp.exp(logits - lse_ref[0, pl.ds(head, 1), :])
+        d_probs = against(rows_of(qkv_ref, value_window), d_heads)
+        weighted = probs * d_probs
+        d_logits = (weighted - probs * jnp.sum(weighted, 0, keepdims=True)).astype(LOW)
+        d_queries = (across(d_logits, keys) * scale).astype(LOW)
+        d_keys = (project(d_logits, queries) * scale).astype(LOW)
+        d_values = project(probs.astype(LOW), d_heads).astype(LOW)
+        put_rows(out_ref, window, mask, d_queries)
+        put_rows(out_ref, key_window, mask, d_keys)
+        put_rows(out_ref, value_window, mask, d_values)
+
+
+def item_block(parts, part, cols):
+    return pl.BlockSpec((parts, 1, part, cols), lambda i: (0, i, 0, 0))
+
+
+def lse_block(heads, slots):
+    return pl.BlockSpec((1, heads, slots), lambda i: (i, 0, 0))
+
+
+def attend(lengths, qkv, model):
+    parts, items, part = qkv.shape[:3]
+    slots = parts * part
+    heads = model // HEAD_DIM
+    return pl.pallas_call(
+        functools.partial(attend_kernel, model),
+        grid=(items,),
+        out_shape=[
+            jax.ShapeDtypeStruct((parts, items, part, model), LOW),
+            jax.ShapeDtypeStruct((items, heads, slots), jnp.float32),
+        ],
+        in_specs=[pl.BlockSpec(memory_space=pltpu.SMEM), item_block(parts, part, 3 * model)],
+        out_specs=[item_block(parts, part, model), lse_block(heads, slots)],
+        compiler_params=pltpu.CompilerParams(vmem_limit_bytes=ATTN_VMEM),
+        name="attend",
+    )(lengths, qkv)
+
+
+def attend_back(lengths, qkv, d_heads, lse, model):
+    parts, items, part = qkv.shape[:3]
+    slots = parts * part
+    heads = model // HEAD_DIM
+    return pl.pallas_call(
+        functools.partial(attend_back_kernel, model),
+        grid=(items,),
+        out_shape=jax.ShapeDtypeStruct((parts, items, part, 3 * model), LOW),
+        in_specs=[
+            pl.BlockSpec(memory_space=pltpu.SMEM),
+            item_block(parts, part, 3 * model),
+            item_block(parts, part, model),
+            lse_block(heads, slots),
+        ],
+        out_specs=item_block(parts, part, 3 * model),
+        compiler_params=pltpu.CompilerParams(vmem_limit_bytes=ATTN_VMEM),
+        name="attend_back",
+    )(lengths, qkv, d_heads, lse)
+
+
 def halves_by_core(place, both):
-    half = both.shape[1] // 2
-    mine = lax.dynamic_slice_in_dim(both, place.c * half, half, 1)
-    got = place.swap_c(lax.dynamic_slice_in_dim(both, (1 - place.c) * half, half, 1))
+    half = both.shape[2] // 2
+    mine = lax.dynamic_slice_in_dim(both, place.c * half, half, 2)
+    got = place.swap_c(lax.dynamic_slice_in_dim(both, (1 - place.c) * half, half, 2))
     first = place.c == 0
-    return jnp.concatenate([jnp.where(first, mine, got), jnp.where(first, got, mine)], 0)
+    return jnp.concatenate([jnp.where(first, mine, got), jnp.where(first, got, mine)], 1)
 
 
 def gather_columns(place, block):
@@ -302,10 +433,9 @@
     return full.reshape(depth * CHIP_X * CHIP_Y * CORES * rows, cols)
 
 
-def gather_fc2(place, low):
+def gather_fc2(place, low, kept):
     rows, cols = low.shape
     half = rows // 2
-    kept = plane_gather(place, low[:half], low[half:])
     piece = jnp.concatenate(kept, 0)[None]
     (line,) = pack_line(place, *line_gather(place, piece), 1)
     other = place.swap_c(line)
@@ -335,11 +465,13 @@
     if place.short:
         return tuple(lax.all_gather(low, BOTH, axis=0, tiled=True) for low in lows)
     rows, unit = 2 * w_proj.shape[0], w_proj.shape[1]
+    pair = halves_by_core(place, jnp.stack([jnp.concatenate([w_qkv, w_proj], 1), w_fc1]))
+    half = w_fc2.shape[0] // 2
+    plane = plane_gather(place, w_fc2[:half], w_fc2[half:])
     skip = gather_skip(place, w_skip)
-    pair = jnp.concatenate([w_qkv, w_proj], 1)
-    qkv, proj = assemble_qkvp(place, gather_columns(place, halves_by_core(place, pair)), rows, unit)
-    fc1 = assemble_fc1(place, gather_columns(place, halves_by_core(place, w_fc1)), rows, unit)
-    fc2 = gather_fc2(place, w_fc2)
+    qkv, proj = assemble_qkvp(place, gather_columns(place, pair[0]), rows, unit)
+    fc1 = assemble_fc1(place, gather_columns(place, pair[1]), rows, unit)
+    fc2 = gather_fc2(place, w_fc2, plane)
     return skip, qkv, proj, fc1, fc2
 
 
@@ -424,11 +556,18 @@
     seconds = (sq_skip, sq_qkv, sq_proj, sq_fc1, sq_fc2)
     model = tokens.shape[-1]
 
-    token_rows = lax.all_to_all(tokens, "narrow", split_axis=0, concat_axis=1, tiled=True)
-    skip_rows = lax.all_to_all(skip_store, "narrow", split_axis=0, concat_axis=2, tiled=True)
-    cot_rows = lax.all_to_all(cotangent, "narrow", split_axis=0, concat_axis=1, tiled=True)
-    items, slots = token_rows.shape[:2]
+    items, part = tokens.shape[0] // narrow, tokens.shape[1]
+    slots = narrow * part
     rows = items * slots
+
+    def swap_items(value):
+        value = value.reshape(narrow, items, *value.shape[1:])
+        return lax.all_to_all(value, "narrow", 0, 0, tiled=True)
+
+    token_rows = swap_items(tokens).reshape(rows, model)
+    skip_rows = swap_items(skip_store).reshape(narrow, items, narrow, part, model // narrow)
+    skip_rows = skip_rows.transpose(2, 1, 3, 0, 4).reshape(rows, model)
+    cot_rows = swap_items(cotangent)
     lengths = lax.dynamic_slice_in_dim(lengths, lax.axis_index("narrow") * items, items)
 
     table_low = norm_table.astype(LOW)
@@ -439,34 +578,26 @@
     lows = tuple(matrix.astype(LOW) for matrix in masters)
     full_skip, full_qkv, full_proj, full_fc1, full_fc2 = gather_weights(place, lows)
 
-    joined = jnp.concatenate([token_rows, skip_rows], -1).reshape(rows, 2 * model)
+    joined = jnp.concatenate([token_rows, skip_rows], -1)
     first = project(joined, full_skip)
     normed_one, inv_one = norm_stats(first)
     act_one = (normed_one * table[0] + table[1]).astype(LOW)
     projected = project(act_one, full_qkv).astype(LOW)
-    heads = model // HEAD_DIM
-    split = projected.reshape(items, slots, 3, heads, HEAD_DIM)
-    queries, keys, values = split[:, :, 0], split[:, :, 1], split[:, :, 2]
-    key_valid = jnp.arange(slots, dtype=jnp.int32)[None, :] < lengths[:, None]
-    scale = 1.0 / math.sqrt(HEAD_DIM)
-    logits = jnp.einsum("inhd,imhd->ihnm", queries, keys, preferred_element_type=jnp.float32) * scale
-    logits = jnp.where(key_valid[:, None, None, :], logits, NEGATIVE)
-    row_max = jnp.max(logits, -1, keepdims=True)
-    log_total = row_max + jnp.log(jnp.sum(jnp.exp(logits - row_max), -1, keepdims=True))
-    probs = jnp.exp(logits - log_total)
-    probs_low = probs.astype(LOW)
-    heads_out = (
-        jnp.einsum("ihnm,imhd->inhd", probs_low, values, preferred_element_type=jnp.float32)
-        .astype(LOW)
-        .reshape(rows, model)
-    )
+    qkv = projected.reshape(narrow, items, part, 3 * model)
+    heads_out, lse = attend(lengths, qkv, model)
+    heads_out = heads_out.reshape(rows, model)
     second = first + project(heads_out, full_proj)
     normed_two, inv_two = norm_stats(second)
     act_two = (normed_two * table[2] + table[3]).astype(LOW)
     pre_act = project(act_two, full_fc1)
     hidden = jax.nn.gelu(pre_act).astype(LOW)
-    block_rows = (second + project(hidden, full_fc2)).astype(LOW).reshape(items, slots, model)
-    block_out = lax.all_to_all(block_rows, "narrow", split_axis=1, concat_axis=0, tiled=True)
+    block_rows = (second + project(hidden, full_fc2)).astype(LOW)
+
+    def swap_back(value):
+        value = value.reshape(narrow, items, part, model)
+        return lax.all_to_all(value, "narrow", 0, 0, tiled=True).reshape(narrow * items, part, model)
+
+    block_out = swap_back(block_rows)
 
     grad_out = cot_rows.reshape(rows, model)
     if place.short:
@@ -488,20 +619,8 @@
     d_act_two = against(d_pre, full_fc1)
     d_second = grad_out.astype(jnp.float32) + norm_back(d_act_two, normed_two, inv_two, table[2])
     d_second_low = d_second.astype(LOW)
-    d_heads = against(d_second_low, full_proj).astype(LOW).reshape(items, slots, heads, HEAD_DIM)
-    d_probs = jnp.einsum("inhd,imhd->ihnm", d_heads, values, preferred_element_type=jnp.float32)
-    d_logits = (probs * (d_probs - jnp.sum(probs * d_probs, -1, keepdims=True))).astype(LOW)
-    d_queries = jnp.einsum("ihnm,imhd->inhd", d_logits, keys, preferred_element_type=jnp.float32)
-    d_keys = jnp.einsum("ihnm,inhd->imhd", d_logits, queries, preferred_element_type=jnp.float32)
-    d_values = jnp.einsum("ihnm,inhd->imhd", probs_low, d_heads, preferred_element_type=jnp.float32)
-    d_projected = jnp.concatenate(
-        [
-            (d_queries * scale).astype(LOW).reshape(rows, model),
-            (d_keys * scale).astype(LOW).reshape(rows, model),
-            d_values.astype(LOW).reshape(rows, model),
-        ],
-        -1,
-    )
+    d_heads = against(d_second_low, full_proj).astype(LOW).reshape(narrow, items, part, model)
+    d_projected = attend_back(lengths, qkv, d_heads, lse, model).reshape(rows, 3 * model)
     if place.short:
         grad_qkv = lax.psum_scatter(across(act_one, d_projected), BOTH, scatter_dimension=0, tiled=True)
         grad_proj = lax.psum_scatter(across(heads_out, d_second_low), BOTH, scatter_dimension=0, tiled=True)
@@ -524,9 +643,11 @@
         grad_skip_lin = lax.psum_scatter(across(joined, d_first_low), BOTH, scatter_dimension=0, tiled=True)
     else:
         grad_skip_lin = scatter_skip(place, joined, d_first_low)
-    d_joined = against(d_first_low, full_skip).astype(LOW).reshape(items, slots, 2 * model)
-    grad_tokens = lax.all_to_all(d_joined[:, :, :model], "narrow", split_axis=1, concat_axis=0, tiled=True)
-    grad_skip = lax.all_to_all(d_joined[:, :, model:], "narrow", split_axis=2, concat_axis=0, tiled=True)
+    d_joined = against(d_first_low, full_skip).astype(LOW)
+    grad_tokens = swap_back(d_joined[:, :model])
+    d_skip = d_joined[:, model:].reshape(narrow, items, part, narrow, model // narrow)
+    d_skip = d_skip.transpose(3, 1, 0, 2, 4).reshape(narrow, items, slots, model // narrow)
+    grad_skip = lax.all_to_all(d_skip, "narrow", 0, 0, tiled=True).reshape(skip_store.shape)
 
     table_grads = jnp.stack(
         [

time: 2480 us -> 881 us (0.36)
  Pallas kernels: 1410 us -> 73 us
  waiting for transfers between devices: 347 us -> 243 us
  local copies, waits for them, and re-layouts: 166 us -> 93.5 us
  matrix products: 213 us -> 166 us
  other arithmetic: 101 us -> 63.7 us
    pallas_call x8, Pallas kernels: 1410 us -> 39.4 us  [run_moves(): pl.pallas_call(body, out_shape=out_shapes, in_specs=[pl.BlockSpec(memory_...]
    ppermute x24, waiting for transfers between devices: 119 us -> 40.4 us  [up_z(): lax.ppermute(value, 'wide', [(i, i + CHIP_X) for i in range(self.wide - C...]
    dot_general x6 -> x0, matrix products: 56 us -> none  [the longest x1 18 us: local(): jnp.einsum('inhd,imhd->ihnm', d_heads, values, preferred_element_type=jnp...]
    pallas_call x0 -> x2, Pallas kernels: none -> 33.6 us  [the longest x1 21 us: attend_back(): pl.pallas_call(functools.partial(attend_back_kernel, model), grid=(items,...]
    reshape x10 -> x4, local copies, waits for them, and re-layouts: 42.5 us -> 11.1 us  [the longest x2 4.51 us: local(): d_joined[:, model:].reshape(narrow, items, part, narrow, model // narrow)]
    ppermute x16, waiting for transfers between devices: 62.7 us -> 34 us  [swap_x(): return lax.ppermute(value, 'wide', [(i, i ^ 1) for i in range(self.wide)])]
  transfers between devices with their start and end apart: 113 -> 112, of which waited for: 38 -> 50; matrix products, arithmetic and copies ran while one was open for 10% -> 32% of each run, Pallas kernels for 24% -> 8%
where the time goes in v2:
time: 881 us; the launch traced here: 869 us
  waiting for transfers between devices  243 us (28%)
  starting transfers between devices  224 us (25%)
  matrix products  166 us (19%)
  local copies, waits for them, and re-layouts  93.5 us (11%)
  Pallas kernels  73 us (8%)
  other arithmetic  63.7 us (7%)
    ppermute x24, starting transfers between devices, up_z(): lax.ppermute(value, 'wide', [(i, i + CHIP_X) for i in range(self.wide - C...  107 us
    ppermute x24, waiting for transfers between devices, down_z(): lax.ppermute(value, 'wide', [(i + CHIP_X, i) for i in range(self.wide - C...  90.7 us
    dot_general x11, matrix products, across(): lax.dot_general(left, right, (((0,), (0,)), ((), ())), preferred_element_...  61.2 us
    ppermute x16, waiting for transfers between devices, swap_y(): lax.ppermute(value, 'narrow', [(i, i ^ 2) for i in range(self.narrow)])  54.6 us
    dot_general x5, matrix products, against(): lax.dot_general(left, right, (((1,), (1,)), ((), ())), preferred_element_...  54.2 us
    dot_general x5, matrix products, project(): return jnp.dot(left, right, preferred_element_type=jnp.float32)  50.2 us
    ppermute x24, waiting for transfers between devices, up_z(): lax.ppermute(value, 'wide', [(i, i + CHIP_X) for i in range(self.wide - C...  40.4 us
    pallas_call x8, Pallas kernels, run_moves(): pl.pallas_call(body, out_shape=out_shapes, in_specs=[pl.BlockSpec(memory_...  39.4 us
  transfers between devices with their start and end apart: 112, of which 50 were waited for; matrix products, arithmetic and copies ran while one was open for 32% of the time, Pallas kernels for 8%

profile of v2, /device:TPU:0, one launch (start us, length us, event | category | flops | bytes accessed | tf_op | source)
XLA Modules:
  0.0 869.1 jit_solution(2062276413306258169)
XLA Ops:
  1.8 4.9 collective-permute-start
  14.4 4.6 collective-permute-start.2
  50.0 4.4 collective-permute-done.20.refs_4_
  61.3 5.1 collective-permute-done.22.refs_5_
  70.8 4.9 all-to-all-start.2
  103.5 5.3 collective-permute-start.35
  110.8 4.7 collective-permute-done.35.refs_2_
  115.4 4.8 collective-permute-done.36.refs_5_
  124.8 12.0 %collective-permute-done.26 = bf16[4,72,1152]{2,1,0:T(8,128)(2,1)S(1)} collective-permute-done((bf16[4,72,1152]{2,1,0:T(8,128)(2,1)S(1)}, bf16[4,72,1152]{2,1,0:T(8,128)(2,1)S(1)}, u32[]{:S(2)}, u32[]{:S(2)}) %collective-permute-start.26) | collective-permute-done | bytes 663584 | tf_op jit(solution)/shard_map/ppermute | solution.py:37
  147.5 10.0 %collective-permute-done.38.refs_6_ = bf16[2,72,1152]{2,1,0:T(8,128)(2,1)S(1)} collective-permute-done((bf16[2,72,1152]{2,1,0:T(8,128)(2,1)}, bf16[2,72,1152]{2,1,0:T(8,128)(2,1)S(1)}, u32[]{:S(2)}, u32[]{:S(2)}) %collective-permute-start.38) | collective-permute-done | bytes 331808 | tf_op jit(solution)/shard_map/ppermute | solution.py:46
  162.9 4.7 collective-permute-start.47
  199.0 4.7 all-to-all-start.4
  203.6 7.5 fusion.168
  212.6 4.5 collective-permute-start.49
  225.8 6.5 assemble_qkvp.1
  232.4 13.6 %collective-permute-done.49.refs_2_ = bf16[1,8,72,1152]{3,2,1,0:T(8,128)(2,1)S(1)} collective-permute-done((bf16[1,8,72,1152]{3,2,1,0:T(8,128)(2,1)}, bf16[1,8,72,1152]{3,2,1,0:T(8,128)(2,1)S(1)}, u32[]{:S(2)}, u32[]{:S(2)}) %collective-permute-start.49) | collective-permute-done | bytes 1327136 | tf_op jit(solution)/shard_map/ppermute | solution.py:43
  253.6 9.5 %convolution_convert_fusion.5 = bf16[640,3456]{1,0:T(8,128)(2,1)S(1)} fusion(bf16[640,1152]{1,0:T(8,128)(2,1)S(1)} %copy-done.62, bf16[1152,3456]{1,0:T(8,128)(2,1)} %bitcast.452), kind=kOutput, calls=%fused_computation.22 | convolution fusion | flops 5098291200 | bytes 13860864 | tf_op jit(solution)/shard_map/dot_general | solution.py:161
  263.1 12.6 %attend.1 = (bf16[4,2,80,1152]{3,2,1,0:T(8,128)(2,1)S(1)}, f32[2,16,320]{2,1,0:T(8,128)S(1)}) custom-call(s32[2]{0:T(128)S(1)} %dynamic_slice.253.lengths_ref, bf16[4,2,80,3456]{3,2,1,0:T(8,128)(2,1)S(1)} %bitcast.400), custom_call_target="tpu_custom_call" | custom-call | tf_op jit(solution)/shard_map/attend/pallas_call | solution.py:286
  275.8 4.7 fusion.169
  283.6 5.2 pack_line.7.refs_0_
  291.4 7.3 assemble_fc1.1
  298.7 13.0 %fusion.170 = f32[640,4608]{1,0:T(8,128)} fusion(bf16[640,1152]{1,0:T(8,128)(2,1)S(1)} %add_convert_fusion.5, bf16[1152,4608]{1,0:T(8,128)(2,1)} %bitcast.425), kind=kOutput, calls=%fused_computation.421 | convolution fusion | flops 6794772480 | bytes 23887872 | tf_op jit(solution)/shard_map/dot_general | solution.py:161
  311.7 15.7 %convolution_convert_fusion = bf16[4608,1152]{1,0:T(8,128)(2,1)} fusion(bf16[640,1152]{1,0:T(8,128)(2,1)} %bitcast.46, f32[640,4608]{1,0:T(8,128)} %fusion.170), kind=kOutput, calls=%fused_computation | convolution fusion | flops 6826622976 | bytes 23887872 | tf_op jit(solution)/shard_map/dot_general | solution.py:165
  327.3 8.8 %constant_dynamic-slice_fusion.5 = (bf16[4,2,2,1,2,72,1152]{6,5,4,3,2,1,0:T(8,128)(2,1)}, bf16[4,2,2,1,2,72,1152]{6,5,4,3,2,1,0:T(8,128)(2,1)}) fusion(bf16[4,2,2,2,2,72,1152]{6,5,4,3,2,1,0:T(8,128)(2,1)} %bitcast.427, s32[]{:T(128)S(6)} %select_n.207, s32[]{:T(128)S(6)} %select_n.208), kind=kLoop, calls=%fused_computation.357 | loop fusion | bytes 21233672 | tf_op jit(solution)/shard_map/jit(dynamic_index_in_dim)/dynamic_slice | solution.py:132
  336.1 5.3 copy.279
  341.9 9.1 %assemble_fc2.1 = bf16[4,2,2,2,2,72,1152]{6,5,4,3,2,1,0:T(8,128)(2,1)} custom-call(s32[4]{0:T(128)S(1)} %pad_add_fusion.spot_ref, bf16[4,8,72,1152]{3,2,1,0:T(8,128)(2,1)} %pack_line.7.refs_0_, bf16[4,8,72,1152]{3,2,1,0:T(8,128)(2,1)} %collective-permute-done.53.refs_1_), custom_call_target="tpu_custom_call" | custom-call | tf_op jit(solution)/shard_map/assemble_fc2/pallas_call | solution.py:66
  351.0 19.9 %fusion.6 = bf16[640,4608]{1,0:T(8,128)(2,1)} fusion(f32[640,4608]{1,0:T(8,128)} %fusion.170, bf16[4608,1152]{1,0:T(8,128)(2,1)} %bitcast.423, bf16[640,1152]{1,0:T(8,128)(2,1)} %bitcast.46), kind=kOutput, calls=%fused_computation.9 | convolution fusion | flops 6853754880 | bytes 29786112 | tf_op jit(solution)/shard_map/dot_general | solution.py:171
  371.0 15.3 %multiply_reduce_fusion = (f32[1152]{0:T(1024)S(1)}, f32[640]{0:T(1024)S(1)}, f32[640]{0:T(1024)S(1)}, f32[1152]{0:T(1024)S(1)}, f32[640,1152]{1,0:T(8,128)}) fusion(f32[640,1152]{1,0:T(8,128)S(1)} %copy-done.34, f32[640]{0:T(1024)S(1)} %add_rsqrt_fusion, f32[640]{0:T(1024)S(1)} %broadcast_multiply_fusion.4, f32[1152]{0:T(1024)S(1)} %get-tuple-element.350, ...), kind=kOutput, calls=%fused_computation.39 | convolution fusion | flops 6801404928 | bytes 22437376 | tf_op jit(solution)/shard_map/dot_general | solution.py:171
  391.8 21.0 %attend_back.1 = bf16[4,2,80,3456]{3,2,1,0:T(8,128)(2,1)S(1)} custom-call(s32[2]{0:T(128)S(1)} %dynamic_slice.253.lengths_ref, bf16[4,2,80,3456]{3,2,1,0:T(8,128)(2,1)} %bitcast.401, bf16[4,2,80,1152]{3,2,1,0:T(8,128)(2,1)S(1)} %bitcast.413, f32[2,16,320]{2,1,0:T(8,128)S(1)} %get-tuple-element.162.lse_ref), custom_call_target="tpu_custom_call" | custom-call | tf_op jit(solution)/shard_map/attend_back/pallas_call | solution.py:304
  412.8 11.4 %multiply_reduce_fusion.1 = (f32[1152]{0:T(1024)S(1)}, f32[640]{0:T(1024)S(1)}, f32[640]{0:T(1024)S(1)}, f32[1152]{0:T(1024)S(1)}, f32[640,1152]{1,0:T(8,128)S(1)}) fusion(f32[640,1152]{1,0:T(8,128)S(1)} %copy-done.32, f32[640]{0:T(1024)S(1)} %add_rsqrt_fusion.1, f32[640]{0:T(1024)S(1)} %broadcast_multiply_fusion.5, f32[1152]{0:T(1024)S(1)} %get-tuple-element.353, ...), kind=kOutput, calls=%fused_computation.40 | convolution fusion | flops 5102711808 | bytes 18308608 | tf_op jit(solution)/shard_map/dot_general | solution.py:171
  424.2 5.4 convolution_convert_fusion.2
  431.1 5.7 convolution_convert_fusion.8
  436.7 5.4 convolution_convert_fusion.7
  442.1 15.5 %fusion.11 = bf16[640,1152]{1,0:T(8,128)(2,1)} fusion(f32[640,1152]{1,0:T(8,128)S(1)} %copy-done.34, bf16[4608,1152]{1,0:T(8,128)(2,1)} %bitcast.424, f32[640,4608]{1,0:T(8,128)} %fusion.170), kind=kOutput, calls=%fused_computation.34 | convolution fusion | flops 6822789120 | bytes 26836992 | tf_op jit(solution)/shard_map/dot_general | solution.py:161
  457.6 5.3 fusion.10
  464.8 4.8 collective-permute-start.61
  478.5 18.3 %collective-permute-done.62 = bf16[2,2,2,72,1152]{4,3,0,2,1:T(8,128)(2,1)S(1)} collective-permute-done((bf16[2,2,2,72,1152]{4,3,0,2,1:T(8,128)(2,1)S(1)}, bf16[2,2,2,72,1152]{4,3,0,2,1:T(8,128)(2,1)S(1)}, u32[]{:S(2)}, u32[]{:S(2)}) %collective-permute-start.62) | collective-permute-done | bytes 1327136 | tf_op jit(solution)/shard_map/ppermute | solution.py:46
  501.4 6.5 collective-permute-start.63
  507.9 5.3 convolution_convert_fusion.1
  515.8 4.9 all-to-all-start.8
  520.8 5.0 convolution_convert_fusion.6
  525.7 5.4 convolution_convert_fusion.4
  551.4 4.8 collective-permute-start.65
  558.0 4.8 add_convert_fusion.1
  563.2 4.6 add_convert_fusion
  567.9 15.3 %collective-permute-done.66 = bf16[2,2,2,72,1152]{4,3,0,2,1:T(8,128)(2,1)S(1)} collective-permute-done((bf16[2,2,2,72,1152]{4,3,0,2,1:T(8,128)(2,1)S(1)}, bf16[2,2,2,72,1152]{4,3,0,2,1:T(8,128)(2,1)S(1)}, u32[]{:S(2)}, u32[]{:S(2)}) %collective-permute-start.66) | collective-permute-done | bytes 1327136 | tf_op jit(solution)/shard_map/ppermute | solution.py:46
  590.4 4.7 collective-permute-done.67
  610.3 22.7 %collective-permute-done.71 = bf16[4,2,72,1152]{3,2,0,1:T(8,128)(2,1)S(1)} collective-permute-done((bf16[4,2,72,1152]{3,2,0,1:T(8,128)(2,1)S(1)}, bf16[4,2,72,1152]{3,2,0,1:T(8,128)(2,1)S(1)}, u32[]{:S(2)}, u32[]{:S(2)}) %collective-permute-start.71) | collective-permute-done | bytes 1327136 | tf_op jit(solution)/shard_map/ppermute | solution.py:34
  640.4 7.1 collective-permute-done.73
  651.1 5.0 collective-permute-start.83
  663.0 5.0 collective-permute-start.85
  671.2 4.7 collective-permute-done.85
  691.1 19.1 %collective-permute-done.76 = bf16[4,2,72,1152]{3,2,0,1:T(8,128)(2,1)S(1)} collective-permute-done((bf16[4,2,72,1152]{3,2,0,1:T(8,128)(2,1)S(1)}, bf16[4,2,72,1152]{3,2,0,1:T(8,128)(2,1)S(1)}, u32[]{:S(2)}, u32[]{:S(2)}) %collective-permute-start.76) | collective-permute-done | bytes 1327136 | tf_op jit(solution)/shard_map/ppermute | solution.py:37
  713.9 10.3 %collective-permute-done.77 = bf16[4,72,1152]{2,1,0:T(8,128)(2,1)S(1)} collective-permute-done((bf16[4,72,1152]{2,1,0:T(8,128)(2,1)S(1)}, bf16[4,72,1152]{2,1,0:T(8,128)(2,1)S(1)}, u32[]{:S(2)}, u32[]{:S(2)}) %collective-permute-start.77) | collective-permute-done | bytes 663584 | tf_op jit(solution)/shard_map/ppermute | solution.py:37
  727.7 6.0 collective-permute-start.89
  743.0 5.0 collective-permute-start.91
  748.3 4.7 collective-permute-done.92
  769.8 5.0 collective-permute-start.95
  779.8 5.7 collective-permute-start.97
  791.8 16.2 %all-to-all-done.5 = bf16[4,2,80,1152]{3,2,1,0:T(8,128)(2,1)S(1)} async-done(((bf16[4,2,80,1152]{3,2,1,0:T(8,128)(2,1)}), bf16[4,2,80,1152]{3,2,1,0:T(8,128)(2,1)S(1)}, u32[]{:S(2)}, u32[]{:S(2)}) %all-to-all-start.5) | async-done | bytes 1474592 | tf_op jit(solution)/shard_map/all_to_all | solution.py:598
  818.9 4.8 collective-permute-start.99
  829.1 6.6 stack.246
  836.3 7.5 all-to-all-start.7
  844.5 6.4 all-to-all-done.7
  (549 shorter events, 337.6 us)
Async XLA Ops:
  14.2 17.8 %collective-permute-start.18 = (bf16[2,36,2304]{2,1,0:T(8,128)(2,1)S(1)}, bf16[2,36,2304]{2,1,0:T(8,128)(2,1)S(1)}, u32[]{:S(2)}, u32[]{:S(2)}) collective-permute-start(bf16[2,36,2304]{2,1,0:T(8,128)(2,1)S(1)} %fusion.81), channel_id=1, source_target_pairs={{0,1},{1,0},{2,3},{3,2},{4,5},{5,4},{6,7},{7,6},{8,9},{9,8},{10,11... | collective-permute-start | bytes 995336 | tf_op jit(solution)/shard_map/ppermute | solution.py:40
  20.4 19.6 %collective-permute-start.8 = (bf16[2,72,1152]{2,1,0:T(8,128)(2,1)S(1)}, bf16[2,72,1152]{2,1,0:T(8,128)(2,1)S(1)}, u32[]{:S(2)}, u32[]{:S(2)}) collective-permute-start(bf16[2,72,1152]{2,1,0:T(8,128)(2,1)S(1)} %pad_maximum_fusion.13), channel_id=1, source_target_pairs={{0,2},{1,3},{2,0},{3,1},{4,6},{5,7},{6,4},{7,5},{8,10},{9,11},{10,... | collective-permute-start | bytes 995336 | tf_op jit(solution)/shard_map/ppermute | solution.py:37
  20.9 19.1 %collective-permute-start.9 = (bf16[2,72,1152]{2,1,0:T(8,128)(2,1)S(1)}, bf16[2,72,1152]{2,1,0:T(8,128)(2,1)S(1)}, u32[]{:S(2)}, u32[]{:S(2)}) collective-permute-start(bf16[2,72,1152]{2,1,0:T(8,128)(2,1)S(1)} %pad_maximum_fusion.14), channel_id=1, source_target_pairs={{0,4},{4,0},{8,12},{12,8},{16,20},{20,16},{24,28},{28,24},{1,5},{5... | collective-permute-start | bytes 995336 | tf_op jit(solution)/shard_map/ppermute | solution.py:34
  48.6 44.2 %collective-permute-start.12 = (bf16[2,4,72,640]{3,2,1,0:T(8,128)(2,1)S(1)}, bf16[2,4,72,640]{3,2,1,0:T(8,128)(2,1)S(1)}, u32[]{:S(2)}, u32[]{:S(2)}) collective-permute-start(bf16[2,4,72,640]{3,2,1,0:T(8,128)(2,1)S(1)} %pad_maximum_fusion.8.refs_0_), channel_id=1, source_target_pairs={{0,2},{1,3},{2,0},{3,1},{4,6},{5,7},{6,4},{7,5},{8,10},{9,11},{10,... | collective-permute-start | bytes 2211848 | tf_op jit(solution)/shard_map/ppermute | solution.py:37
  59.4 33.3 %collective-permute-start.13 = (bf16[2,4,72,512]{3,2,1,0:T(8,128)(2,1)}, bf16[2,4,72,512]{3,2,1,0:T(8,128)(2,1)}, u32[]{:S(2)}, u32[]{:S(2)}) collective-permute-start(bf16[2,4,72,512]{3,2,1,0:T(8,128)(2,1)} %pad_maximum_fusion.10.refs_2_), channel_id=1, source_target_pairs={{0,4},{4,0},{8,12},{12,8},{16,20},{20,16},{24,28},{28,24},{1,5},{5... | collective-permute-start | bytes 1769480 | tf_op jit(solution)/shard_map/ppermute | solution.py:34
  70.8 25.1 %all-to-all-start.2 = ((bf16[32,1,144]{2,1,0:T(2,128)(2,1)}), bf16[32,1,144]{2,1,0:T(2,128)(2,1)S(1)}, u32[]{:S(2)}, u32[]{:S(2)}) async-start(bf16[32,1,144]{2,1,0:T(2,128)(2,1)} %broadcast_in_dim.14), calls=%async_computation.2 | async-start | bytes 65536 | tf_op jit(solution)/shard_map/all_to_all | solution.py:575
  78.4 25.1 %collective-permute-start.33 = (bf16[2,72,1152]{2,1,0:T(8,128)(2,1)S(1)}, bf16[2,72,1152]{2,1,0:T(8,128)(2,1)}, u32[]{:S(2)}, u32[]{:S(2)}) collective-permute-start(bf16[2,72,1152]{2,1,0:T(8,128)(2,1)S(1)} %pad_maximum_fusion.16.refs_0_), channel_id=1, source_target_pairs={{0,8},{4,12},{8,16},{12,20},{16,24},{20,28},{1,9},{5,13},{9,17},{1... | collective-permute-start | bytes 995336 | tf_op jit(solution)/shard_map/ppermute | solution.py:43
  82.7 20.8 %collective-permute-start.34 = (bf16[2,72,1152]{2,1,0:T(8,128)(2,1)S(1)}, bf16[2,72,1152]{2,1,0:T(8,128)(2,1)}, u32[]{:S(2)}, u32[]{:S(2)}) collective-permute-start(bf16[2,72,1152]{2,1,0:T(8,128)(2,1)S(1)} %pad_maximum_fusion.16.refs_0_), channel_id=1, source_target_pairs={{8,0},{12,4},{16,8},{20,12},{24,16},{28,20},{9,1},{13,5},{17,9},{2... | collective-permute-start | bytes 995336 | tf_op jit(solution)/shard_map/ppermute | solution.py:46
  92.8 30.7 %collective-permute-start.25 = (bf16[4,72,1152]{2,1,0:T(8,128)(2,1)S(1)}, bf16[4,72,1152]{2,1,0:T(8,128)(2,1)}, u32[]{:S(2)}, u32[]{:S(2)}) collective-permute-start(bf16[4,72,1152]{2,1,0:T(8,128)(2,1)S(1)} %get-tuple-element.137), channel_id=1, source_target_pairs={{0,4},{4,0},{8,12},{12,8},{16,20},{20,16},{24,28},{28,24},{1,5},{5... | collective-permute-start | bytes 1990664 | tf_op jit(solution)/shard_map/ppermute | solution.py:34
  96.0 43.8 %all-to-all-start.1 = ((bf16[4,2,320,288]{2,3,1,0:T(8,128)(2,1)}), bf16[4,2,320,288]{2,3,1,0:T(8,128)(2,1)}, u32[]{:S(2)}, u32[]{:S(2)}) async-start(bf16[4,2,320,288]{2,3,1,0:T(8,128)(2,1)} %bitcast.438), calls=%async_computation.1 | async-start | bytes 3538944 | tf_op jit(solution)/shard_map/all_to_all | solution.py:565
  101.5 35.2 %collective-permute-start.26 = (bf16[4,72,1152]{2,1,0:T(8,128)(2,1)S(1)}, bf16[4,72,1152]{2,1,0:T(8,128)(2,1)S(1)}, u32[]{:S(2)}, u32[]{:S(2)}) collective-permute-start(bf16[4,72,1152]{2,1,0:T(8,128)(2,1)S(1)} %get-tuple-element.138), channel_id=1, source_target_pairs={{0,2},{1,3},{2,0},{3,1},{4,6},{5,7},{6,4},{7,5},{8,10},{9,11},{10,... | collective-permute-start | bytes 1990664 | tf_op jit(solution)/shard_map/ppermute | solution.py:37
  110.8 33.3 %collective-permute-start.16 = (bf16[2,4,72,512]{3,2,1,0:T(8,128)(2,1)}, bf16[2,4,72,512]{3,2,1,0:T(8,128)(2,1)}, u32[]{:S(2)}, u32[]{:S(2)}) collective-permute-start(bf16[2,4,72,512]{3,2,1,0:T(8,128)(2,1)} %pad_maximum_fusion.10.refs_2_), channel_id=1, source_target_pairs={{0,1},{1,0},{2,3},{3,2},{4,5},{5,4},{6,7},{7,6},{8,9},{9,8},{10,11... | collective-permute-start | bytes 1769480 | tf_op jit(solution)/shard_map/ppermute | solution.py:40
  120.3 24.4 %collective-permute-start.37 = (bf16[2,72,1152]{2,1,0:T(8,128)(2,1)}, bf16[2,72,1152]{2,1,0:T(8,128)(2,1)}, u32[]{:S(2)}, u32[]{:S(2)}) collective-permute-start(bf16[2,72,1152]{2,1,0:T(8,128)(2,1)} %collective-permute-done.35.refs_2_), channel_id=1, source_target_pairs={{0,8},{4,12},{8,16},{12,20},{16,24},{20,28},{1,9},{5,13},{9,17},{1... | collective-permute-start | bytes 995336 | tf_op jit(solution)/shard_map/ppermute | solution.py:43
  138.0 57.6 %collective-permute-start.27 = (bf16[2,4,72,1152]{3,2,1,0:T(8,128)(2,1)S(1)}, bf16[2,4,72,1152]{3,2,1,0:T(8,128)(2,1)}, u32[]{:S(2)}, u32[]{:S(2)}) collective-permute-start(bf16[2,4,72,1152]{3,2,1,0:T(8,128)(2,1)S(1)} %pad_maximum_fusion.1.refs_0_), channel_id=1, source_target_pairs={{0,2},{1,3},{2,0},{3,1},{4,6},{5,7},{6,4},{7,5},{8,10},{9,11},{10,... | collective-permute-start | bytes 3981320 | tf_op jit(solution)/shard_map/ppermute | solution.py:37
  138.4 57.2 %collective-permute-start.28 = (bf16[2,4,72,1152]{3,2,1,0:T(8,128)(2,1)S(1)}, bf16[2,4,72,1152]{3,2,1,0:T(8,128)(2,1)}, u32[]{:S(2)}, u32[]{:S(2)}) collective-permute-start(bf16[2,4,72,1152]{3,2,1,0:T(8,128)(2,1)S(1)} %pad_maximum_fusion.2.refs_2_), channel_id=1, source_target_pairs={{0,4},{4,0},{8,12},{12,8},{16,20},{20,16},{24,28},{28,24},{1,5},{5... | collective-permute-start | bytes 3981320 | tf_op jit(solution)/shard_map/ppermute | solution.py:34
  139.7 21.8 %collective-permute-start.14 = (bf16[2,4,72,640]{3,2,1,0:T(8,128)(2,1)S(1)}, bf16[2,4,72,640]{3,2,1,0:T(8,128)(2,1)}, u32[]{:S(2)}, u32[]{:S(2)}) collective-permute-start(bf16[2,4,72,640]{3,2,1,0:T(8,128)(2,1)S(1)} %pad_maximum_fusion.8.refs_0_), channel_id=1, source_target_pairs={{0,1},{1,0},{2,3},{3,2},{4,5},{5,4},{6,7},{7,6},{8,9},{9,8},{10,11... | collective-permute-start | bytes 2211848 | tf_op jit(solution)/shard_map/ppermute | solution.py:40
  139.7 59.2 %all-to-all-start = ((bf16[4,2,80,1152]{3,2,1,0:T(8,128)(2,1)}), bf16[4,2,80,1152]{3,2,1,0:T(8,128)(2,1)}, u32[]{:S(2)}, u32[]{:S(2)}) async-start(bf16[4,2,80,1152]{3,2,1,0:T(8,128)(2,1)} %bitcast.439), calls=%async_computation | async-start | bytes 2949120 | tf_op jit(solution)/shard_map/all_to_all | solution.py:565
  144.1 23.5 %collective-permute-start.15 = (bf16[2,4,72,640]{3,2,1,0:T(8,128)(2,1)}, bf16[2,4,72,640]{3,2,1,0:T(8,128)(2,1)S(1)}, u32[]{:S(2)}, u32[]{:S(2)}) collective-permute-start(bf16[2,4,72,640]{3,2,1,0:T(8,128)(2,1)} %copy-done.5), channel_id=1, source_target_pairs={{0,1},{1,0},{2,3},{3,2},{4,5},{5,4},{6,7},{7,6},{8,9},{9,8},{10,11... | collective-permute-start | bytes 2211848 | tf_op jit(solution)/shard_map/ppermute | solution.py:40
  161.6 50.6 %collective-permute-start.29 = (bf16[2,4,72,1152]{3,2,1,0:T(8,128)(2,1)S(1)}, bf16[2,4,72,1152]{3,2,1,0:T(8,128)(2,1)}, u32[]{:S(2)}, u32[]{:S(2)}) collective-permute-start(bf16[2,4,72,1152]{3,2,1,0:T(8,128)(2,1)S(1)} %pad_maximum_fusion.1.refs_0_), channel_id=1, source_target_pairs={{0,1},{1,0},{2,3},{3,2},{4,5},{5,4},{6,7},{7,6},{8,9},{9,8},{10,11... | collective-permute-start | bytes 3981320 | tf_op jit(solution)/shard_map/ppermute | solution.py:40
  162.9 48.7 %collective-permute-start.47 = (bf16[1,8,72,1152]{3,2,1,0:T(8,128)(2,1)}, bf16[1,8,72,1152]{3,2,1,0:T(8,128)(2,1)}, u32[]{:S(2)}, u32[]{:S(2)}) collective-permute-start(bf16[1,8,72,1152]{3,2,1,0:T(8,128)(2,1)} %bitcast.41.refs_0_), channel_id=1, source_target_pairs={{0,8},{4,12},{8,16},{12,20},{16,24},{20,28},{1,9},{5,13},{9,17},{1... | collective-permute-start | bytes 3981320 | tf_op jit(solution)/shard_map/ppermute | solution.py:43
  168.5 43.6 %collective-permute-start.48 = (bf16[1,8,72,1152]{3,2,1,0:T(8,128)(2,1)}, bf16[1,8,72,1152]{3,2,1,0:T(8,128)(2,1)}, u32[]{:S(2)}, u32[]{:S(2)}) collective-permute-start(bf16[1,8,72,1152]{3,2,1,0:T(8,128)(2,1)} %bitcast.41.refs_0_), channel_id=1, source_target_pairs={{8,0},{12,4},{16,8},{20,12},{24,16},{28,20},{9,1},{13,5},{17,9},{2... | collective-permute-start | bytes 3981320 | tf_op jit(solution)/shard_map/ppermute | solution.py:46
  195.7 17.0 %collective-permute-start.39 = (bf16[4,72,1152]{2,1,0:T(8,128)(2,1)}, bf16[4,72,1152]{2,1,0:T(8,128)(2,1)}, u32[]{:S(2)}, u32[]{:S(2)}) collective-permute-start(bf16[4,72,1152]{2,1,0:T(8,128)(2,1)} %get-tuple-element.152), channel_id=1, source_target_pairs={{0,4},{4,0},{8,12},{12,8},{16,20},{20,16},{24,28},{28,24},{1,5},{5... | collective-permute-start | bytes 1990664 | tf_op jit(solution)/shard_map/ppermute | solution.py:34
  197.2 20.0 %collective-permute-start.40 = (bf16[4,72,1152]{2,1,0:T(8,128)(2,1)S(1)}, bf16[4,72,1152]{2,1,0:T(8,128)(2,1)}, u32[]{:S(2)}, u32[]{:S(2)}) collective-permute-start(bf16[4,72,1152]{2,1,0:T(8,128)(2,1)S(1)} %get-tuple-element.153), channel_id=1, source_target_pairs={{0,2},{1,3},{2,0},{3,1},{4,6},{5,7},{6,4},{7,5},{8,10},{9,11},{10,... | collective-permute-start | bytes 1990664 | tf_op jit(solution)/shard_map/ppermute | solution.py:37
  199.0 112.7 %all-to-all-start.4 = ((bf16[4,2,80,1152]{3,2,1,0:T(8,128)(2,1)}), bf16[4,2,80,1152]{3,2,1,0:T(8,128)(2,1)}, u32[]{:S(2)}, u32[]{:S(2)}) async-start(bf16[4,2,80,1152]{3,2,1,0:T(8,128)(2,1)} %bitcast.440), calls=%async_computation.4 | async-start | bytes 2949120 | tf_op jit(solution)/shard_map/all_to_all | solution.py:565
  212.6 33.4 %collective-permute-start.49 = (bf16[1,8,72,1152]{3,2,1,0:T(8,128)(2,1)}, bf16[1,8,72,1152]{3,2,1,0:T(8,128)(2,1)S(1)}, u32[]{:S(2)}, u32[]{:S(2)}) collective-permute-start(bf16[1,8,72,1152]{3,2,1,0:T(8,128)(2,1)} %collective-permute-done.47.refs_1_), channel_id=1, source_target_pairs={{0,8},{4,12},{8,16},{12,20},{16,24},{20,28},{1,9},{5,13},{9,17},{1... | collective-permute-start | bytes 3981320 | tf_op jit(solution)/shard_map/ppermute | solution.py:43
  217.1 32.9 %collective-permute-start.50 = (bf16[1,8,72,1152]{3,2,1,0:T(8,128)(2,1)}, bf16[1,8,72,1152]{3,2,1,0:T(8,128)(2,1)S(1)}, u32[]{:S(2)}, u32[]{:S(2)}) collective-permute-start(bf16[1,8,72,1152]{3,2,1,0:T(8,128)(2,1)} %collective-permute-done.48.refs_4_), channel_id=1, source_target_pairs={{8,0},{12,4},{16,8},{20,12},{24,16},{28,20},{9,1},{13,5},{17,9},{2... | collective-permute-start | bytes 3981320 | tf_op jit(solution)/shard_map/ppermute | solution.py:46
  222.8 68.5 %collective-permute-start.43 = (bf16[2,4,72,1152]{3,2,1,0:T(8,128)(2,1)S(1)}, bf16[2,4,72,1152]{3,2,1,0:T(8,128)(2,1)}, u32[]{:S(2)}, u32[]{:S(2)}) collective-permute-start(bf16[2,4,72,1152]{3,2,1,0:T(8,128)(2,1)S(1)} %pad_maximum_fusion.3.refs_0_), channel_id=1, source_target_pairs={{0,1},{1,0},{2,3},{3,2},{4,5},{5,4},{6,7},{7,6},{8,9},{9,8},{10,11... | collective-permute-start | bytes 3981320 | tf_op jit(solution)/shard_map/ppermute | solution.py:40
  222.9 57.6 %collective-permute-start.41 = (bf16[2,4,72,1152]{3,2,1,0:T(8,128)(2,1)S(1)}, bf16[2,4,72,1152]{3,2,1,0:T(8,128)(2,1)}, u32[]{:S(2)}, u32[]{:S(2)}) collective-permute-start(bf16[2,4,72,1152]{3,2,1,0:T(8,128)(2,1)S(1)} %pad_maximum_fusion.3.refs_0_), channel_id=1, source_target_pairs={{0,2},{1,3},{2,0},{3,1},{4,6},{5,7},{6,4},{7,5},{8,10},{9,11},{10,... | collective-permute-start | bytes 3981320 | tf_op jit(solution)/shard_map/ppermute | solution.py:37
  224.6 56.0 %collective-permute-start.42 = (bf16[2,4,72,1152]{3,2,1,0:T(8,128)(2,1)S(1)}, bf16[2,4,72,1152]{3,2,1,0:T(8,128)(2,1)}, u32[]{:S(2)}, u32[]{:S(2)}) collective-permute-start(bf16[2,4,72,1152]{3,2,1,0:T(8,128)(2,1)S(1)} %pad_maximum_fusion.4.refs_2_), channel_id=1, source_target_pairs={{0,4},{4,0},{8,12},{12,8},{16,20},{20,16},{24,28},{28,24},{1,5},{5... | collective-permute-start | bytes 3981320 | tf_op jit(solution)/shard_map/ppermute | solution.py:34
  250.1 31.0 %collective-permute-start.51 = (bf16[1,8,72,1152]{3,2,1,0:T(8,128)(2,1)S(1)}, bf16[1,8,72,1152]{3,2,1,0:T(8,128)(2,1)S(1)}, u32[]{:S(2)}, u32[]{:S(2)}) collective-permute-start(bf16[1,8,72,1152]{3,2,1,0:T(8,128)(2,1)S(1)} %collective-permute-done.49.refs_2_), channel_id=1, source_target_pairs={{0,8},{4,12},{8,16},{12,20},{16,24},{20,28},{1,9},{5,13},{9,17},{1... | collective-permute-start | bytes 3981320 | tf_op jit(solution)/shard_map/ppermute | solution.py:43
  252.3 31.4 %collective-permute-start.52 = (bf16[1,8,72,1152]{3,2,1,0:T(8,128)(2,1)S(1)}, bf16[1,8,72,1152]{3,2,1,0:T(8,128)(2,1)S(1)}, u32[]{:S(2)}, u32[]{:S(2)}) collective-permute-start(bf16[1,8,72,1152]{3,2,1,0:T(8,128)(2,1)S(1)} %collective-permute-done.50.refs_5_), channel_id=1, source_target_pairs={{8,0},{12,4},{16,8},{20,12},{24,16},{28,20},{9,1},{13,5},{17,9},{2... | collective-permute-start | bytes 3981320 | tf_op jit(solution)/shard_map/ppermute | solution.py:46
  288.8 53.1 %collective-permute-start.53 = (bf16[4,8,72,1152]{3,2,1,0:T(8,128)(2,1)}, bf16[4,8,72,1152]{3,2,1,0:T(8,128)(2,1)}, u32[]{:S(2)}, u32[]{:S(2)}) collective-permute-start(bf16[4,8,72,1152]{3,2,1,0:T(8,128)(2,1)} %pack_line.7.refs_0_), channel_id=1, source_target_pairs={{0,1},{1,0},{2,3},{3,2},{4,5},{5,4},{6,7},{7,6},{8,9},{9,8},{10,11... | collective-permute-start | bytes 15925256 | tf_op jit(solution)/shard_map/ppermute | solution.py:40
  341.4 116.2 %collective-permute-start.60 = (bf16[4,2,2,2,72,1152]{5,4,1,3,2,0:T(8,128)(2,1)}, bf16[4,2,2,2,72,1152]{5,4,1,3,2,0:T(8,128)(2,1)}, u32[]{:S(2)}, u32[]{:S(2)}) collective-permute-start(bf16[4,2,2,2,72,1152]{5,4,1,3,2,0:T(8,128)(2,1)} %bitcast.393), channel_id=1, source_target_pairs={{0,1},{1,0},{2,3},{3,2},{4,5},{5,4},{6,7},{7,6},{8,9},{9,8},{10,11... | collective-permute-start | bytes 15925256 | tf_op jit(solution)/shard_map/ppermute | solution.py:40
  463.2 33.6 %collective-permute-start.62 = (bf16[2,2,2,72,1152]{4,3,0,2,1:T(8,128)(2,1)S(1)}, bf16[2,2,2,72,1152]{4,3,0,2,1:T(8,128)(2,1)S(1)}, u32[]{:S(2)}, u32[]{:S(2)}) collective-permute-start(bf16[2,2,2,72,1152]{4,3,0,2,1:T(8,128)(2,1)S(1)} %get-tuple-element.164), channel_id=1, source_target_pairs={{8,0},{12,4},{16,8},{20,12},{24,16},{28,20},{9,1},{13,5},{17,9},{2... | collective-permute-start | bytes 3981320 | tf_op jit(solution)/shard_map/ppermute | solution.py:46
  464.8 33.2 %collective-permute-start.61 = (bf16[2,2,2,72,1152]{4,3,0,2,1:T(8,128)(2,1)S(1)}, bf16[2,2,2,72,1152]{4,3,0,2,1:T(8,128)(2,1)S(1)}, u32[]{:S(2)}, u32[]{:S(2)}) collective-permute-start(bf16[2,2,2,72,1152]{4,3,0,2,1:T(8,128)(2,1)S(1)} %get-tuple-element.163), channel_id=1, source_target_pairs={{0,8},{4,12},{8,16},{12,20},{16,24},{20,28},{1,9},{5,13},{9,17},{1... | collective-permute-start | bytes 3981320 | tf_op jit(solution)/shard_map/ppermute | solution.py:43
  471.9 79.5 %collective-permute-start.55 = (bf16[4,2,2,72,512]{4,3,0,1,2:T(8,128)(2,1)}, bf16[4,2,2,72,512]{4,3,0,1,2:T(8,128)(2,1)}, u32[]{:S(2)}, u32[]{:S(2)}) collective-permute-start(bf16[4,2,2,72,512]{4,3,0,1,2:T(8,128)(2,1)} %bitcast.399), channel_id=1, source_target_pairs={{0,1},{1,0},{2,3},{3,2},{4,5},{5,4},{6,7},{7,6},{8,9},{9,8},{10,11... | collective-permute-start | bytes 3538952 | tf_op jit(solution)/shard_map/ppermute | solution.py:40
  471.9 86.0 %collective-permute-start.58 = (bf16[1152,1152]{1,0:T(8,128)(2,1)}, bf16[1152,1152]{1,0:T(8,128)(2,1)}, u32[]{:S(2)}, u32[]{:S(2)}) collective-permute-start(bf16[1152,1152]{1,0:T(8,128)(2,1)} %convolution_convert_fusion.2), channel_id=1, source_target_pairs={{0,1},{1,0},{2,3},{3,2},{4,5},{5,4},{6,7},{7,6},{8,9},{9,8},{10,11... | collective-permute-start | bytes 7962632 | tf_op jit(solution)/shard_map/ppermute | solution.py:40
  500.1 46.1 %collective-permute-start.64 = (bf16[2,2,2,72,1152]{4,3,0,2,1:T(8,128)(2,1)}, bf16[2,2,2,72,1152]{4,3,0,2,1:T(8,128)(2,1)}, u32[]{:S(2)}, u32[]{:S(2)}) collective-permute-start(bf16[2,2,2,72,1152]{4,3,0,2,1:T(8,128)(2,1)} %get-tuple-element.166), channel_id=1, source_target_pairs={{8,0},{12,4},{16,8},{20,12},{24,16},{28,20},{9,1},{13,5},{17,9},{2... | collective-permute-start | bytes 3981320 | tf_op jit(solution)/shard_map/ppermute | solution.py:46
  501.4 45.3 %collective-permute-start.63 = (bf16[2,2,2,72,1152]{4,3,0,2,1:T(8,128)(2,1)}, bf16[2,2,2,72,1152]{4,3,0,2,1:T(8,128)(2,1)}, u32[]{:S(2)}, u32[]{:S(2)}) collective-permute-start(bf16[2,2,2,72,1152]{4,3,0,2,1:T(8,128)(2,1)} %get-tuple-element.165), channel_id=1, source_target_pairs={{0,8},{4,12},{8,16},{12,20},{16,24},{20,28},{1,9},{5,13},{9,17},{1... | collective-permute-start | bytes 3981320 | tf_op jit(solution)/shard_map/ppermute | solution.py:43
  513.2 49.6 %collective-permute-start.59 = (bf16[1152,1152]{1,0:T(8,128)(2,1)}, bf16[1152,1152]{1,0:T(8,128)(2,1)}, u32[]{:S(2)}, u32[]{:S(2)}) collective-permute-start(bf16[1152,1152]{1,0:T(8,128)(2,1)} %convolution_convert_fusion.1), channel_id=1, source_target_pairs={{0,1},{1,0},{2,3},{3,2},{4,5},{5,4},{6,7},{7,6},{8,9},{9,8},{10,11... | collective-permute-start | bytes 7962632 | tf_op jit(solution)/shard_map/ppermute | solution.py:40
  515.8 25.8 %all-to-all-start.8 = ((f32[32,1,144]{2,1,0:T(1,128)}), f32[32,1,144]{2,1,0:T(1,128)S(1)}, u32[]{:S(2)}, u32[]{:S(2)}) async-start(f32[32,1,144]{2,1,0:T(1,128)} %all_to_all.42), calls=%async_computation.8 | async-start | bytes 65536 | tf_op jit(solution)/shard_map/all_to_all | solution.py:661
  541.6 243.9 %all-to-all-start.3 = ((bf16[4,2,80,1152]{3,2,1,0:T(8,128)(2,1)}), bf16[4,2,80,1152]{3,2,1,0:T(8,128)(2,1)}, u32[]{:S(2)}, u32[]{:S(2)}) async-start(bf16[4,2,80,1152]{3,2,1,0:T(8,128)(2,1)} %bitcast.43), calls=%async_computation.3 | async-start | bytes 2949120 | tf_op jit(solution)/shard_map/all_to_all | solution.py:598
  546.2 59.2 %collective-permute-start.54 = (bf16[4,2,2,72,640]{4,3,0,2,1:T(8,128)(2,1)S(1)}, bf16[4,2,2,72,640]{4,3,0,2,1:T(8,128)(2,1)S(1)}, u32[]{:S(2)}, u32[]{:S(2)}) collective-permute-start(bf16[4,2,2,72,640]{4,3,0,2,1:T(8,128)(2,1)S(1)} %bitcast.441), channel_id=1, source_target_pairs={{0,1},{1,0},{2,3},{3,2},{4,5},{5,4},{6,7},{7,6},{8,9},{9,8},{10,11... | collective-permute-start | bytes 4423688 | tf_op jit(solution)/shard_map/ppermute | solution.py:40
  550.0 33.1 %collective-permute-start.66 = (bf16[2,2,2,72,1152]{4,3,0,2,1:T(8,128)(2,1)S(1)}, bf16[2,2,2,72,1152]{4,3,0,2,1:T(8,128)(2,1)S(1)}, u32[]{:S(2)}, u32[]{:S(2)}) collective-permute-start(bf16[2,2,2,72,1152]{4,3,0,2,1:T(8,128)(2,1)S(1)} %get-tuple-element.168), channel_id=1, source_target_pairs={{8,0},{12,4},{16,8},{20,12},{24,16},{28,20},{9,1},{13,5},{17,9},{2... | collective-permute-start | bytes 3981320 | tf_op jit(solution)/shard_map/ppermute | solution.py:46
  551.4 32.9 %collective-permute-start.65 = (bf16[2,2,2,72,1152]{4,3,0,2,1:T(8,128)(2,1)S(1)}, bf16[2,2,2,72,1152]{4,3,0,2,1:T(8,128)(2,1)S(1)}, u32[]{:S(2)}, u32[]{:S(2)}) collective-permute-start(bf16[2,2,2,72,1152]{4,3,0,2,1:T(8,128)(2,1)S(1)} %get-tuple-element.167), channel_id=1, source_target_pairs={{0,8},{4,12},{8,16},{12,20},{16,24},{20,28},{1,9},{5,13},{9,17},{1... | collective-permute-start | bytes 3981320 | tf_op jit(solution)/shard_map/ppermute | solution.py:43
  557.9 76.8 %collective-permute-start.56 = (bf16[1152,1152]{1,0:T(8,128)(2,1)S(1)}, bf16[1152,1152]{1,0:T(8,128)(2,1)S(1)}, u32[]{:S(2)}, u32[]{:S(2)}) collective-permute-start(bf16[1152,1152]{1,0:T(8,128)(2,1)S(1)} %copy-done.93), channel_id=1, source_target_pairs={{0,1},{1,0},{2,3},{3,2},{4,5},{5,4},{6,7},{7,6},{8,9},{9,8},{10,11... | collective-permute-start | bytes 7962632 | tf_op jit(solution)/shard_map/ppermute | solution.py:40
  562.8 43.5 %collective-permute-start.57 = (bf16[1152,1152]{1,0:T(8,128)(2,1)S(1)}, bf16[1152,1152]{1,0:T(8,128)(2,1)S(1)}, u32[]{:S(2)}, u32[]{:S(2)}) collective-permute-start(bf16[1152,1152]{1,0:T(8,128)(2,1)S(1)} %copy-done.92), channel_id=1, source_target_pairs={{0,1},{1,0},{2,3},{3,2},{4,5},{5,4},{6,7},{7,6},{8,9},{9,8},{10,11... | collective-permute-start | bytes 7962632 | tf_op jit(solution)/shard_map/ppermute | solution.py:40
  605.0 28.0 %collective-permute-start.71 = (bf16[4,2,72,1152]{3,2,0,1:T(8,128)(2,1)S(1)}, bf16[4,2,72,1152]{3,2,0,1:T(8,128)(2,1)S(1)}, u32[]{:S(2)}, u32[]{:S(2)}) collective-permute-start(bf16[4,2,72,1152]{3,2,0,1:T(8,128)(2,1)S(1)} %bitcast.445), channel_id=1, source_target_pairs={{0,4},{4,0},{8,12},{12,8},{16,20},{20,16},{24,28},{28,24},{1,5},{5... | collective-permute-start | bytes 3981320 | tf_op jit(solution)/shard_map/ppermute | solution.py:34
  605.9 28.1 %collective-permute-start.72 = (bf16[4,2,72,1152]{3,2,0,1:T(8,128)(2,1)S(1)}, bf16[4,2,72,1152]{3,2,0,1:T(8,128)(2,1)S(1)}, u32[]{:S(2)}, u32[]{:S(2)}) collective-permute-start(bf16[4,2,72,1152]{3,2,0,1:T(8,128)(2,1)S(1)} %bitcast.444), channel_id=1, source_target_pairs={{0,2},{1,3},{2,0},{3,1},{4,6},{5,7},{6,4},{7,5},{8,10},{9,11},{10,... | collective-permute-start | bytes 3981320 | tf_op jit(solution)/shard_map/ppermute | solution.py:37
  634.4 13.1 %collective-permute-start.73 = (bf16[4,72,1152]{2,1,0:T(8,128)(2,1)S(1)}, bf16[4,72,1152]{2,1,0:T(8,128)(2,1)S(1)}, u32[]{:S(2)}, u32[]{:S(2)}) collective-permute-start(bf16[4,72,1152]{2,1,0:T(8,128)(2,1)S(1)} %dynamic-slice_bitcast_fusion.6), channel_id=1, source_target_pairs={{0,2},{1,3},{2,0},{3,1},{4,6},{5,7},{6,4},{7,5},{8,10},{9,11},{10,... | collective-permute-start | bytes 1990664 | tf_op jit(solution)/shard_map/ppermute | solution.py:37
  668.1 22.6 %collective-permute-start.75 = (bf16[4,2,72,1152]{3,2,0,1:T(8,128)(2,1)S(1)}, bf16[4,2,72,1152]{3,2,0,1:T(8,128)(2,1)S(1)}, u32[]{:S(2)}, u32[]{:S(2)}) collective-permute-start(bf16[4,2,72,1152]{3,2,0,1:T(8,128)(2,1)S(1)} %bitcast.442), channel_id=1, source_target_pairs={{0,4},{4,0},{8,12},{12,8},{16,20},{20,16},{24,28},{28,24},{1,5},{5... | collective-permute-start | bytes 3981320 | tf_op jit(solution)/shard_map/ppermute | solution.py:34
  684.1 26.1 %collective-permute-start.76 = (bf16[4,2,72,1152]{3,2,0,1:T(8,128)(2,1)S(1)}, bf16[4,2,72,1152]{3,2,0,1:T(8,128)(2,1)S(1)}, u32[]{:S(2)}, u32[]{:S(2)}) collective-permute-start(bf16[4,2,72,1152]{3,2,0,1:T(8,128)(2,1)S(1)} %bitcast.443), channel_id=1, source_target_pairs={{0,2},{1,3},{2,0},{3,1},{4,6},{5,7},{6,4},{7,5},{8,10},{9,11},{10,... | collective-permute-start | bytes 3981320 | tf_op jit(solution)/shard_map/ppermute | solution.py:37
  689.7 24.0 %collective-permute-start.102 = (f32[2,36,1152]{2,1,0:T(8,128)S(1)}, f32[2,36,1152]{2,1,0:T(8,128)S(1)}, u32[]{:S(2)}, u32[]{:S(2)}) collective-permute-start(f32[2,36,1152]{2,1,0:T(8,128)S(1)} %constant_dynamic-slice_fusion), channel_id=1, source_target_pairs={{0,1},{1,0},{2,3},{3,2},{4,5},{5,4},{6,7},{7,6},{8,9},{9,8},{10,11... | collective-permute-start | bytes 995336 | tf_op jit(solution)/shard_map/ppermute | solution.py:40
  710.6 13.5 %collective-permute-start.77 = (bf16[4,72,1152]{2,1,0:T(8,128)(2,1)S(1)}, bf16[4,72,1152]{2,1,0:T(8,128)(2,1)S(1)}, u32[]{:S(2)}, u32[]{:S(2)}) collective-permute-start(bf16[4,72,1152]{2,1,0:T(8,128)(2,1)S(1)} %dynamic-slice_bitcast_fusion.4), channel_id=1, source_target_pairs={{0,2},{1,3},{2,0},{3,1},{4,6},{5,7},{6,4},{7,5},{8,10},{9,11},{10,... | collective-permute-start | bytes 1990664 | tf_op jit(solution)/shard_map/ppermute | solution.py:37
  712.4 13.1 %collective-permute-start.78 = (bf16[4,72,1152]{2,1,0:T(8,128)(2,1)S(1)}, bf16[4,72,1152]{2,1,0:T(8,128)(2,1)S(1)}, u32[]{:S(2)}, u32[]{:S(2)}) collective-permute-start(bf16[4,72,1152]{2,1,0:T(8,128)(2,1)S(1)} %dynamic-slice_bitcast_fusion.3), channel_id=1, source_target_pairs={{0,4},{4,0},{8,12},{12,8},{16,20},{20,16},{24,28},{28,24},{1,5},{5... | collective-permute-start | bytes 1990664 | tf_op jit(solution)/shard_map/ppermute | solution.py:34
  725.5 22.6 %collective-permute-start.80 = (bf16[4,2,72,512]{3,2,0,1:T(8,128)(2,1)S(1)}, bf16[4,2,72,512]{3,2,0,1:T(8,128)(2,1)S(1)}, u32[]{:S(2)}, u32[]{:S(2)}) collective-permute-start(bf16[4,2,72,512]{3,2,0,1:T(8,128)(2,1)S(1)} %dynamic-slice_bitcast_fusion.7), channel_id=1, source_target_pairs={{0,2},{1,3},{2,0},{3,1},{4,6},{5,7},{6,4},{7,5},{8,10},{9,11},{10,... | collective-permute-start | bytes 1769480 | tf_op jit(solution)/shard_map/ppermute | solution.py:37
  727.7 13.9 %collective-permute-start.89 = (bf16[2,72,1152]{2,1,0:T(8,128)(2,1)S(1)}, bf16[2,72,1152]{2,1,0:T(8,128)(2,1)S(1)}, u32[]{:S(2)}, u32[]{:S(2)}) collective-permute-start(bf16[2,72,1152]{2,1,0:T(8,128)(2,1)S(1)} %get-tuple-element.191), channel_id=1, source_target_pairs={{0,8},{4,12},{8,16},{12,20},{16,24},{20,28},{1,9},{5,13},{9,17},{1... | collective-permute-start | bytes 995336 | tf_op jit(solution)/shard_map/ppermute | solution.py:43
  736.0 24.3 %collective-permute-start.79 = (bf16[4,2,72,640]{3,2,0,1:T(8,128)(2,1)S(1)}, bf16[4,2,72,640]{3,2,0,1:T(8,128)(2,1)S(1)}, u32[]{:S(2)}, u32[]{:S(2)}) collective-permute-start(bf16[4,2,72,640]{3,2,0,1:T(8,128)(2,1)S(1)} %dynamic-slice_bitcast_fusion.2), channel_id=1, source_target_pairs={{0,4},{4,0},{8,12},{12,8},{16,20},{20,16},{24,28},{28,24},{1,5},{5... | collective-permute-start | bytes 2211848 | tf_op jit(solution)/shard_map/ppermute | solution.py:34
  774.9 14.1 %collective-permute-start.101 = (f32[2,36,1152]{2,1,0:T(8,128)S(1)}, f32[2,36,1152]{2,1,0:T(8,128)}, u32[]{:S(2)}, u32[]{:S(2)}) collective-permute-start(f32[2,36,1152]{2,1,0:T(8,128)S(1)} %constant_dynamic-slice_fusion.1), channel_id=1, source_target_pairs={{0,1},{1,0},{2,3},{3,2},{4,5},{5,4},{6,7},{7,6},{8,9},{9,8},{10,11... | collective-permute-start | bytes 995336 | tf_op jit(solution)/shard_map/ppermute | solution.py:40
  778.5 38.0 %collective-permute-start.98 = (bf16[72,1152]{1,0:T(8,128)(2,1)}, bf16[72,1152]{1,0:T(8,128)(2,1)}, u32[]{:S(2)}, u32[]{:S(2)}) collective-permute-start(bf16[72,1152]{1,0:T(8,128)(2,1)} %get-tuple-element.200), channel_id=1, source_target_pairs={{8,0},{12,4},{16,8},{20,12},{24,16},{28,20},{9,1},{13,5},{17,9},{2... | collective-permute-start | bytes 497672 | tf_op jit(solution)/shard_map/ppermute | solution.py:46
  779.8 36.8 %collective-permute-start.97 = (bf16[72,1152]{1,0:T(8,128)(2,1)}, bf16[72,1152]{1,0:T(8,128)(2,1)}, u32[]{:S(2)}, u32[]{:S(2)}) collective-permute-start(bf16[72,1152]{1,0:T(8,128)(2,1)} %get-tuple-element.199), channel_id=1, source_target_pairs={{0,8},{4,12},{8,16},{12,20},{16,24},{20,28},{1,9},{5,13},{9,17},{1... | collective-permute-start | bytes 497672 | tf_op jit(solution)/shard_map/ppermute | solution.py:43
  785.5 22.6 %all-to-all-start.5 = ((bf16[4,2,80,1152]{3,2,1,0:T(8,128)(2,1)}), bf16[4,2,80,1152]{3,2,1,0:T(8,128)(2,1)S(1)}, u32[]{:S(2)}, u32[]{:S(2)}) async-start(bf16[4,2,80,1152]{3,2,1,0:T(8,128)(2,1)} %bitcast.50), calls=%async_computation.5 | async-start | bytes 2949120 | tf_op jit(solution)/shard_map/all_to_all | solution.py:598
  809.1 26.6 %all-to-all-start.6 = ((bf16[4,2,320,288]{2,3,1,0:T(8,128)(2,1)}), bf16[4,2,320,288]{2,3,1,0:T(8,128)(2,1)S(1)}, u32[]{:S(2)}, u32[]{:S(2)}) async-start(bf16[4,2,320,288]{2,3,1,0:T(8,128)(2,1)} %copy.220), calls=%async_computation.6 | async-start | bytes 3538944 | tf_op jit(solution)/shard_map/all_to_all | solution.py:650
  836.3 14.6 %all-to-all-start.7 = ((f32[32,1,10]{2,1,0:T(1,128)}), f32[32,1,10]{2,1,0:T(1,128)S(1)}, u32[]{:S(2)}, u32[]{:S(2)}) async-start(f32[32,1,10]{2,1,0:T(1,128)} %broadcast_in_dim.17), calls=%async_computation.7 | async-start | bytes 32768 | tf_op jit(solution)/shard_map/all_to_all | solution.py:674
  (147 other events, 1682.5 us)

commit v3 on v2

v3 whole, which is shorter than its diff:
```python
import functools
import math

import jax
import jax.numpy as jnp
from jax import lax
from jax.experimental import pallas as pl
from jax.experimental.pallas import tpu as pltpu
from jax.sharding import PartitionSpec as P

LOW = jnp.bfloat16
CHIP_X = 2
CHIP_Y = 2
CORES = 2
SEMAPHORES = 128


class Place:
    def __init__(self, wide, narrow):
        self.wide, self.narrow = wide, narrow
        self.depth = wide // CHIP_X
        at_wide, at_narrow = lax.axis_index("wide"), lax.axis_index("narrow")
        self.z, self.x = at_wide // CHIP_X, at_wide % CHIP_X
        self.y, self.c = at_narrow // CORES, at_narrow % CORES
        self.n = at_narrow
        self.spot = jnp.stack([self.z, self.x, self.y, self.c, self.n]).astype(jnp.int32)

    def swap_x(self, value):
        return lax.ppermute(value, "wide", [(i, i ^ 1) for i in range(self.wide)])

    def swap_y(self, value):
        return lax.ppermute(value, "narrow", [(i, i ^ 2) for i in range(self.narrow)])

    def swap_c(self, value):
        return lax.ppermute(value, "narrow", [(i, i ^ 1) for i in range(self.narrow)])

    def swap_z(self, turn):
        pairs = [(i, i ^ (turn * CHIP_X)) for i in range(self.wide)]
        return lambda value: lax.ppermute(value, "wide", pairs)


def run_moves(name, place, inputs, out_shapes, plan, stage=False):
    count = len(inputs)
    out_count = len(out_shapes)

    def body(spot_ref, *refs):
        ins, outs, sems = refs[:count], refs[count : count + out_count], refs[count + out_count]
        held = refs[count + out_count + 1 :] if stage else outs
        spot = [spot_ref[k] for k in range(5)]
        moves = plan(spot, ins, held)
        assert len(moves) + out_count <= SEMAPHORES
        for start in (True, False):
            for at, (when, source, target) in enumerate(moves):
                copy = pltpu.make_async_copy(source, target, sems.at[at])
                act = copy.start if start else copy.wait
                if when is None:
                    act()
                else:
                    pl.when(when)(act)
        if stage:
            copies = [
                pltpu.make_async_copy(source, target, sems.at[len(moves) + at])
                for at, (source, target) in enumerate(zip(held, outs))
            ]
            for copy in copies:
                copy.start()
            for copy in copies:
                copy.wait()

    scratch = [pltpu.VMEM(shape.shape, shape.dtype) for shape in out_shapes] if stage else []
    return pl.pallas_call(
        body,
        out_shape=out_shapes,
        in_specs=[pl.BlockSpec(memory_space=pltpu.SMEM)] + [pl.BlockSpec(memory_space=pl.ANY)] * count,
        out_specs=[pl.BlockSpec(memory_space=pl.ANY if stage else pltpu.VMEM)] * out_count,
        scratch_shapes=[pltpu.SemaphoreType.DMA((SEMAPHORES,))] + scratch,
        compiler_params=pltpu.CompilerParams(vmem_limit_bytes=62 * 1024 * 1024),
        name=name,
    )(jnp.zeros(5, jnp.int32) if place is None else place.spot, *inputs)


class Pipe:
    def __init__(self, steps):
        self.steps, self.value = steps, None
        self.feed(None)

    def feed(self, results):
        try:
            self.wants = self.steps.send(results)
        except StopIteration as stop:
            self.wants, self.value = None, stop.value


def prepared(pipe):
    return (lambda *values: values), tuple(value for _, value in pipe.wants)


def prepare(pipe, values):
    pipe.wants = [(hop, value) for (hop, _), value in zip(pipe.wants, values)]


class Clock:
    def __init__(self):
        self.fence = ()

    def behind(self, values):
        return lax.optimization_barrier((values, self.fence))[0]

    def slot(self, pipes, *works, loose=()):
        pipes = [pipe for pipe in (*pipes, *loose) if pipe.wants]
        asked = [self.behind([value for _, value in pipe.wants]) for pipe in pipes]
        given = [lax.optimization_barrier((inputs, self.fence, asked))[0] for _, inputs in works]
        results = [work(*inputs) for (work, _), inputs in zip(works, given)]
        got = [[hop(value) for (hop, _), value in zip(pipe.wants, values)] for pipe, values in zip(pipes, asked)]
        self.fence = ([values for pipe, values in zip(pipes, got) if pipe not in loose], results)
        first = ()
        for pipe, values in zip(pipes, got):
            pipe.feed(lax.optimization_barrier((values, first))[0])
            first = [value for _, value in pipe.wants] if pipe.wants else first
        return results[0] if len(results) == 1 else results


def line_gather(place, piece):
    got = yield [(place.swap_z(turn), piece) for turn in range(1, place.depth)]
    return jnp.stack([piece, *got])


def spread_to(place, values, outs, at):
    count, shape = len(values), values[0].shape[1:]
    two = jax.ShapeDtypeStruct((2, count, *shape), values[0].dtype)

    def cut(spot, ins, outs):
        y = spot[2]
        moves = []
        for k, ref in enumerate(ins):
            for j in range(2):
                moves.append((None, ref.at[2 * y + j], outs[0].at[j, k]))
                moves.append((None, ref.at[2 - 2 * y + j], outs[1].at[j, k]))
        return moves

    own, send = run_moves("spread_cut", place, values, [two, two], cut)
    (far,) = yield [(place.swap_y, send)]

    def pick(spot, ins, outs):
        return [(None, ref.at[1 - spot[3]], outs[0].at[k]) for k, ref in enumerate(ins)]

    (send,) = run_moves("spread_pick", place, [own, far], [two], pick)
    (other,) = yield [(place.swap_c, send)]

    def put(spot, ins, outs):
        mine, n = spot[3], spot[4]
        moves = []
        for k in range(count):
            sources = (ins[0].at[mine, k], ins[2].at[0, k], ins[1].at[mine, k], ins[2].at[1, k])
            moves += [(None, ref, outs[k].at[at(n ^ turn)]) for turn, ref in enumerate(sources)]
        return moves

    out = [jax.ShapeDtypeStruct(shape, values[0].dtype) for shape in outs]
    return run_moves("spread_to", place, [own, far, other], out, put)


def plane_gather(place, first, second):
    first_got, second_got = yield [(place.swap_x, first), (place.swap_y, second)]
    first = jnp.stack([first, first_got])
    second = jnp.stack([second, second_got])
    first_far, second_far, first_core, second_core = yield [
        (place.swap_y, first),
        (place.swap_x, second),
        (place.swap_c, first),
        (place.swap_c, second),
    ]
    far_core = yield [(place.swap_c, first_far), (place.swap_c, second_far)]
    return first, first_far, second, second_far, first_core, far_core[0], second_core, far_core[1]


def total(*terms):
    return sum(term.astype(jnp.float32) for term in terms)


HEAD_DIM = 72
STEP = 10
EPS_NORM = 1e-05
BETA_ONE = 0.5
BETA_TWO = 0.5
EPS_ADAM = 1e-06
DECAY = 0.01
RATE = 0.5
RATE_TABLE = 0.1
NEGATIVE = -1e30
BOTH = ("wide", "narrow")
TABLE_COLS = 128


def project(left, right):
    return jnp.dot(left, right, preferred_element_type=jnp.float32)


def across(left, right):
    return lax.dot_general(
        left, right, (((0,), (0,)), ((), ())), preferred_element_type=jnp.float32
    )


def against(left, right):
    return lax.dot_general(
        left, right, (((1,), (1,)), ((), ())), preferred_element_type=jnp.float32
    )


def adam_step(grad, moment, square):
    new_mom = BETA_ONE * moment + (1.0 - BETA_ONE) * grad
    new_sq = BETA_TWO * square + (1.0 - BETA_TWO) * grad * grad
    step_dir = (
        new_mom / (1.0 - BETA_ONE**STEP) / (jnp.sqrt(new_sq / (1.0 - BETA_TWO**STEP)) + EPS_ADAM)
    )
    return (new_mom, new_sq, step_dir)


ATTN_VMEM = 60 * 1024 * 1024


def head_window(head):
    start = head * HEAD_DIM
    base = start // 128 * 128
    width = 128 if start - base + HEAD_DIM <= 128 else 256
    return base, width, start - base


def lane_mask(rows, width, offset):
    lane = lax.broadcasted_iota(jnp.int32, (rows, width), 1)
    return (lane >= offset) & (lane < offset + HEAD_DIM)


def score_rows(queries, keys, length, slots):
    logits = against(keys, queries) * (1.0 / math.sqrt(HEAD_DIM))
    key_at = lax.broadcasted_iota(jnp.int32, (slots, slots), 0)
    return jnp.where(key_at < length, logits, NEGATIVE)


def put_rows(ref, window, mask, value):
    ref[:, window] = jnp.where(mask, value, ref[:, window])


def attend_kernel(model, lengths_ref, qkv_ref, out_ref, lse_ref):
    slots = qkv_ref.shape[0]
    length = lengths_ref[pl.program_id(0)]
    for head in range(model // HEAD_DIM):
        base, width, offset = head_window(head)
        mask = lane_mask(slots, width, offset)
        window = pl.ds(base, width)
        queries = jnp.where(mask, qkv_ref[:, window], jnp.zeros((), LOW))
        logits = score_rows(queries, qkv_ref[:, pl.ds(model + base, width)], length, slots)
        top = jnp.max(logits, 0, keepdims=True)
        expo = jnp.exp(logits - top)
        scale = jnp.sum(expo, 0, keepdims=True)
        probs = (expo * (1.0 / scale)).astype(LOW)
        lse_ref[0, pl.ds(head, 1), :] = top + jnp.log(scale)
        heads_out = across(probs, qkv_ref[:, pl.ds(2 * model + base, width)]).astype(LOW)
        put_rows(out_ref, window, mask, heads_out)


def attend_back_kernel(model, lengths_ref, qkv_ref, d_heads_ref, lse_ref, out_ref):
    slots = qkv_ref.shape[0]
    length = lengths_ref[pl.program_id(0)]
    scale = 1.0 / math.sqrt(HEAD_DIM)
    for head in range(model // HEAD_DIM):
        base, width, offset = head_window(head)
        mask = lane_mask(slots, width, offset)
        window = pl.ds(base, width)
        key_window = pl.ds(model + base, width)
        value_window = pl.ds(2 * model + base, width)
        zero = jnp.zeros((), LOW)
        queries = jnp.where(mask, qkv_ref[:, window], zero)
        d_heads = jnp.where(mask, d_heads_ref[:, window], zero)
        keys = qkv_ref[:, key_window]
        logits = score_rows(queries, keys, length, slots)
        probs = jnp.exp(logits - lse_ref[0, pl.ds(head, 1), :])
        d_probs = against(qkv_ref[:, value_window], d_heads)
        weighted = probs * d_probs
        d_logits = (weighted - probs * jnp.sum(weighted, 0, keepdims=True)).astype(LOW)
        d_queries = (across(d_logits, keys) * scale).astype(LOW)
        d_keys = (project(d_logits, queries) * scale).astype(LOW)
        d_values = project(probs.astype(LOW), d_heads).astype(LOW)
        put_rows(out_ref, window, mask, d_queries)
        put_rows(out_ref, key_window, mask, d_keys)
        put_rows(out_ref, value_window, mask, d_values)


def item_block(slots, cols):
    return pl.BlockSpec((slots, cols), lambda i: (i, 0))


def lse_block(heads, slots):
    return pl.BlockSpec((1, heads, slots), lambda i: (i, 0, 0))


def attend(lengths, qkv, model):
    items = lengths.shape[0]
    slots = qkv.shape[0] // items
    heads = model // HEAD_DIM
    return pl.pallas_call(
        functools.partial(attend_kernel, model),
        grid=(items,),
        out_shape=[
            jax.ShapeDtypeStruct((items * slots, model), LOW),
            jax.ShapeDtypeStruct((items, heads, slots), jnp.float32),
        ],
        in_specs=[pl.BlockSpec(memory_space=pltpu.SMEM), item_block(slots, 3 * model)],
        out_specs=[item_block(slots, model), lse_block(heads, slots)],
        compiler_params=pltpu.CompilerParams(vmem_limit_bytes=ATTN_VMEM),
        name="attend",
    )(lengths, qkv)


def attend_back(lengths, qkv, d_heads, lse, model):
    items = lengths.shape[0]
    slots = qkv.shape[0] // items
    heads = model // HEAD_DIM
    return pl.pallas_call(
        functools.partial(attend_back_kernel, model),
        grid=(items,),
        out_shape=jax.ShapeDtypeStruct((items * slots, 3 * model), LOW),
        in_specs=[
            pl.BlockSpec(memory_space=pltpu.SMEM),
            item_block(slots, 3 * model),
            item_block(slots, model),
            lse_block(heads, slots),
        ],
        out_specs=item_block(slots, 3 * model),
        compiler_params=pltpu.CompilerParams(vmem_limit_bytes=ATTN_VMEM),
        name="attend_back",
    )(lengths, qkv, d_heads, lse)


KERNEL_VMEM = 60 * 1024 * 1024


def whole(shape):
    return pl.BlockSpec(shape, lambda *_: (0,) * len(shape))


def call(body, name, grid, ins, outs, scratch=(), scalars=()):
    spec = pltpu.PrefetchScalarGridSpec(
        num_scalar_prefetch=len(scalars),
        grid=grid,
        in_specs=[block for _, block in ins],
        out_specs=[block for _, _, block in outs],
        scratch_shapes=list(scratch),
    )
    return pl.pallas_call(
        body,
        grid_spec=spec,
        out_shape=[jax.ShapeDtypeStruct(shape, dtype) for shape, dtype, _ in outs],
        compiler_params=pltpu.CompilerParams(vmem_limit_bytes=KERNEL_VMEM),
        name=name,
    )(*scalars, *[array for array, _ in ins])


def gelu_pair(value):
    scale = math.sqrt(2.0 / math.pi)
    square = value * value
    bend = jnp.tanh(scale * value * (1.0 + 0.044715 * square))
    half = 0.5 * (1.0 + bend)
    slope = half + 0.5 * value * (1.0 - bend * bend) * (scale * (1.0 + 3.0 * 0.044715 * square))
    return value * half, slope


def widen_kernel(act_ref, weight_ref, hidden_ref, slope_ref):
    value, slope = gelu_pair(project(act_ref[...], weight_ref[...]))
    hidden_ref[...] = value.astype(LOW)
    slope_ref[...] = slope.astype(LOW)


def widen_rows(act, weight, block=768):
    rows, model = act.shape
    cols = weight.shape[1]
    tile = pl.BlockSpec((rows, block), lambda j: (0, j))
    return call(
        widen_kernel,
        "widen",
        (cols // block,),
        [(act, whole((rows, model))), (weight, pl.BlockSpec((model, block), lambda j: (0, j)))],
        [((rows, cols), LOW, tile), ((rows, cols), LOW, tile)],
    )


def flat(ref):
    return ref[...].reshape(-1, ref.shape[-1])


def fc2_block(weight, block):
    each = weight.shape[1]
    return pl.BlockSpec((block // each, each, weight.shape[2]), lambda k: (k, 0, 0))


def narrow_back_kernel(grad_ref, weight_ref, slope_ref, out_ref):
    out_ref[...] = (against(grad_ref[...], flat(weight_ref)) * slope_ref[...]).astype(LOW)


def narrow_back_rows(grad, weight, slope, block=1152):
    rows, model = grad.shape
    cols = slope.shape[1]
    tile = pl.BlockSpec((rows, block), lambda j: (0, j))
    (out,) = call(
        narrow_back_kernel,
        "narrow_back",
        (cols // block,),
        [(grad, whole((rows, model))), (weight, fc2_block(weight, block)), (slope, tile)],
        [((rows, cols), LOW, tile)],
    )
    return out


def narrow_kernel(hidden_ref, weight_ref, second_ref, out_ref, total_ref):
    step = pl.program_id(0)

    @pl.when(step == 0)
    def _():
        total_ref[...] = second_ref[...]

    total_ref[...] += project(hidden_ref[...], flat(weight_ref))

    @pl.when(step == pl.num_programs(0) - 1)
    def _():
        out_ref[...] = total_ref[...].astype(LOW)


def narrow_rows(hidden, weight, second, block=1152):
    rows, depth = hidden.shape
    model = second.shape[1]
    (out,) = call(
        narrow_kernel,
        "narrow",
        (depth // block,),
        [
            (hidden, pl.BlockSpec((rows, block), lambda k: (0, k))),
            (weight, fc2_block(weight, block)),
            (second, whole((rows, model))),
        ],
        [((rows, model), LOW, whole((rows, model)))],
        [pltpu.VMEM((rows, model), jnp.float32)],
    )
    return out


def row_grads_kernel(spot_ref, left_ref, right_ref, send_ref, keep_ref, full_ref):
    core = spot_ref[3]
    units, chips, each, _ = send_ref.shape
    full_ref[...] = across(left_ref[...], right_ref[...])
    for chip in range(chips):
        for ref, at in ((send_ref, 1 - core), (keep_ref, core)):
            for unit in range(units):
                start = pl.multiple_of(units * each * (2 * chip + at) + each * unit, 8)
                ref[unit, chip] = full_ref[pl.ds(start, each), :].astype(LOW)


def row_grads(place, left, right, each, block=1152):
    rows, width = left.shape
    cols = right.shape[1]
    chips = block // (4 * each)
    tile = pl.BlockSpec((2, chips, each, cols), lambda k, spot: (0, k, 0, 0))
    shape = (2, width // (4 * each), each, cols)
    return call(
        row_grads_kernel,
        "row_grads",
        (width // block,),
        [(left, pl.BlockSpec((rows, block), lambda k, spot: (0, k))), (right, whole((rows, cols)))],
        [(shape, LOW, tile)] * 2,
        [pltpu.VMEM((block, cols), jnp.float32)],
        [place.spot],
    )


def column_grads_kernel(spot_ref, left_ref, right_ref, send_ref, keep_ref):
    step = pl.program_id(0)
    product = across(left_ref[...], right_ref[...]).astype(LOW)

    @pl.when(step < 2)
    def _():
        send_ref[0] = product

    @pl.when(step >= 2)
    def _():
        keep_ref[0] = product


def column_grads(place, left, right):
    rows, model = left.shape

    def unit(u, spot):
        return (u // 2 + 1 - spot[3]) % 2 * 2 + u % 2

    return call(
        column_grads_kernel,
        "column_grads",
        (4,),
        [
            (left, pl.BlockSpec((rows, model), lambda u, spot: (0, 0))),
            (right, pl.BlockSpec((rows, model), lambda u, spot: (0, unit(u, spot)))),
        ],
        [
            ((2, model, model), LOW, pl.BlockSpec((1, model, model), lambda u, spot: (jnp.minimum(u, 1), 0, 0))),
            ((2, model, model), LOW, pl.BlockSpec((1, model, model), lambda u, spot: (jnp.maximum(u - 2, 0), 0, 0))),
        ],
        scalars=[place.spot],
    )


def mixed_grads_kernel(spot_ref, act_ref, heads_ref, right_ref, second_ref, send_ref, keep_ref):
    step = pl.program_id(0)
    last = (step % 2 == 1) & ((step // 2 + 1 - spot_ref[3]) % 2 == 1)

    def put(product):
        product = product.astype(LOW)

        @pl.when(step < 2)
        def _():
            send_ref[0] = product

        @pl.when(step >= 2)
        def _():
            keep_ref[0] = product

    @pl.when(last)
    def _():
        put(across(heads_ref[...], second_ref[...]))

    @pl.when(jnp.logical_not(last))
    def _():
        put(across(act_ref[...], right_ref[...]))


def mixed_grads(place, act, heads_out, d_projected, d_second):
    rows, model = act.shape
    full = pl.BlockSpec((rows, model), lambda u, spot: (0, 0))

    def unit(u, spot):
        return jnp.minimum((u // 2 + 1 - spot[3]) % 2 * 2 + u % 2, 2)

    return call(
        mixed_grads_kernel,
        "mixed_grads",
        (4,),
        [
            (act, full),
            (heads_out, full),
            (d_projected, pl.BlockSpec((rows, model), lambda u, spot: (0, unit(u, spot)))),
            (d_second, full),
        ],
        [
            ((2, model, model), LOW, pl.BlockSpec((1, model, model), lambda u, spot: (jnp.minimum(u, 1), 0, 0))),
            ((2, model, model), LOW, pl.BlockSpec((1, model, model), lambda u, spot: (jnp.maximum(u - 2, 0), 0, 0))),
        ],
        scalars=[place.spot],
    )


def norm_back_sums(d_act, normed, inv, gain):
    scaled = d_act * gain
    back = inv * (
        scaled
        - jnp.mean(scaled, -1, keepdims=True)
        - normed * jnp.mean(scaled * normed, -1, keepdims=True)
    )
    sums = jnp.concatenate(
        [jnp.sum(d_act * normed, 0, keepdims=True), jnp.sum(d_act, 0, keepdims=True)], 0
    )
    return back, sums


def norm_rows(value):
    center = value - jnp.mean(value, -1, keepdims=True)
    inv = lax.rsqrt(jnp.mean(center * center, -1, keepdims=True) + EPS_NORM)
    return center * inv, inv


def widen_back_kernel(d_pre_ref, w_fc1_ref, w_proj_ref, grad_ref, second_ref, table_ref, d_second_ref, low_ref, heads_ref, sums_ref, total_ref):
    step = pl.program_id(0)

    @pl.when(step == 0)
    def _():
        total_ref[...] = jnp.zeros_like(total_ref)

    total_ref[...] += against(d_pre_ref[...], w_fc1_ref[...])

    @pl.when(step == pl.num_programs(0) - 1)
    def _():
        normed, inv = norm_rows(second_ref[...])
        back, sums = norm_back_sums(total_ref[...], normed, inv, table_ref[2:3, :])
        d_second = grad_ref[...].astype(jnp.float32) + back
        low = d_second.astype(LOW)
        sums_ref[...] = sums
        d_second_ref[...] = d_second
        low_ref[...] = low
        heads_ref[...] = against(low, w_proj_ref[...]).astype(LOW)


def widen_back_rows(d_pre, w_fc1, w_proj, grad, second, table, block=1536):
    rows, depth = d_pre.shape
    model = grad.shape[1]
    full = whole((rows, model))
    return call(
        widen_back_kernel,
        "widen_back",
        (depth // block,),
        [
            (d_pre, pl.BlockSpec((rows, block), lambda k: (0, k))),
            (w_fc1, pl.BlockSpec((model, block), lambda k: (0, k))),
            (w_proj, whole((model, model))),
            (grad, full),
            (second, full),
            (table, whole((4, model))),
        ],
        [
            ((rows, model), jnp.float32, full),
            ((rows, model), LOW, full),
            ((rows, model), LOW, full),
            ((2, model), jnp.float32, whole((2, model))),
        ],
        [pltpu.VMEM((rows, model), jnp.float32)],
    )


def enter_back_kernel(d_projected_ref, weight_ref, d_second_ref, first_ref, table_ref, low_ref, sums_ref, total_ref):
    step = pl.program_id(0)

    @pl.when(step == 0)
    def _():
        total_ref[...] = jnp.zeros_like(total_ref)

    total_ref[...] += against(d_projected_ref[...], weight_ref[...])

    @pl.when(step == pl.num_programs(0) - 1)
    def _():
        normed, inv = norm_rows(first_ref[...])
        back, sums = norm_back_sums(total_ref[...], normed, inv, table_ref[0:1, :])
        sums_ref[...] = sums
        low_ref[...] = (d_second_ref[...] + back).astype(LOW)


def enter_back_rows(d_projected, weight, d_second, first, table, block=1152):
    rows, depth = d_projected.shape
    model = first.shape[1]
    full = whole((rows, model))
    return call(
        enter_back_kernel,
        "enter_back",
        (depth // block,),
        [
            (d_projected, pl.BlockSpec((rows, block), lambda k: (0, k))),
            (weight, pl.BlockSpec((model, block), lambda k: (0, k))),
            (d_second, full),
            (first, full),
            (table, whole((4, model))),
        ],
        [((rows, model), LOW, full), ((2, model), jnp.float32, whole((2, model)))],
        [pltpu.VMEM((rows, model), jnp.float32)],
    )


def enter_kernel(token_ref, store_ref, weight_ref, table_ref, first_ref, act_ref):
    model = token_ref.shape[1]
    blocks, items, each, _ = store_ref.shape
    parts = [
        sum(
            across(store_ref[at, item], weight_ref[model + each * at : model + each * (at + 1), :])
            for at in range(blocks)
        )
        for item in range(items)
    ]
    first = project(token_ref[...], weight_ref[:model, :]) + jnp.concatenate(parts, 0)
    first_ref[...] = first
    normed, _ = norm_rows(first)
    act_ref[...] = (normed * table_ref[0:1, :] + table_ref[1:2, :]).astype(LOW)


def enter_rows(token_rows, store, weight, table):
    rows, model = token_rows.shape
    full = whole((rows, model))
    return call(
        enter_kernel,
        "enter",
        (1,),
        [(token_rows, full), (store, whole(store.shape)), (weight, whole((2 * model, model))), (table, whole((4, model)))],
        [((rows, model), jnp.float32, full), ((rows, model), LOW, full)],
    )


def skip_grads_kernel(token_ref, store_ref, right_ref, table_ref, out_ref):
    step = pl.program_id(0)
    cols = right_ref.shape[1]
    out_ref[:, cols:] = table_ref[...].astype(LOW)

    @pl.when(step == 0)
    def _():
        out_ref[:, :cols] = across(token_ref[...], right_ref[...]).astype(LOW)

    @pl.when(step == 1)
    def _():
        blocks, items, block, slots = store_ref.shape
        for at in range(blocks):
            parts = [
                project(store_ref[at, item], right_ref[slots * item : slots * (item + 1), :])
                for item in range(items)
            ]
            out_ref[block * at : block * (at + 1), :cols] = sum(parts).astype(LOW)


def skip_grads_rows(token_rows, store, right, table):
    rows, model = token_rows.shape
    cols = right.shape[1]
    extra = table.shape[1]
    (out,) = call(
        skip_grads_kernel,
        "skip_grads",
        (2,),
        [
            (token_rows, whole((rows, model))),
            (store, whole(store.shape)),
            (right, whole((rows, cols))),
            (table, pl.BlockSpec((model, extra), lambda k: (k, 0))),
        ],
        [((2 * model, cols + extra), LOW, pl.BlockSpec((model, cols + extra), lambda k: (k, 0)))],
    )
    return out


def leave_back_kernel(left_ref, weight_ref, token_ref, store_ref):
    model = left_ref.shape[1]
    blocks, items, each, slots = store_ref.shape
    token_ref[...] = against(left_ref[...], weight_ref[:model, :]).astype(LOW)
    for at in range(blocks):
        rows = weight_ref[model + each * at : model + each * (at + 1), :]
        for item in range(items):
            left = left_ref[slots * item : slots * (item + 1), :]
            store_ref[at, item] = against(rows, left).astype(LOW)


def leave_back_rows(left, weight, blocks, items):
    rows, model = left.shape
    shape = (blocks, items, model // blocks, rows // items)
    return call(
        leave_back_kernel,
        "leave_back",
        (1,),
        [(left, whole((rows, model))), (weight, whole((2 * model, model)))],
        [((rows, model), LOW, whole((rows, model))), (shape, LOW, whole(shape))],
    )


def product_kernel(left_ref, right_ref, out_ref):
    out_ref[...] = project(left_ref[...], right_ref[...]).astype(LOW)


def product_rows(left, right, block=1152):
    rows, depth = left.shape
    cols = right.shape[1]
    (out,) = call(
        product_kernel,
        "product",
        (cols // block,),
        [(left, whole((rows, depth))), (right, pl.BlockSpec((depth, block), lambda j: (0, j)))],
        [((rows, cols), LOW, pl.BlockSpec((rows, block), lambda j: (0, j)))],
    )
    return out


def merge_kernel(heads_ref, weight_ref, first_ref, table_ref, second_ref, act_ref):
    second = first_ref[...] + project(heads_ref[...], weight_ref[...])
    second_ref[...] = second
    normed, _ = norm_rows(second)
    act_ref[...] = (normed * table_ref[2:3, :] + table_ref[3:4, :]).astype(LOW)


def merge_rows(heads_out, weight, first, table):
    rows, model = heads_out.shape
    full = whole((rows, model))
    return call(
        merge_kernel,
        "merge",
        (1,),
        [(heads_out, full), (weight, whole((model, model))), (first, full), (table, whole((4, model)))],
        [((rows, model), jnp.float32, full), ((rows, model), LOW, full)],
    )


def summed(*refs):
    value = refs[0][...].astype(jnp.float32)
    for ref in refs[1:]:
        value += ref[...].astype(jnp.float32).reshape(value.shape)
    return value


def hop_one_kernel(spot_ref, keep_one, got_one, keep_two, got_two, one_ref, two_ref):
    one_ref[...] = summed(keep_one, got_one).reshape(one_ref.shape).astype(LOW)
    two_ref[...] = summed(keep_two, got_two).reshape(two_ref.shape).astype(LOW)


def hop_one(place, keep, got):
    depth, rows, cols = place.depth, *keep.shape[4:]
    block = (1, depth, 1, 1, rows, cols)
    one = pl.BlockSpec(block, lambda j, spot: (0, 0, 1 - spot[1], j, 0, 0))
    two = pl.BlockSpec(block, lambda j, spot: (1, 0, j, 1 - spot[2], 0, 0))
    out = ((depth, 2, rows, cols), LOW, pl.BlockSpec((depth, 1, rows, cols), lambda j, spot: (0, j, 0, 0)))
    ins = [(keep, one), (got, one), (keep, two), (got, two)]
    return call(hop_one_kernel, "hop_one", (2,), ins, [out, out], scalars=[place.spot])


def hop_two_kernel(spot_ref, keep_one, got_one, near_one, keep_two, got_two, near_two, one_ref, two_ref):
    one_ref[...] = summed(keep_one, got_one, near_one).reshape(one_ref.shape).astype(LOW)
    two_ref[...] = summed(keep_two, got_two, near_two).reshape(two_ref.shape).astype(LOW)


def hop_two(place, keep, got, near_one, near_two):
    depth, rows, cols = place.depth, *keep.shape[4:]
    block = (1, depth // 2, 1, 1, rows, cols)
    one = pl.BlockSpec(block, lambda j, spot: (0, j, spot[1], 1 - spot[2], 0, 0))
    two = pl.BlockSpec(block, lambda j, spot: (1, j, 1 - spot[1], spot[2], 0, 0))
    block = (depth // 2, 1, rows, cols)
    ins = [
        (keep, one),
        (got, one),
        (near_one, pl.BlockSpec(block, lambda j, spot: (j, 1 - spot[2], 0, 0))),
        (keep, two),
        (got, two),
        (near_two, pl.BlockSpec(block, lambda j, spot: (j, 1 - spot[1], 0, 0))),
    ]
    out = ((depth, rows, cols), LOW, pl.BlockSpec((depth // 2, rows, cols), lambda j, spot: (j, 0, 0)))
    return call(hop_two_kernel, "hop_two", (2,), ins, [out, out], scalars=[place.spot])


def hop_three_kernel(spot_ref, *refs):
    ins, outs = refs[:8], refs[8:]
    for turn, ref in enumerate(outs):
        at = spot_ref[0] ^ turn
        for unit in range(2):
            keep, got, near, far = ins[4 * unit : 4 * unit + 4]
            parts = keep[0, at, 0, 0], got[0, at, 0, 0], near[at, 0], far[at]
            ref[unit] = total(*parts).astype(ref.dtype)


def hop_three(place, keep, got, near_one, near_two, far_one, far_two):
    depth, rows, cols = place.depth, *keep.shape[4:]
    block = (1, depth, 1, 1, rows, cols)
    near = (depth, 1, rows, cols)
    one = pl.BlockSpec(block, lambda t, spot: (0, 0, spot[1], spot[2], 0, 0))
    two = pl.BlockSpec(block, lambda t, spot: (1, 0, spot[1], spot[2], 0, 0))
    ins = [
        (keep, one),
        (got, one),
        (near_one, pl.BlockSpec(near, lambda t, spot: (0, spot[2], 0, 0))),
        (far_one, whole(far_one.shape)),
        (keep, two),
        (got, two),
        (near_two, pl.BlockSpec(near, lambda t, spot: (0, spot[1], 0, 0))),
        (far_two, whole(far_two.shape)),
    ]
    shape = (2, rows, cols)
    outs = [(shape, jnp.float32 if turn == 0 else LOW, whole(shape)) for turn in range(depth)]
    return call(hop_three_kernel, "hop_three", (1,), ins, outs, scalars=[place.spot])


def halves_by_core(place, both):
    half = both.shape[2] // 2
    mine = lax.dynamic_slice_in_dim(both, place.c * half, half, 2)
    (got,) = yield [(place.swap_c, lax.dynamic_slice_in_dim(both, (1 - place.c) * half, half, 2))]
    first = place.c == 0
    return jnp.concatenate([jnp.where(first, mine, got), jnp.where(first, got, mine)], 1)


def gather_columns(place, block):
    unit = block.shape[1] // 2
    line = yield from line_gather(place, block)
    return (yield from plane_gather(place, line[..., :unit], line[..., unit:]))


def plane_moves(spot, kept, out_one, out_two, when_one=None, when_two=None):
    z, x, y = spot[0], spot[1], spot[2]
    moves = []
    for turn in range(2):
        for line in range(kept[0].shape[1]):
            depth = z ^ line
            at = x ^ turn
            moves.append((when_one, kept[0].at[turn, line], out_one(depth, at, y)))
            moves.append((when_one, kept[1].at[turn, line], out_one(depth, at, 1 - y)))
            at = y ^ turn
            moves.append((when_two, kept[2].at[turn, line], out_two(depth, x, at)))
            moves.append((when_two, kept[3].at[turn, line], out_two(depth, 1 - x, at)))
    return moves


def gather_qkvp(place, block):
    rows, unit = block.shape[0], block.shape[1] // 2
    kept = yield from gather_columns(place, block)
    depth = place.depth
    lead = (depth, CHIP_X, CHIP_Y, rows)
    out = [jax.ShapeDtypeStruct(lead + (3 * unit,), LOW), jax.ShapeDtypeStruct(lead + (unit,), LOW)]

    def plan(spot, ins, outs):
        moves = []
        for core in range(2):
            at = spot[3] if core == 0 else 1 - spot[3]
            start = pl.multiple_of(at * (2 * unit), 128)
            x, y = spot[1], spot[2]

            def one(z, x, y, start=start):
                return outs[0].at[z, x, y, :, pl.ds(start, unit)]

            def key(z, x, y):
                return outs[0].at[z, x, y, :, pl.ds(unit, unit)]

            def last(z, x, y):
                return outs[1].at[z, x, y]

            kept = ins[4 * core : 4 * core + 4]
            for turn, move in enumerate(plane_moves(spot, kept, one, key)):
                if turn % 4 < 2:
                    moves.append(move)
                else:
                    moves.append((at == 0, move[1], move[2]))
            for turn, move in enumerate(plane_moves(spot, kept, one, last)):
                if turn % 4 >= 2:
                    moves.append((at == 1, move[1], move[2]))
        return moves

    qkv, proj = run_moves("assemble_qkvp", place, kept, out, plan, stage=True)
    full = depth * CHIP_X * CHIP_Y * rows
    return qkv.reshape(full, 3 * unit), proj.reshape(full, unit)


def split_fc1(full, start):
    chips, cores, rows, cols = full.shape
    half = cols - start
    out = [jax.ShapeDtypeStruct((chips, rows, cores * half), LOW)]

    def plan(spot, ins, outs):
        return [
            (None, ins[0].at[:, at, :, pl.ds(start, half)], outs[0].at[:, :, pl.ds(at * half, half)])
            for at in range(cores)
        ]

    (joined,) = run_moves("split_fc1", None, [full], out, plan, stage=True)
    return joined.reshape(chips * rows, cores * half)


def scatter_columns(place, got, keep, cuts):
    parts = yield from scatter_units(place, keep, got, cuts)
    return (yield from halves_to_rows(place, parts))


def halves_to_rows(place, parts):
    rows = parts.shape[1] // 2
    keep = lax.dynamic_slice_in_dim(parts, place.c * rows, rows, 1)
    (got,) = yield [(place.swap_c, lax.dynamic_slice_in_dim(parts, (1 - place.c) * rows, rows, 1))]
    left = place.c == 0
    low, high = jnp.where(left, keep, got), jnp.where(left, got, keep)
    return jnp.concatenate([low[0], low[1], high[0], high[1]], 1)


def scatter_units(place, keep, got, cuts=((1, 2, 3),)):
    lead = (2, place.depth, CHIP_X, CHIP_Y)
    terms = [value.reshape(*lead, -1, value.shape[-1]) if value.ndim == 3 else value.reshape(*lead, *value.shape[2:]) for value in (keep, got)]
    first, second = hop_one(place, *terms)
    near = yield [(place.swap_x, first), (place.swap_y, second)]
    first, second = hop_two(place, *terms, *near)
    far = yield [(place.swap_y, first), (place.swap_x, second)]
    own, *sends = hop_three(place, *terms, *near, *far)
    for turns in cuts:
        got = yield [(place.swap_z(turn), sends[turn - 1]) for turn in turns]
        own = total(own, *got)
    return own


def scatter_fc2(place, send, keep):
    (got,) = yield [(place.swap_c, send)]
    parts = yield from scatter_units(place, keep, got)
    return parts.reshape(-1, parts.shape[2])


def gather_plain(low):
    return lax.all_gather(low, BOTH, axis=0, tiled=True)


def scatter_plain(grad):
    return lax.psum_scatter(grad, BOTH, scatter_dimension=0, tiled=True)


def exchange(hop, value):
    (got,) = yield [(hop, value)]
    return got


def local(
    short,
    wide,
    narrow,
    tokens,
    skip_store,
    cotangent,
    lengths,
    w_skip,
    mom_skip,
    sq_skip,
    w_qkv,
    mom_qkv,
    sq_qkv,
    w_proj,
    mom_proj,
    sq_proj,
    w_fc1,
    mom_fc1,
    sq_fc1,
    w_fc2,
    mom_fc2,
    sq_fc2,
    norm_table,
    norm_mom,
    norm_sq,
):
    place = Place(wide, narrow)
    devices = wide * narrow
    masters = (w_skip, w_qkv, w_proj, w_fc1, w_fc2)
    momenta = (mom_skip, mom_qkv, mom_proj, mom_fc1, mom_fc2)
    seconds = (sq_skip, sq_qkv, sq_proj, sq_fc1, sq_fc2)
    model = tokens.shape[-1]

    items, part = tokens.shape[0] // narrow, tokens.shape[1]
    rows = narrow * items * part
    clock = Clock()

    def swap_all(value):
        return lax.all_to_all(value, BOTH, 0, 0, tiled=True)

    def rows_in(value):
        value = value.reshape(narrow, items, part, model)
        shape = (items, narrow, part, model)
        (value,) = yield from spread_to(place, [value], [shape], lambda at: (slice(None), at))
        return value.reshape(rows, model)

    def rows_out(*values):
        values = [value.reshape(items, narrow, part, model).transpose(1, 0, 2, 3) for value in values]
        values = yield from spread_to(place, values, [value.shape for value in values], lambda at: at)
        return [value.reshape(tokens.shape) for value in values]

    def store_in(value):
        (value,) = yield from spread_to(place, [value], [value.shape], lambda at: at)
        return value

    token_pipe = Pipe(rows_in(tokens))
    store_shape = (narrow, items, model // narrow, narrow * part)
    store_pipe = Pipe(store_in(skip_store.swapaxes(1, 2).reshape(store_shape)))
    cot_pipe = Pipe(rows_in(cotangent))
    lengths = lax.dynamic_slice_in_dim(lengths, lax.axis_index("narrow") * items, items)

    low_skip, low_qkv, low_proj, low_fc1, low_fc2 = (matrix.astype(LOW) for matrix in masters)
    pair = jnp.concatenate([low_qkv, low_proj], 1)
    each = norm_table.shape[0]
    beside = jnp.pad(norm_table.astype(LOW), ((0, low_skip.shape[0] - each), (0, TABLE_COLS - 4)))
    low_skip = jnp.concatenate([low_skip, beside], 1)
    start = model + TABLE_COLS
    if short:
        q_pipe = Pipe(exchange(gather_plain, pair))
        full_fc1 = gather_plain(low_fc1)
        full_skip = gather_plain(low_skip)
        clock.slot([q_pipe, token_pipe, store_pipe])
        clock.slot([token_pipe, store_pipe])
    else:
        halves = Pipe(halves_by_core(place, jnp.stack([pair, low_fc1])))
        clock.slot([halves])
        q_pipe = Pipe(gather_qkvp(place, halves.value[0]))
        full_skip = gather_plain(jnp.concatenate([low_skip, halves.value[1]], 1))
        full_fc1 = split_fc1(full_skip.reshape(-1, CORES, low_skip.shape[0], full_skip.shape[1]), start)
        low_fc2, _ = lax.optimization_barrier((low_fc2, halves.value))
        clock.slot([q_pipe, token_pipe, store_pipe])
        clock.slot([q_pipe, token_pipe, store_pipe])
        clock.slot([q_pipe])
    full_fc2 = lax.all_gather(low_fc2, BOTH, axis=0, tiled=False)
    table = full_skip[:, model:start].reshape(devices, -1, TABLE_COLS)[:, :each, :4]
    table = table.reshape(model, 4).astype(jnp.float32).T

    def mix(act, first, weight, table):
        qkv = product_rows(act, weight[0])
        heads_out, lse = attend(lengths, qkv, model)
        return qkv, lse, heads_out, *merge_rows(heads_out, weight[1], first, table)

    token_rows, store = token_pipe.value, store_pipe.value
    clock.slot([q_pipe])
    w_mix = (q_pipe.value[:, : 3 * model], q_pipe.value[:, 3 * model :]) if short else q_pipe.value
    (first, act_one), w_mix = clock.slot(
        [cot_pipe], (enter_rows, (token_rows, store, full_skip, table)), (lambda *weights: weights, w_mix)
    )
    qkv, lse, heads_out, second, act_two = clock.slot([cot_pipe], (mix, (act_one, first, w_mix, table)))
    hidden, slope = clock.slot([], (widen_rows, (act_two, full_fc1)))

    grad_out = cot_pipe.value

    def leave(second, hidden, weight):
        return narrow_rows(hidden, weight, second)

    def fc2_grads(hidden, grad_out):
        if short:
            return (across(hidden, grad_out),) * 2
        return row_grads(place, hidden, grad_out, masters[4].shape[0] // 2)

    def fc1_grads(act, d_pre):
        return (across(act, d_pre),) * 2 if short else column_grads(place, act, d_pre)

    def mix_back(qkv, d_heads, lse):
        return attend_back(lengths, qkv, d_heads, lse, model)

    def qkvp_grads(act, heads_out, d_projected, d_second_low):
        if short:
            return (jnp.concatenate([across(act, d_projected), across(heads_out, d_second_low)], 1),) * 2
        return mixed_grads(place, act, heads_out, d_projected, d_second_low)

    def skip_grads(token_rows, store, d_first_low, sums):
        sums = jnp.concatenate(sums, 0).T.reshape(devices, each, 4)
        sums = jnp.pad(sums, ((0, 0), (0, masters[0].shape[0] - each), (0, TABLE_COLS - 4)))
        return skip_grads_rows(token_rows, store, d_first_low, sums.reshape(-1, TABLE_COLS))

    def leave_back(d_first_low, weight):
        return leave_back_rows(d_first_low, weight, narrow, items)

    def scatter(steps, send, keep, *cut):
        return Pipe(exchange(scatter_plain, send) if short else steps(place, send, keep, *cut))

    def core(send):
        pipe = Pipe(exchange(place.swap_c, send))
        if short:
            pipe.wants, pipe.value = None, send
        return pipe

    send, keep = clock.slot([], (fc2_grads, (hidden, grad_out)))
    g_back = scatter(scatter_fc2, send, keep)
    d_pre = clock.slot([g_back], (narrow_back_rows, (grad_out, full_fc2, slope)))

    def spread_back(d_pre, act, w_fc1, w_proj, grad_out, second, table):
        return fc1_grads(act, d_pre), widen_back_rows(d_pre, w_fc1, w_proj, grad_out, second, table)

    both, (d_second, d_second_low, d_heads, sums_two) = clock.slot(
        [g_back], (spread_back, (d_pre, act_two, full_fc1, w_mix[1], grad_out, second, table))
    )
    f_core = core(both[0])
    d_projected = clock.slot([g_back, f_core], (mix_back, (qkv, d_heads, lse)))
    f_back = scatter(scatter_columns, f_core.value, both[1], ((1, 2, 3),))

    def turn_back(act, heads_out, d_projected, d_second_low, w_qkv, d_second, first, table):
        grads = qkvp_grads(act, heads_out, d_projected, d_second_low)
        return grads, enter_back_rows(d_projected, w_qkv, d_second, first, table)

    (send, keep), (d_first_low, sums_one) = clock.slot(
        [f_back, g_back],
        (turn_back, (act_one, heads_out, d_projected, d_second_low, w_mix[0], d_second, first, table)),
    )
    q_core = core(send)
    skip_grad, (d_tokens, d_store) = clock.slot(
        [q_core, f_back],
        (skip_grads, (token_rows, store, d_first_low, (sums_one, sums_two))),
        (leave_back, (d_first_low, full_skip)),
    )
    q_back = scatter(scatter_columns, q_core.value, keep, ((1, 2, 3),))
    grad_skip_lin = scatter_plain(skip_grad).astype(jnp.float32)
    out_store_pipe = Pipe(store_in(d_store))
    block_rows, sends = clock.slot(
        [q_back, f_back], (leave, (second, hidden, full_fc2)), prepared(out_store_pipe)
    )
    prepare(out_store_pipe, sends)
    out_pipe = Pipe(rows_out(block_rows, d_tokens))
    sends = clock.slot([q_back, out_store_pipe, f_back], prepared(out_pipe))
    prepare(out_pipe, sends)

    def renew(grad, moment, square, master):
        new_mom, new_sq, step_dir = adam_step(grad, moment, square)
        update = step_dir + DECAY * master
        sums = [jnp.sum(jnp.sum(value * value, 0).reshape(-1, 128), 0) for value in (master, update)]
        return new_mom, new_sq, update, *sums

    def state(index):
        return momenta[index], seconds[index], masters[index]

    renewed = {}
    renewed[3], renewed[4] = clock.slot(
        [q_back, out_pipe, out_store_pipe],
        (renew, (f_back.value, *state(3))),
        (renew, (g_back.value, *state(4))),
    )
    clock.slot([q_back, out_pipe])
    (block_out, grad_tokens), grad_skip = out_pipe.value, out_store_pipe.value
    both = q_back.value
    renewed[1] = renew(both[:, : 3 * model], *state(1))
    renewed[2] = renew(both[:, 3 * model :], *state(2))
    renewed[0] = renew(grad_skip_lin[:, :model], *state(0))
    table_grad = grad_skip_lin[:each, model : model + 4]
    grad_skip = grad_skip.reshape(-1, *store_shape[2:]).swapaxes(1, 2)

    renewed = [renewed[index] for index in range(5)]
    update_list = [value[2] for value in renewed]
    squares = jnp.stack([value[index] for index in (3, 4) for value in renewed])
    squares = jnp.broadcast_to(squares[None], (devices, *squares.shape))
    totals = jnp.sqrt(jnp.sum(swap_all(squares), (0, 2)))
    weight_norm, update_norm = totals[:5], totals[5:]
    trust = weight_norm / (update_norm + EPS_ADAM)
    new_weights = [masters[index] - RATE * trust[index] * update_list[index] for index in range(5)]
    table_mom, table_sq, table_step = adam_step(table_grad, norm_mom, norm_sq)
    new_table = norm_table - RATE_TABLE * table_step
    lamb_stats = jnp.stack([weight_norm, update_norm, trust], 0)
    outs = [block_out, grad_tokens, grad_skip]
    for index in range(5):
        outs += [new_weights[index], *renewed[index][:2], new_weights[index].astype(LOW)]
    return (*outs, new_table, table_mom, table_sq, lamb_stats)


def solution(mesh):
    wide, narrow = mesh.shape["wide"], mesh.shape["narrow"]
    short = not (wide == 8 and narrow == 4)
    rows = P("wide", "narrow", None)
    store = P("wide", None, "narrow")
    shard = P(BOTH, None)
    return jax.shard_map(
        functools.partial(local, short, wide, narrow),
        mesh=mesh,
        in_specs=(rows, store, rows, P("wide")) + (shard,) * 18,
        out_specs=(rows, rows, store) + (shard,) * 23 + (P(),),
        check_vma=False,
    )
```

time: 881 us -> 623 us (0.71)
  Pallas kernels: 73 us -> 345 us
  starting transfers between devices: 224 us -> 54.8 us
  matrix products: 166 us -> 0 us
  waiting for transfers between devices: 243 us -> 140 us
  local copies, waits for them, and re-layouts: 93.5 us -> 29.8 us
  other arithmetic: 63.7 us -> 29.9 us
  between operations: 6.81 us -> 18.3 us
    pallas_call x0 -> x22, Pallas kernels: none -> 225 us  [call(): pl.pallas_call(body, grid_spec=spec, out_shape=[jax.ShapeDtypeStruct(shap...]
    dot_general x21 -> x0, matrix products: 166 us -> none  [the longest x11 61.2 us: across(): lax.dot_general(left, right, (((0,), (0,)), ((), ())), preferred_element_...]
    ppermute x48 -> x12, starting transfers between devices: 138 us -> 22.7 us  [swap_z(): return lambda value: lax.ppermute(value, 'wide', pairs)]
    ppermute x48 -> x12, waiting for transfers between devices: 131 us -> 30.6 us  [swap_z(): return lambda value: lax.ppermute(value, 'wide', pairs)]
    pallas_call x8 -> x17, Pallas kernels: 39.4 us -> 85.1 us  [run_moves(): pl.pallas_call(body, out_shape=out_shapes, in_specs=[pl.BlockSpec(memory_...]
    ppermute x16 -> x13, waiting for transfers between devices: 54.6 us -> 92.9 us  [swap_y(): lax.ppermute(value, 'narrow', [(i, i ^ 2) for i in range(self.narrow)])]
    all_to_all x9 -> x1, starting transfers between devices: 42.2 us -> 7.04 us  [swap_all(): return lax.all_to_all(value, BOTH, 0, 0, tiled=True)]
    all_to_all x9 -> x1, waiting for transfers between devices: 22.7 us -> 0.01 us  [swap_all(): return lax.all_to_all(value, BOTH, 0, 0, tiled=True)]
  transfers between devices with their start and end apart: 112 -> 52, of which waited for: 50 -> 14; matrix products, arithmetic and copies ran while one was open for 32% -> 6% of each run, Pallas kernels for 8% -> 54%
where the time goes in v3:
time: 623 us; the launch traced here: 618 us
  Pallas kernels  345 us (55%)
  waiting for transfers between devices  140 us (22%)
  starting transfers between devices  54.8 us (9%)
  other arithmetic  29.9 us (5%)
  local copies, waits for them, and re-layouts  29.8 us (5%)
  between operations  18.3 us (3%)
    pallas_call x22, Pallas kernels, call(): pl.pallas_call(body, grid_spec=spec, out_shape=[jax.ShapeDtypeStruct(shap...  225 us
    ppermute x13, waiting for transfers between devices, swap_y(): lax.ppermute(value, 'narrow', [(i, i ^ 2) for i in range(self.narrow)])  92.9 us
    pallas_call x17, Pallas kernels, run_moves(): pl.pallas_call(body, out_shape=out_shapes, in_specs=[pl.BlockSpec(memory_...  85.1 us
    ppermute x12, waiting for transfers between devices, swap_z(): return lambda value: lax.ppermute(value, 'wide', pairs)  30.6 us
    ppermute x12, starting transfers between devices, swap_z(): return lambda value: lax.ppermute(value, 'wide', pairs)  22.7 us
    pallas_call x1, Pallas kernels, attend_back(): pl.pallas_call(functools.partial(attend_back_kernel, model), grid=(items,...  22.2 us
    unnamed x147, local copies, waits for them, and re-layouts  15.8 us
    ppermute x8, waiting for transfers between devices, swap_x(): return lax.ppermute(value, 'wide', [(i, i ^ 1) for i in range(self.wide)])  15.4 us
  transfers between devices with their start and end apart: 52, of which 14 were waited for; matrix products, arithmetic and copies ran while one was open for 6% of the time, Pallas kernels for 54%

profile of v3, /device:TPU:0, one launch (start us, length us, event | category | flops | bytes accessed | tf_op | source)
XLA Modules:
  0.0 618.4 jit_solution(10453303156567157624)
XLA Ops:
  13.5 3.0 collective-permute-start.2
  16.5 2.6 collective-permute-start.3
  19.8 4.2 spread_cut.5
  24.0 4.5 spread_cut.6
  30.6 4.4 collective-permute-done.2
  35.0 6.3 %collective-permute-done.3 = bf16[72,2304]{1,0:T(8,128)(2,1)} collective-permute-done((bf16[72,2304]{1,0:T(8,128)(2,1)S(1)}, bf16[72,2304]{1,0:T(8,128)(2,1)}, u32[]{:S(2)}, u32[]{:S(2)}) %collective-permute-start.3) | collective-permute-done | bytes 331808 | tf_op jit(solution)/shard_map/ppermute | solution.py:39
  41.3 5.9 collective-permute-done.4
  50.2 18.8 %collective-permute-done.5.refs_1_ = bf16[2,1,2,288,320]{4,3,2,1,0:T(8,128)(2,1)} collective-permute-done((bf16[2,1,2,288,320]{4,3,2,1,0:T(8,128)(2,1)}, bf16[2,1,2,288,320]{4,3,2,1,0:T(8,128)(2,1)}, u32[]{:S(2)}, u32[]{:S(2)}) %collective-permute-start.5) | collective-permute-done | bytes 737312 | tf_op jit(solution)/shard_map/ppermute | solution.py:32
  70.4 2.5 collective-permute-start.8
  72.9 3.8 spread_pick.5
  76.7 4.0 spread_pick.6
  81.2 12.7 %collective-permute-done.7 = bf16[4,72,1152]{2,1,0:T(8,128)(2,1)} collective-permute-done((bf16[4,72,1152]{2,1,0:T(8,128)(2,1)}, bf16[4,72,1152]{2,1,0:T(8,128)(2,1)}, u32[]{:S(2)}, u32[]{:S(2)}) %collective-permute-start.7) | collective-permute-done | bytes 663584 | tf_op jit(solution)/shard_map/ppermute | solution.py:29
  98.1 46.3 %collective-permute-done.10.refs_1_ = bf16[2,4,72,1152]{3,2,1,0:T(8,128)(2,1)S(1)} collective-permute-done((bf16[2,4,72,1152]{3,2,1,0:T(8,128)(2,1)S(1)}, bf16[2,4,72,1152]{3,2,1,0:T(8,128)(2,1)S(1)}, u32[]{:S(2)}, u32[]{:S(2)}) %collective-permute-start.10) | collective-permute-done | bytes 1327136 | tf_op jit(solution)/shard_map/ppermute | solution.py:32
  144.4 2.5 collective-permute-done.11.refs_3_
  149.0 4.3 spread_cut.7
  153.6 4.2 spread_to.5
  157.8 4.4 spread_to.6.store_ref
  162.3 10.3 %assemble_qkvp.1 = (bf16[4,2,2,72,3456]{4,3,2,1,0:T(8,128)(2,1)}, bf16[4,2,2,72,1152]{4,3,2,1,0:T(8,128)(2,1)}) custom-call(s32[5]{0:T(128)} %stack.107.spot_ref, bf16[2,4,72,1152]{3,2,1,0:T(8,128)(2,1)} %copy-done.7, bf16[2,4,72,1152]{3,2,1,0:T(8,128)(2,1)} %copy-done.26, bf16[2,4,72,1152]{3,2,1,0:T(8,128)(2,1)} %copy-done.8, ...), custom_call_target="tpu_custom_call" | custom-call | tf_op jit(solution)/shard_map/assemble_qkvp/pallas_call | solution.py:71
  173.5 3.8 spread_pick.7
  179.5 11.1 %enter.1 = (f32[640,1152]{1,0:T(8,128)}, bf16[640,1152]{1,0:T(8,128)(2,1)}) custom-call(bf16[640,1152]{1,0:T(8,128)(2,1)} %bitcast.152, bf16[4,2,288,320]{3,2,1,0:T(8,128)(2,1)} %spread_to.6.store_ref, bf16[2304,3584]{1,0:T(8,128)(2,1)} %all-gather.4.cloned.1.call-done.weight_ref, f32[4,1152]{1,0:T(4,128)} %bitcast.170), custom_call_target="tpu_custom_call" | custom-call | tf_op jit(solution)/shard_map/enter/pallas_call | solution.py:350
  191.5 10.4 %product.1.qkv_ref = bf16[640,3456]{1,0:T(8,128)(2,1)} custom-call(bf16[640,1152]{1,0:T(8,128)(2,1)} %get-tuple-element.342.left_ref.act_ref, bf16[1152,3456]{1,0:T(8,128)(2,1)} %bitcast.147), custom_call_target="tpu_custom_call" | custom-call | tf_op jit(solution)/shard_map/product/pallas_call | solution.py:350
  201.9 13.4 %attend.1 = (bf16[640,1152]{1,0:T(8,128)(2,1)}, f32[2,16,320]{2,1,0:T(8,128)}) custom-call(s32[2]{0:T(128)} %dynamic_slice.21.lengths_ref, bf16[640,3456]{1,0:T(8,128)(2,1)} %product.1.qkv_ref), custom_call_target="tpu_custom_call" | custom-call | tf_op jit(solution)/shard_map/attend/pallas_call | solution.py:301
  215.8 9.9 %split_fc1.1 = bf16[16,72,4608]{2,1,0:T(8,128)(2,1)} custom-call(s32[5]{0:T(128)} %broadcast_27_spot_ref.2.spot_ref, bf16[16,2,72,3584]{3,2,1,0:T(8,128)(2,1)} %bitcast.142), custom_call_target="tpu_custom_call" | custom-call | tf_op jit(solution)/shard_map/split_fc1/pallas_call | solution.py:71
  225.7 7.4 %merge.1 = (f32[640,1152]{1,0:T(8,128)}, bf16[640,1152]{1,0:T(8,128)(2,1)}) custom-call(bf16[640,1152]{1,0:T(8,128)(2,1)} %get-tuple-element.343.heads_ref, bf16[1152,1152]{1,0:T(8,128)(2,1)} %bitcast.154, f32[640,1152]{1,0:T(8,128)} %get-tuple-element.350.first_ref, f32[4,1152]{1,0:T(4,128)} %bitcast.171), custom_call_target="tpu_custom_call" | custom-call | tf_op jit(solution)/shard_map/merge/pallas_call | solution.py:350
  233.1 4.3 spread_to.7
  237.4 17.2 %widen.1 = (bf16[640,4608]{1,0:T(8,128)(2,1)}, bf16[640,4608]{1,0:T(8,128)(2,1)}) custom-call(bf16[640,1152]{1,0:T(8,128)(2,1)} %get-tuple-element.313.act_ref.left_ref, bf16[1152,4608]{1,0:T(8,128)(2,1)} %bitcast.143), custom_call_target="tpu_custom_call" | custom-call | tf_op jit(solution)/shard_map/widen/pallas_call | solution.py:350
  254.5 24.8 %row_grads.1 = (bf16[2,16,72,1152]{3,2,1,0:T(8,128)(2,1)}, bf16[2,16,72,1152]{3,2,1,0:T(8,128)(2,1)}) custom-call(s32[5]{0:T(128)} %stack.107.spot_ref, bf16[640,4608]{1,0:T(8,128)(2,1)} %get-tuple-element.382.left_ref.hidden_ref, bf16[640,1152]{1,0:T(8,128)(2,1)} %bitcast.149), custom_call_target="tpu_custom_call" | custom-call | tf_op jit(solution)/shard_map/row_grads/pallas_call | solution.py:350
  279.6 13.5 %narrow_back.1.d_pre_ref.right_ref = bf16[640,4608]{1,0:T(8,128)(2,1)} custom-call(bf16[640,1152]{1,0:T(8,128)(2,1)} %bitcast.150, bf16[32,144,1152]{2,1,0:T(8,128)(2,1)} %bitcast.145, bf16[640,4608]{1,0:T(8,128)(2,1)} %get-tuple-element.301.slope_ref), custom_call_target="tpu_custom_call" | custom-call | tf_op jit(solution)/shard_map/narrow_back/pallas_call | solution.py:350
  293.1 4.6 hop_one.3
  298.5 1.9 collective-permute-start.20
  300.4 15.8 %column_grads.1 = (bf16[2,1152,1152]{2,1,0:T(8,128)(2,1)}, bf16[2,1152,1152]{2,1,0:T(8,128)(2,1)}) custom-call(s32[5]{0:T(128)} %stack.107.spot_ref, bf16[640,1152]{1,0:T(8,128)(2,1)} %get-tuple-element.313.act_ref.left_ref, bf16[640,4608]{1,0:T(8,128)(2,1)} %narrow_back.1.d_pre_ref.right_ref), custom_call_target="tpu_custom_call" | custom-call | tf_op jit(solution)/shard_map/column_grads/pallas_call | solution.py:350
  316.2 19.9 %widen_back.1 = (f32[640,1152]{1,0:T(8,128)}, bf16[640,1152]{1,0:T(8,128)(2,1)}, bf16[640,1152]{1,0:T(8,128)(2,1)}, f32[2,1152]{1,0:T(2,128)}) custom-call(bf16[640,4608]{1,0:T(8,128)(2,1)} %narrow_back.1.d_pre_ref.right_ref, bf16[1152,4608]{1,0:T(8,128)(2,1)} %bitcast.144, bf16[1152,1152]{1,0:T(8,128)(2,1)} %bitcast.155, bf16[640,1152]{1,0:T(8,128)(2,1)} %bitcast.151, ...), custom_call_target="tpu_custom_call" | custom-call | tf_op jit(solution)/shard_map/widen_back/pallas_call | solution.py:350
  337.5 3.8 hop_two.3
  342.8 22.2 %attend_back.1.right_ref.d_projected_ref = bf16[640,3456]{1,0:T(8,128)(2,1)} custom-call(s32[2]{0:T(128)} %dynamic_slice.21.lengths_ref, bf16[640,3456]{1,0:T(8,128)(2,1)} %product.1.qkv_ref, bf16[640,1152]{1,0:T(8,128)(2,1)} %get-tuple-element.327.d_heads_ref, f32[2,16,320]{2,1,0:T(8,128)} %get-tuple-element.328.lse_ref), custom_call_target="tpu_custom_call" | custom-call | tf_op jit(solution)/shard_map/attend_back/pallas_call | solution.py:319
  366.6 4.6 hop_three.3
  371.3 4.7 hop_one.4
  376.8 1.9 collective-permute-start.25
  380.5 1.9 collective-permute-start.27
  383.1 17.2 %mixed_grads.1 = (bf16[2,1152,1152]{2,1,0:T(8,128)(2,1)}, bf16[2,1152,1152]{2,1,0:T(8,128)(2,1)}) custom-call(s32[5]{0:T(128)} %stack.107.spot_ref, bf16[640,1152]{1,0:T(8,128)(2,1)} %get-tuple-element.342.left_ref.act_ref, bf16[640,1152]{1,0:T(8,128)(2,1)} %get-tuple-element.343.heads_ref, bf16[640,3456]{1,0:T(8,128)(2,1)} %attend_back.1.right_ref.d_projected_ref, ...), custom_call_target="tpu_custom_call" | custom-call | tf_op jit(solution)/shard_map/mixed_grads/pallas_call | solution.py:350
  400.3 14.2 %enter_back.1 = (bf16[640,1152]{1,0:T(8,128)(2,1)}, f32[2,1152]{1,0:T(2,128)}) custom-call(bf16[640,3456]{1,0:T(8,128)(2,1)} %attend_back.1.right_ref.d_projected_ref, bf16[1152,3456]{1,0:T(8,128)(2,1)} %bitcast.148, f32[640,1152]{1,0:T(8,128)} %get-tuple-element.349.d_second_ref, f32[640,1152]{1,0:T(8,128)} %get-tuple-element.350.first_ref, f32[4,1152]{1,0:T(4,128)} %bitcast.173), custom_call_target="tpu_custom_call" | custom-call | tf_op jit(solution)/shard_map/enter_back/pallas_call | solution.py:350
  415.8 3.8 hop_two.4
  421.2 9.9 %skip_grads.1 = bf16[2304,1280]{1,0:T(8,128)(2,1)} custom-call(bf16[640,1152]{1,0:T(8,128)(2,1)} %bitcast.153, bf16[4,2,288,320]{3,2,1,0:T(8,128)(2,1)} %spread_to.6.store_ref, bf16[640,1152]{1,0:T(8,128)(2,1)} %get-tuple-element.366.right_ref.left_ref, f32[2304,128]{1,0:T(8,128)} %bitcast.159), custom_call_target="tpu_custom_call" | custom-call | tf_op jit(solution)/shard_map/skip_grads/pallas_call | solution.py:350
  433.7 9.5 %leave_back.1 = (bf16[640,1152]{1,0:T(8,128)(2,1)}, bf16[4,2,288,320]{3,2,1,0:T(8,128)(2,1)}) custom-call(bf16[640,1152]{1,0:T(8,128)(2,1)} %get-tuple-element.366.right_ref.left_ref, bf16[2304,3584]{1,0:T(8,128)(2,1)} %all-gather.4.cloned.1.call-done.weight_ref), custom_call_target="tpu_custom_call" | custom-call | tf_op jit(solution)/shard_map/leave_back/pallas_call | solution.py:350
  443.2 4.8 hop_one.5
  451.6 4.8 hop_three.4
  457.4 2.9 collective-permute-start.35
  460.8 4.5 spread_cut.9
  465.3 2.6 copy.117
  468.0 14.0 %narrow.1 = bf16[640,1152]{1,0:T(8,128)(2,1)} custom-call(bf16[640,4608]{1,0:T(8,128)(2,1)} %get-tuple-element.382.left_ref.hidden_ref, bf16[32,144,1152]{2,1,0:T(8,128)(2,1)} %bitcast.146, f32[640,1152]{1,0:T(8,128)} %get-tuple-element.384.second_ref), custom_call_target="tpu_custom_call" | custom-call | tf_op jit(solution)/shard_map/narrow/pallas_call | solution.py:350
  482.0 3.9 hop_two.5
  494.0 5.2 spread_cut.8
  499.2 9.7 %collective-permute-done.37.refs_3_ = bf16[4,72,1152]{2,1,0:T(8,128)(2,1)S(1)} collective-permute-done((bf16[4,72,1152]{2,1,0:T(8,128)(2,1)}, bf16[4,72,1152]{2,1,0:T(8,128)(2,1)S(1)}, u32[]{:S(2)}, u32[]{:S(2)}) %collective-permute-start.37) | collective-permute-done | bytes 663584 | tf_op jit(solution)/shard_map/ppermute | solution.py:32
  509.8 4.7 hop_three.5
  514.5 17.7 %collective-permute-done.39.refs_1_ = bf16[2,1,2,288,320]{4,3,2,1,0:T(8,128)(2,1)} collective-permute-done((bf16[2,1,2,288,320]{4,3,2,1,0:T(8,128)(2,1)}, bf16[2,1,2,288,320]{4,3,2,1,0:T(8,128)(2,1)}, u32[]{:S(2)}, u32[]{:S(2)}) %collective-permute-start.39) | collective-permute-done | bytes 737312 | tf_op jit(solution)/shard_map/ppermute | solution.py:32
  532.5 4.2 collective-permute-start.42
  536.7 2.7 collective-permute-start.43
  540.8 3.9 spread_pick.9
  551.6 13.9 %collective-permute-done.43 = bf16[2,72,1152]{2,1,0:T(8,128)(2,1)} collective-permute-done((bf16[2,72,1152]{2,1,0:T(8,128)(2,1)}, bf16[2,72,1152]{2,1,0:T(8,128)(2,1)}, u32[]{:S(2)}, u32[]{:S(2)}) %collective-permute-start.43) | collective-permute-done | bytes 331808 | tf_op jit(solution)/shard_map/ppermute | solution.py:39
  568.7 2.1 multiply_reduce_fusion.6
  575.3 7.0 %all-to-all-start = ((f32[32,10,128]{2,1,0:T(8,128)}), f32[32,10,128]{2,1,0:T(8,128)}, u32[]{:S(2)}, u32[]{:S(2)}) async-start(f32[32,10,128]{2,1,0:T(8,128)} %broadcast_in_dim.2), calls=%async_computation.1 | async-start | bytes 524288 | tf_op jit(solution)/shard_map/all_to_all | solution.py:1032
  585.5 4.3 spread_pick.8
  590.0 4.4 spread_to.9
  598.9 2.2 fusion.16
  606.5 5.2 spread_to.8
  (303 shorter events, 79.0 us)
Async XLA Ops:
  7.2 170.1 %all-gather.4.cloned.1.call-start = ((), (), s32[]{:S(2)}) async-start(), calls=%async_computation.2 | async-start | bytes 17031168 | tf_op jit(solution)/shard_map/all_gather | solution.py:981
  9.5 1.8 collective-permute-start
  12.5 267.1 %all-gather.6.cloned.1.call-start = ((), (), s32[]{:S(2)}) async-start(), calls=%async_computation.4 | async-start | bytes 10948608 | tf_op jit(solution)/shard_map/all_gather | solution.py:1077
  13.4 554.1 %reduce-scatter.2.cloned.1.call-start = ((), (), s32[]{:S(2)}) async-start(), calls=%async_computation.3 | async-start | bytes 6082560 | tf_op jit(solution)/shard_map/reduce_scatter | solution.py:985
  13.5 21.5 %collective-permute-start.2 = (bf16[72,2304]{1,0:T(8,128)(2,1)S(1)}, bf16[72,2304]{1,0:T(8,128)(2,1)}, u32[]{:S(2)}, u32[]{:S(2)}) collective-permute-start(bf16[72,2304]{1,0:T(8,128)(2,1)S(1)} %bitcast.167), channel_id=1, source_target_pairs={{0,8},{4,12},{8,0},{12,4},{16,24},{20,28},{24,16},{28,20},{1,9},{5... | collective-permute-start | bytes 995336 | tf_op jit(solution)/shard_map/ppermute | solution.py:39
  16.5 24.8 %collective-permute-start.3 = (bf16[72,2304]{1,0:T(8,128)(2,1)S(1)}, bf16[72,2304]{1,0:T(8,128)(2,1)}, u32[]{:S(2)}, u32[]{:S(2)}) collective-permute-start(bf16[72,2304]{1,0:T(8,128)(2,1)S(1)} %bitcast.168), channel_id=1, source_target_pairs={{0,16},{4,20},{8,24},{12,28},{16,0},{20,4},{24,8},{28,12},{1,17},{... | collective-permute-start | bytes 995336 | tf_op jit(solution)/shard_map/ppermute | solution.py:39
  19.1 28.1 %collective-permute-start.4 = (bf16[72,2304]{1,0:T(8,128)(2,1)S(1)}, bf16[72,2304]{1,0:T(8,128)(2,1)}, u32[]{:S(2)}, u32[]{:S(2)}) collective-permute-start(bf16[72,2304]{1,0:T(8,128)(2,1)S(1)} %bitcast.169), channel_id=1, source_target_pairs={{0,24},{4,28},{8,16},{12,20},{16,8},{20,12},{24,0},{28,4},{1,25},{... | collective-permute-start | bytes 995336 | tf_op jit(solution)/shard_map/ppermute | solution.py:39
  28.5 21.7 %collective-permute-start.1 = (bf16[2,1,2,80,1152]{4,3,2,1,0:T(8,128)(2,1)}, bf16[2,1,2,80,1152]{4,3,2,1,0:T(8,128)(2,1)S(1)}, u32[]{:S(2)}, u32[]{:S(2)}) collective-permute-start(bf16[2,1,2,80,1152]{4,3,2,1,0:T(8,128)(2,1)} %get-tuple-element.234), channel_id=1, source_target_pairs={{0,2},{1,3},{2,0},{3,1},{4,6},{5,7},{6,4},{7,5},{8,10},{9,11},{10,... | collective-permute-start | bytes 2211848 | tf_op jit(solution)/shard_map/ppermute | solution.py:32
  30.3 38.6 %collective-permute-start.5 = (bf16[2,1,2,288,320]{4,3,2,1,0:T(8,128)(2,1)}, bf16[2,1,2,288,320]{4,3,2,1,0:T(8,128)(2,1)}, u32[]{:S(2)}, u32[]{:S(2)}) collective-permute-start(bf16[2,1,2,288,320]{4,3,2,1,0:T(8,128)(2,1)} %get-tuple-element.243), channel_id=1, source_target_pairs={{0,2},{1,3},{2,0},{3,1},{4,6},{5,7},{6,4},{7,5},{8,10},{9,11},{10,... | collective-permute-start | bytes 2211848 | tf_op jit(solution)/shard_map/ppermute | solution.py:32
  50.1 22.7 %copy-start.14 = (bf16[2,1,2,80,1152]{4,3,2,1,0:T(8,128)(2,1)}, bf16[2,1,2,80,1152]{4,3,2,1,0:T(8,128)(2,1)S(1)}, u32[]{:S(2)}) copy-start(bf16[2,1,2,80,1152]{4,3,2,1,0:T(8,128)(2,1)S(1)} %collective-permute-done.1.refs_1_) | copy-start | bytes 2211844
  68.9 24.9 %collective-permute-start.7 = (bf16[4,72,1152]{2,1,0:T(8,128)(2,1)}, bf16[4,72,1152]{2,1,0:T(8,128)(2,1)}, u32[]{:S(2)}, u32[]{:S(2)}) collective-permute-start(bf16[4,72,1152]{2,1,0:T(8,128)(2,1)} %get-tuple-element.245), channel_id=1, source_target_pairs={{0,4},{4,0},{8,12},{12,8},{16,20},{20,16},{24,28},{28,24},{1,5},{5... | collective-permute-start | bytes 1990664 | tf_op jit(solution)/shard_map/ppermute | solution.py:29
  70.4 23.5 %collective-permute-start.8 = (bf16[4,72,1152]{2,1,0:T(8,128)(2,1)}, bf16[4,72,1152]{2,1,0:T(8,128)(2,1)}, u32[]{:S(2)}, u32[]{:S(2)}) collective-permute-start(bf16[4,72,1152]{2,1,0:T(8,128)(2,1)} %get-tuple-element.246), channel_id=1, source_target_pairs={{0,2},{1,3},{2,0},{3,1},{4,6},{5,7},{6,4},{7,5},{8,10},{9,11},{10,... | collective-permute-start | bytes 1990664 | tf_op jit(solution)/shard_map/ppermute | solution.py:32
  76.6 17.2 %copy-start.17 = (bf16[1,4,72,1152]{3,2,1,0:T(8,128)(2,1)S(1)}, bf16[1,4,72,1152]{3,2,1,0:T(8,128)(2,1)}, u32[]{:S(2)}) copy-start(bf16[1,4,72,1152]{3,2,1,0:T(8,128)(2,1)} %get-tuple-element.605) | copy-start | bytes 1990660
  76.6 17.2 %copy-start.18 = (bf16[1,4,72,1152]{3,2,1,0:T(8,128)(2,1)S(1)}, bf16[1,4,72,1152]{3,2,1,0:T(8,128)(2,1)}, u32[]{:S(2)}) copy-start(bf16[1,4,72,1152]{3,2,1,0:T(8,128)(2,1)} %get-tuple-element.606) | copy-start | bytes 1990660
  76.7 18.8 %collective-permute-start.6 = (bf16[2,1,2,80,1152]{4,3,2,1,0:T(8,128)(2,1)}, bf16[2,1,2,80,1152]{4,3,2,1,0:T(8,128)(2,1)}, u32[]{:S(2)}, u32[]{:S(2)}) collective-permute-start(bf16[2,1,2,80,1152]{4,3,2,1,0:T(8,128)(2,1)} %spread_pick.5), channel_id=1, source_target_pairs={{0,1},{1,0},{2,3},{3,2},{4,5},{5,4},{6,7},{7,6},{8,9},{9,8},{10,11... | collective-permute-start | bytes 2211848 | tf_op jit(solution)/shard_map/ppermute | solution.py:35
  80.7 14.8 %collective-permute-start.9 = (bf16[2,1,2,288,320]{4,3,2,1,0:T(8,128)(2,1)}, bf16[2,1,2,288,320]{4,3,2,1,0:T(8,128)(2,1)S(1)}, u32[]{:S(2)}, u32[]{:S(2)}) collective-permute-start(bf16[2,1,2,288,320]{4,3,2,1,0:T(8,128)(2,1)} %spread_pick.6), channel_id=1, source_target_pairs={{0,1},{1,0},{2,3},{3,2},{4,5},{5,4},{6,7},{7,6},{8,9},{9,8},{10,11... | collective-permute-start | bytes 2211848 | tf_op jit(solution)/shard_map/ppermute | solution.py:35
  95.5 51.4 %copy-start.8 = (bf16[2,4,72,1152]{3,2,1,0:T(8,128)(2,1)}, bf16[2,4,72,1152]{3,2,1,0:T(8,128)(2,1)S(1)}, u32[]{:S(2)}) copy-start(bf16[2,4,72,1152]{3,2,1,0:T(8,128)(2,1)S(1)} %get-tuple-element.257.refs_2_) | copy-start | bytes 3981316
  95.5 53.5 %copy-start.29 = (bf16[2,1,2,288,320]{4,3,2,1,0:T(8,128)(2,1)}, bf16[2,1,2,288,320]{4,3,2,1,0:T(8,128)(2,1)S(1)}, u32[]{:S(2)}) copy-start(bf16[2,1,2,288,320]{4,3,2,1,0:T(8,128)(2,1)S(1)} %collective-permute-done.9.refs_2_) | copy-start | bytes 2211844
  95.5 48.9 %collective-permute-start.10 = (bf16[2,4,72,1152]{3,2,1,0:T(8,128)(2,1)S(1)}, bf16[2,4,72,1152]{3,2,1,0:T(8,128)(2,1)S(1)}, u32[]{:S(2)}, u32[]{:S(2)}) collective-permute-start(bf16[2,4,72,1152]{3,2,1,0:T(8,128)(2,1)S(1)} %get-tuple-element.256.refs_0_), channel_id=1, source_target_pairs={{0,2},{1,3},{2,0},{3,1},{4,6},{5,7},{6,4},{7,5},{8,10},{9,11},{10,... | collective-permute-start | bytes 3981320 | tf_op jit(solution)/shard_map/ppermute | solution.py:32
  97.1 49.8 %collective-permute-start.11 = (bf16[2,4,72,1152]{3,2,1,0:T(8,128)(2,1)S(1)}, bf16[2,4,72,1152]{3,2,1,0:T(8,128)(2,1)}, u32[]{:S(2)}, u32[]{:S(2)}) collective-permute-start(bf16[2,4,72,1152]{3,2,1,0:T(8,128)(2,1)S(1)} %get-tuple-element.257.refs_2_), channel_id=1, source_target_pairs={{0,4},{4,0},{8,12},{12,8},{16,20},{20,16},{24,28},{28,24},{1,5},{5... | collective-permute-start | bytes 3981320 | tf_op jit(solution)/shard_map/ppermute | solution.py:29
  97.6 49.3 %collective-permute-start.12 = (bf16[2,4,72,1152]{3,2,1,0:T(8,128)(2,1)S(1)}, bf16[2,4,72,1152]{3,2,1,0:T(8,128)(2,1)S(1)}, u32[]{:S(2)}, u32[]{:S(2)}) collective-permute-start(bf16[2,4,72,1152]{3,2,1,0:T(8,128)(2,1)S(1)} %get-tuple-element.256.refs_0_), channel_id=1, source_target_pairs={{0,1},{1,0},{2,3},{3,2},{4,5},{5,4},{6,7},{7,6},{8,9},{9,8},{10,11... | collective-permute-start | bytes 3981320 | tf_op jit(solution)/shard_map/ppermute | solution.py:35
  97.6 49.3 %collective-permute-start.13 = (bf16[2,4,72,1152]{3,2,1,0:T(8,128)(2,1)S(1)}, bf16[2,4,72,1152]{3,2,1,0:T(8,128)(2,1)S(1)}, u32[]{:S(2)}, u32[]{:S(2)}) collective-permute-start(bf16[2,4,72,1152]{3,2,1,0:T(8,128)(2,1)S(1)} %get-tuple-element.257.refs_2_), channel_id=1, source_target_pairs={{0,1},{1,0},{2,3},{3,2},{4,5},{5,4},{6,7},{7,6},{8,9},{9,8},{10,11... | collective-permute-start | bytes 3981320 | tf_op jit(solution)/shard_map/ppermute | solution.py:35
  144.4 9.1 %copy-start.26 = (bf16[2,4,72,1152]{3,2,1,0:T(8,128)(2,1)}, bf16[2,4,72,1152]{3,2,1,0:T(8,128)(2,1)S(1)}, u32[]{:S(2)}) copy-start(bf16[2,4,72,1152]{3,2,1,0:T(8,128)(2,1)S(1)} %collective-permute-done.10.refs_1_) | copy-start | bytes 3981316
  147.9 5.4 collective-permute-start.14
  149.0 4.5 collective-permute-start.15
  153.5 19.1 %collective-permute-start.16 = (bf16[2,1,2,80,1152]{4,3,2,1,0:T(8,128)(2,1)}, bf16[2,1,2,80,1152]{4,3,2,1,0:T(8,128)(2,1)S(1)}, u32[]{:S(2)}, u32[]{:S(2)}) collective-permute-start(bf16[2,1,2,80,1152]{4,3,2,1,0:T(8,128)(2,1)} %get-tuple-element.263), channel_id=1, source_target_pairs={{0,2},{1,3},{2,0},{3,1},{4,6},{5,7},{6,4},{7,5},{8,10},{9,11},{10,... | collective-permute-start | bytes 2211848 | tf_op jit(solution)/shard_map/ppermute | solution.py:32
  179.5 11.1 %copy-start.32 = (bf16[2,1,2,80,1152]{4,3,2,1,0:T(8,128)(2,1)S(1)}, bf16[2,1,2,80,1152]{4,3,2,1,0:T(8,128)(2,1)}, u32[]{:S(2)}) copy-start(bf16[2,1,2,80,1152]{4,3,2,1,0:T(8,128)(2,1)} %spread_pick.7) | copy-start | bytes 2211844
  179.5 11.4 %copy-start.70 = (s32[8]{0:T(128)S(1)}, s32[8]{0:T(128)}, u32[]{:S(2)}) copy-start(s32[8]{0:T(128)} %param.25) | copy-start | bytes 100
  190.6 42.4 %collective-permute-start.17 = (bf16[2,1,2,80,1152]{4,3,2,1,0:T(8,128)(2,1)S(1)}, bf16[2,1,2,80,1152]{4,3,2,1,0:T(8,128)(2,1)}, u32[]{:S(2)}, u32[]{:S(2)}) collective-permute-start(bf16[2,1,2,80,1152]{4,3,2,1,0:T(8,128)(2,1)S(1)} %copy-done.32), channel_id=1, source_target_pairs={{0,1},{1,0},{2,3},{3,2},{4,5},{5,4},{6,7},{7,6},{8,9},{9,8},{10,11... | collective-permute-start | bytes 2211848 | tf_op jit(solution)/shard_map/ppermute | solution.py:35
  279.4 13.7 %collective-permute-start.18 = (bf16[2,16,72,1152]{3,2,1,0:T(8,128)(2,1)}, bf16[2,16,72,1152]{3,2,1,0:T(8,128)(2,1)}, u32[]{:S(2)}, u32[]{:S(2)}) collective-permute-start(bf16[2,16,72,1152]{3,2,1,0:T(8,128)(2,1)} %get-tuple-element.298), channel_id=1, source_target_pairs={{0,1},{1,0},{2,3},{3,2},{4,5},{5,4},{6,7},{7,6},{8,9},{9,8},{10,11... | collective-permute-start | bytes 15925256 | tf_op jit(solution)/shard_map/ppermute | solution.py:35
  297.7 38.4 %collective-permute-start.19 = (bf16[4,2,72,1152]{3,2,1,0:T(8,128)(2,1)}, bf16[4,2,72,1152]{3,2,1,0:T(8,128)(2,1)S(1)}, u32[]{:S(2)}, u32[]{:S(2)}) collective-permute-start(bf16[4,2,72,1152]{3,2,1,0:T(8,128)(2,1)} %get-tuple-element.304), channel_id=1, source_target_pairs={{0,4},{4,0},{8,12},{12,8},{16,20},{20,16},{24,28},{28,24},{1,5},{5... | collective-permute-start | bytes 3981320 | tf_op jit(solution)/shard_map/ppermute | solution.py:29
  298.5 37.6 %collective-permute-start.20 = (bf16[4,2,72,1152]{3,2,1,0:T(8,128)(2,1)}, bf16[4,2,72,1152]{3,2,1,0:T(8,128)(2,1)S(1)}, u32[]{:S(2)}, u32[]{:S(2)}) collective-permute-start(bf16[4,2,72,1152]{3,2,1,0:T(8,128)(2,1)} %get-tuple-element.305), channel_id=1, source_target_pairs={{0,2},{1,3},{2,0},{3,1},{4,6},{5,7},{6,4},{7,5},{8,10},{9,11},{10,... | collective-permute-start | bytes 3981320 | tf_op jit(solution)/shard_map/ppermute | solution.py:32
  336.1 35.2 %collective-permute-start.23 = (bf16[2,1152,1152]{2,1,0:T(8,128)(2,1)}, bf16[2,1152,1152]{2,1,0:T(8,128)(2,1)}, u32[]{:S(2)}, u32[]{:S(2)}) collective-permute-start(bf16[2,1152,1152]{2,1,0:T(8,128)(2,1)} %get-tuple-element.325), channel_id=1, source_target_pairs={{0,1},{1,0},{2,3},{3,2},{4,5},{5,4},{6,7},{7,6},{8,9},{9,8},{10,11... | collective-permute-start | bytes 15925256 | tf_op jit(solution)/shard_map/ppermute | solution.py:35
  341.3 23.6 %collective-permute-start.21 = (bf16[4,72,1152]{2,1,0:T(8,128)(2,1)}, bf16[4,72,1152]{2,1,0:T(8,128)(2,1)S(1)}, u32[]{:S(2)}, u32[]{:S(2)}) collective-permute-start(bf16[4,72,1152]{2,1,0:T(8,128)(2,1)} %get-tuple-element.323), channel_id=1, source_target_pairs={{0,2},{1,3},{2,0},{3,1},{4,6},{5,7},{6,4},{7,5},{8,10},{9,11},{10,... | collective-permute-start | bytes 1990664 | tf_op jit(solution)/shard_map/ppermute | solution.py:32
  341.5 23.5 %collective-permute-start.22 = (bf16[4,72,1152]{2,1,0:T(8,128)(2,1)}, bf16[4,72,1152]{2,1,0:T(8,128)(2,1)S(1)}, u32[]{:S(2)}, u32[]{:S(2)}) collective-permute-start(bf16[4,72,1152]{2,1,0:T(8,128)(2,1)} %get-tuple-element.324), channel_id=1, source_target_pairs={{0,4},{4,0},{8,12},{12,8},{16,20},{20,16},{24,28},{28,24},{1,5},{5... | collective-permute-start | bytes 1990664 | tf_op jit(solution)/shard_map/ppermute | solution.py:29
  371.3 9.2 %copy-start.68 = (bf16[2,72,1152]{2,1,0:T(8,128)(2,1)S(1)}, bf16[2,72,1152]{2,1,0:T(8,128)(2,1)}, u32[]{:S(2)}) copy-start(bf16[2,72,1152]{2,1,0:T(8,128)(2,1)} %get-tuple-element.340) | copy-start | bytes 995332
  371.3 11.1 %copy-start.67 = (bf16[2,72,1152]{2,1,0:T(8,128)(2,1)S(1)}, bf16[2,72,1152]{2,1,0:T(8,128)(2,1)}, u32[]{:S(2)}) copy-start(bf16[2,72,1152]{2,1,0:T(8,128)(2,1)} %get-tuple-element.341) | copy-start | bytes 995332
  376.1 38.5 %collective-permute-start.24 = (bf16[4,2,72,1152]{3,2,1,0:T(8,128)(2,1)}, bf16[4,2,72,1152]{3,2,1,0:T(8,128)(2,1)S(1)}, u32[]{:S(2)}, u32[]{:S(2)}) collective-permute-start(bf16[4,2,72,1152]{3,2,1,0:T(8,128)(2,1)} %get-tuple-element.337), channel_id=1, source_target_pairs={{0,4},{4,0},{8,12},{12,8},{16,20},{20,16},{24,28},{28,24},{1,5},{5... | collective-permute-start | bytes 3981320 | tf_op jit(solution)/shard_map/ppermute | solution.py:29
  376.8 37.8 %collective-permute-start.25 = (bf16[4,2,72,1152]{3,2,1,0:T(8,128)(2,1)}, bf16[4,2,72,1152]{3,2,1,0:T(8,128)(2,1)}, u32[]{:S(2)}, u32[]{:S(2)}) collective-permute-start(bf16[4,2,72,1152]{3,2,1,0:T(8,128)(2,1)} %get-tuple-element.338), channel_id=1, source_target_pairs={{0,2},{1,3},{2,0},{3,1},{4,6},{5,7},{6,4},{7,5},{8,10},{9,11},{10,... | collective-permute-start | bytes 3981320 | tf_op jit(solution)/shard_map/ppermute | solution.py:32
  378.7 35.9 %collective-permute-start.26 = (bf16[2,72,1152]{2,1,0:T(8,128)(2,1)S(1)}, bf16[2,72,1152]{2,1,0:T(8,128)(2,1)S(1)}, u32[]{:S(2)}, u32[]{:S(2)}) collective-permute-start(bf16[2,72,1152]{2,1,0:T(8,128)(2,1)S(1)} %copy-done.69), channel_id=1, source_target_pairs={{0,8},{4,12},{8,0},{12,4},{16,24},{20,28},{24,16},{28,20},{1,9},{5... | collective-permute-start | bytes 995336 | tf_op jit(solution)/shard_map/ppermute | solution.py:39
  380.5 34.1 %collective-permute-start.27 = (bf16[2,72,1152]{2,1,0:T(8,128)(2,1)S(1)}, bf16[2,72,1152]{2,1,0:T(8,128)(2,1)S(1)}, u32[]{:S(2)}, u32[]{:S(2)}) collective-permute-start(bf16[2,72,1152]{2,1,0:T(8,128)(2,1)S(1)} %copy-done.68), channel_id=1, source_target_pairs={{0,16},{4,20},{8,24},{12,28},{16,0},{20,4},{24,8},{28,12},{1,17},{... | collective-permute-start | bytes 995336 | tf_op jit(solution)/shard_map/ppermute | solution.py:39
  382.4 32.2 %collective-permute-start.28 = (bf16[2,72,1152]{2,1,0:T(8,128)(2,1)S(1)}, bf16[2,72,1152]{2,1,0:T(8,128)(2,1)S(1)}, u32[]{:S(2)}, u32[]{:S(2)}) collective-permute-start(bf16[2,72,1152]{2,1,0:T(8,128)(2,1)S(1)} %copy-done.67), channel_id=1, source_target_pairs={{0,24},{4,28},{8,16},{12,20},{16,8},{20,12},{24,0},{28,4},{1,25},{... | collective-permute-start | bytes 995336 | tf_op jit(solution)/shard_map/ppermute | solution.py:39
  414.7 28.5 %collective-permute-start.29 = (bf16[2,1152,1152]{2,1,0:T(8,128)(2,1)}, bf16[2,1152,1152]{2,1,0:T(8,128)(2,1)}, u32[]{:S(2)}, u32[]{:S(2)}) collective-permute-start(bf16[2,1152,1152]{2,1,0:T(8,128)(2,1)} %get-tuple-element.354), channel_id=1, source_target_pairs={{0,1},{1,0},{2,3},{3,2},{4,5},{5,4},{6,7},{7,6},{8,9},{9,8},{10,11... | collective-permute-start | bytes 15925256 | tf_op jit(solution)/shard_map/ppermute | solution.py:35
  432.2 16.3 %collective-permute-start.30 = (bf16[4,72,1152]{2,1,0:T(8,128)(2,1)S(1)}, bf16[4,72,1152]{2,1,0:T(8,128)(2,1)S(1)}, u32[]{:S(2)}, u32[]{:S(2)}) collective-permute-start(bf16[4,72,1152]{2,1,0:T(8,128)(2,1)S(1)} %copy-done.66), channel_id=1, source_target_pairs={{0,2},{1,3},{2,0},{3,1},{4,6},{5,7},{6,4},{7,5},{8,10},{9,11},{10,... | collective-permute-start | bytes 1990664 | tf_op jit(solution)/shard_map/ppermute | solution.py:32
  432.4 16.3 %collective-permute-start.31 = (bf16[4,72,1152]{2,1,0:T(8,128)(2,1)S(1)}, bf16[4,72,1152]{2,1,0:T(8,128)(2,1)S(1)}, u32[]{:S(2)}, u32[]{:S(2)}) collective-permute-start(bf16[4,72,1152]{2,1,0:T(8,128)(2,1)S(1)} %copy-done.65), channel_id=1, source_target_pairs={{0,4},{4,0},{8,12},{12,8},{16,20},{20,16},{24,28},{28,24},{1,5},{5... | collective-permute-start | bytes 1990664 | tf_op jit(solution)/shard_map/ppermute | solution.py:29
  448.7 12.1 %copy-start.63 = (f32[36,4]{0,1:T(4,128)S(1)}, f32[36,4]{0,1:T(4,128)}, u32[]{:S(2)}) copy-start(f32[36,4]{0,1:T(4,128)} %param.42) | copy-start | bytes 1732
  448.7 33.3 %collective-permute-start.32 = (bf16[4,2,72,1152]{3,2,1,0:T(8,128)(2,1)}, bf16[4,2,72,1152]{3,2,1,0:T(8,128)(2,1)}, u32[]{:S(2)}, u32[]{:S(2)}) collective-permute-start(bf16[4,2,72,1152]{3,2,1,0:T(8,128)(2,1)} %get-tuple-element.372), channel_id=1, source_target_pairs={{0,4},{4,0},{8,12},{12,8},{16,20},{20,16},{24,28},{28,24},{1,5},{5... | collective-permute-start | bytes 3981320 | tf_op jit(solution)/shard_map/ppermute | solution.py:29
  450.1 32.0 %collective-permute-start.33 = (bf16[4,2,72,1152]{3,2,1,0:T(8,128)(2,1)}, bf16[4,2,72,1152]{3,2,1,0:T(8,128)(2,1)}, u32[]{:S(2)}, u32[]{:S(2)}) collective-permute-start(bf16[4,2,72,1152]{3,2,1,0:T(8,128)(2,1)} %get-tuple-element.373), channel_id=1, source_target_pairs={{0,2},{1,3},{2,0},{3,1},{4,6},{5,7},{6,4},{7,5},{8,10},{9,11},{10,... | collective-permute-start | bytes 3981320 | tf_op jit(solution)/shard_map/ppermute | solution.py:32
  456.4 29.5 %collective-permute-start.34 = (bf16[2,72,1152]{2,1,0:T(8,128)(2,1)}, bf16[2,72,1152]{2,1,0:T(8,128)(2,1)S(1)}, u32[]{:S(2)}, u32[]{:S(2)}) collective-permute-start(bf16[2,72,1152]{2,1,0:T(8,128)(2,1)} %get-tuple-element.379), channel_id=1, source_target_pairs={{0,8},{4,12},{8,0},{12,4},{16,24},{20,28},{24,16},{28,20},{1,9},{5... | collective-permute-start | bytes 995336 | tf_op jit(solution)/shard_map/ppermute | solution.py:39
  457.4 28.6 %collective-permute-start.35 = (bf16[2,72,1152]{2,1,0:T(8,128)(2,1)}, bf16[2,72,1152]{2,1,0:T(8,128)(2,1)S(1)}, u32[]{:S(2)}, u32[]{:S(2)}) collective-permute-start(bf16[2,72,1152]{2,1,0:T(8,128)(2,1)} %get-tuple-element.380), channel_id=1, source_target_pairs={{0,16},{4,20},{8,24},{12,28},{16,0},{20,4},{24,8},{28,12},{1,17},{... | collective-permute-start | bytes 995336 | tf_op jit(solution)/shard_map/ppermute | solution.py:39
  460.3 25.7 %collective-permute-start.36 = (bf16[2,72,1152]{2,1,0:T(8,128)(2,1)}, bf16[2,72,1152]{2,1,0:T(8,128)(2,1)S(1)}, u32[]{:S(2)}, u32[]{:S(2)}) collective-permute-start(bf16[2,72,1152]{2,1,0:T(8,128)(2,1)} %get-tuple-element.381), channel_id=1, source_target_pairs={{0,24},{4,28},{8,16},{12,20},{16,8},{20,12},{24,0},{28,4},{1,25},{... | collective-permute-start | bytes 995336 | tf_op jit(solution)/shard_map/ppermute | solution.py:39
  486.8 22.2 %collective-permute-start.37 = (bf16[4,72,1152]{2,1,0:T(8,128)(2,1)}, bf16[4,72,1152]{2,1,0:T(8,128)(2,1)S(1)}, u32[]{:S(2)}, u32[]{:S(2)}) collective-permute-start(bf16[4,72,1152]{2,1,0:T(8,128)(2,1)} %get-tuple-element.393), channel_id=1, source_target_pairs={{0,2},{1,3},{2,0},{3,1},{4,6},{5,7},{6,4},{7,5},{8,10},{9,11},{10,... | collective-permute-start | bytes 1990664 | tf_op jit(solution)/shard_map/ppermute | solution.py:32
  487.3 21.7 %collective-permute-start.38 = (bf16[4,72,1152]{2,1,0:T(8,128)(2,1)}, bf16[4,72,1152]{2,1,0:T(8,128)(2,1)}, u32[]{:S(2)}, u32[]{:S(2)}) collective-permute-start(bf16[4,72,1152]{2,1,0:T(8,128)(2,1)} %get-tuple-element.394), channel_id=1, source_target_pairs={{0,4},{4,0},{8,12},{12,8},{16,20},{20,16},{24,28},{28,24},{1,5},{5... | collective-permute-start | bytes 1990664 | tf_op jit(solution)/shard_map/ppermute | solution.py:29
  488.3 43.9 %collective-permute-start.39 = (bf16[2,1,2,288,320]{4,3,2,1,0:T(8,128)(2,1)}, bf16[2,1,2,288,320]{4,3,2,1,0:T(8,128)(2,1)}, u32[]{:S(2)}, u32[]{:S(2)}) collective-permute-start(bf16[2,1,2,288,320]{4,3,2,1,0:T(8,128)(2,1)} %get-tuple-element.395), channel_id=1, source_target_pairs={{0,2},{1,3},{2,0},{3,1},{4,6},{5,7},{6,4},{7,5},{8,10},{9,11},{10,... | collective-permute-start | bytes 2211848 | tf_op jit(solution)/shard_map/ppermute | solution.py:32
  491.8 22.7 %collective-permute-start.40 = (f32[2,36,1152]{2,1,0:T(8,128)}, f32[2,36,1152]{2,1,0:T(8,128)}, u32[]{:S(2)}, u32[]{:S(2)}) collective-permute-start(f32[2,36,1152]{2,1,0:T(8,128)} %constant_dynamic-slice_fusion.1), channel_id=1, source_target_pairs={{0,1},{1,0},{2,3},{3,2},{4,5},{5,4},{6,7},{7,6},{8,9},{9,8},{10,11... | collective-permute-start | bytes 995336 | tf_op jit(solution)/shard_map/ppermute | solution.py:35
  532.2 36.4 %collective-permute-start.41 = (bf16[2,2,2,80,1152]{4,3,2,1,0:T(8,128)(2,1)}, bf16[2,2,2,80,1152]{4,3,2,1,0:T(8,128)(2,1)}, u32[]{:S(2)}, u32[]{:S(2)}) collective-permute-start(bf16[2,2,2,80,1152]{4,3,2,1,0:T(8,128)(2,1)} %get-tuple-element.402), channel_id=1, source_target_pairs={{0,2},{1,3},{2,0},{3,1},{4,6},{5,7},{6,4},{7,5},{8,10},{9,11},{10,... | collective-permute-start | bytes 4423688 | tf_op jit(solution)/shard_map/ppermute | solution.py:32
  532.5 19.1 %collective-permute-start.42 = (bf16[2,72,1152]{2,1,0:T(8,128)(2,1)}, bf16[2,72,1152]{2,1,0:T(8,128)(2,1)S(1)}, u32[]{:S(2)}, u32[]{:S(2)}) collective-permute-start(bf16[2,72,1152]{2,1,0:T(8,128)(2,1)} %get-tuple-element.409), channel_id=1, source_target_pairs={{0,8},{4,12},{8,0},{12,4},{16,24},{20,28},{24,16},{28,20},{1,9},{5... | collective-permute-start | bytes 995336 | tf_op jit(solution)/shard_map/ppermute | solution.py:39
  536.7 28.8 %collective-permute-start.43 = (bf16[2,72,1152]{2,1,0:T(8,128)(2,1)}, bf16[2,72,1152]{2,1,0:T(8,128)(2,1)}, u32[]{:S(2)}, u32[]{:S(2)}) collective-permute-start(bf16[2,72,1152]{2,1,0:T(8,128)(2,1)} %get-tuple-element.410), channel_id=1, source_target_pairs={{0,16},{4,20},{8,24},{12,28},{16,0},{20,4},{24,8},{28,12},{1,17},{... | collective-permute-start | bytes 995336 | tf_op jit(solution)/shard_map/ppermute | solution.py:39
  539.4 26.1 %collective-permute-start.44 = (bf16[2,72,1152]{2,1,0:T(8,128)(2,1)}, bf16[2,72,1152]{2,1,0:T(8,128)(2,1)}, u32[]{:S(2)}, u32[]{:S(2)}) collective-permute-start(bf16[2,72,1152]{2,1,0:T(8,128)(2,1)} %get-tuple-element.411), channel_id=1, source_target_pairs={{0,24},{4,28},{8,16},{12,20},{16,8},{20,12},{24,0},{28,4},{1,25},{... | collective-permute-start | bytes 995336 | tf_op jit(solution)/shard_map/ppermute | solution.py:39
  544.7 23.9 %collective-permute-start.45 = (bf16[2,1,2,288,320]{4,3,2,1,0:T(8,128)(2,1)}, bf16[2,1,2,288,320]{4,3,2,1,0:T(8,128)(2,1)}, u32[]{:S(2)}, u32[]{:S(2)}) collective-permute-start(bf16[2,1,2,288,320]{4,3,2,1,0:T(8,128)(2,1)} %spread_pick.9), channel_id=1, source_target_pairs={{0,1},{1,0},{2,3},{3,2},{4,5},{5,4},{6,7},{7,6},{8,9},{9,8},{10,11... | collective-permute-start | bytes 2211848 | tf_op jit(solution)/shard_map/ppermute | solution.py:35
  549.6 15.9 %copy-start.43 = (f32[2,72,1152]{2,1,0:T(8,128)S(1)}, f32[2,72,1152]{2,1,0:T(8,128)}, u32[]{:S(2)}) copy-start(f32[2,72,1152]{2,1,0:T(8,128)} %get-tuple-element.405) | copy-start | bytes 1990660
  568.6 2.2 collective-permute-start.47
  575.3 19.1 %all-to-all-start = ((f32[32,10,128]{2,1,0:T(8,128)}), f32[32,10,128]{2,1,0:T(8,128)}, u32[]{:S(2)}, u32[]{:S(2)}) async-start(f32[32,10,128]{2,1,0:T(8,128)} %broadcast_in_dim.2), calls=%async_computation.1 | async-start | bytes 524288 | tf_op jit(solution)/shard_map/all_to_all | solution.py:1032
  589.7 16.8 %collective-permute-start.46 = (bf16[2,2,2,80,1152]{4,3,2,1,0:T(8,128)(2,1)}, bf16[2,2,2,80,1152]{4,3,2,1,0:T(8,128)(2,1)}, u32[]{:S(2)}, u32[]{:S(2)}) collective-permute-start(bf16[2,2,2,80,1152]{4,3,2,1,0:T(8,128)(2,1)} %spread_pick.8), channel_id=1, source_target_pairs={{0,1},{1,0},{2,3},{3,2},{4,5},{5,4},{6,7},{7,6},{8,9},{9,8},{10,11... | collective-permute-start | bytes 4423688 | tf_op jit(solution)/shard_map/ppermute | solution.py:35
  (59 other events, 157.1 us)
Sparse Core Ops, SparseCore 0:
  12.6 164.5 all-gather.3
  180.7 85.0 all-gather.5
  431.2 134.3 reduce-scatter.1
